TPU v7x, 256 devices: a whole 4x4x8 slice. The times are simulated.
256 devices in a mesh: gx: 8 (over x, core), gy: 4 (over y), gz: 8 (over z).
Axes of the slice: x: 4, y: 4, z: 8, core: 2. Of those that a mesh axis runs over, the one named last changes fastest.
Arguments:
- attributes: bfloat16 [32, 64, 32, 1024], P(None, 'gx', 'gy', 'gz'), may hold values from -11 to 11, as said below
- start_centroids: float32 [32, 32], replicated, may hold values from -6 to 6
Outputs:
- centroids: float32 [32, 32], replicated
- memberships: float32 [32, 64, 32, 1024], P(None, 'gx', 'gy', 'gz')
Inputs may be any that keep to these rules, and one draw needn't show every extreme that they name: `attributes`: each voxel's attribute values.
All inputs are finite; a program needn't handle non-finite values.
Results may differ from a plain program's by a relative error of at most 0.011.
Values may be sent and summed in bfloat16 or wider, within the bound.
No kernel may reach another device: no remote copies, remote signals or barrier semaphores. Data moves between devices by JAX's collectives and lax.ppermute only.
A program may use at most 64 MiB of HBM per device.

v0:
```python
import jax
import jax.numpy as jnp
from jax import lax
from jax.sharding import PartitionSpec as P

UPDATES = 2


def extended(cells, sides, width):
    for axis, dim in sides:
        count = lax.axis_size(axis)
        ends = count - 1
        head = lax.slice_in_dim(cells, 0, width, axis=dim)
        tail = lax.slice_in_dim(cells, cells.shape[dim] - width, cells.shape[dim], axis=dim)
        cells = jnp.concatenate(
            [
                lax.ppermute(tail, axis, [(i, (i + 1) % count) for i in range(ends)]),
                cells,
                lax.ppermute(head, axis, [((i + 1) % count, i) for i in range(ends)]),
            ],
            axis=dim,
        )
    return cells


def window_sum(padded, dim):
    count = padded.shape[dim] - 4
    total = lax.slice_in_dim(padded, 0, count, axis=dim)
    for shift in range(1, 5):
        total = total + lax.slice_in_dim(padded, shift, shift + count, axis=dim)
    return total


def smooth(rounded):
    padded = extended(rounded, (("gx", 1), ("gy", 2), ("gz", 3)), 2)
    padded = padded.astype(jnp.float32)
    return window_sum(window_sum(window_sum(padded, 3), 2), 1)


def total_sums(numer, denom):
    return lax.psum((numer, denom), ("gx", "gy", "gz"))


def per_device(attributes, start_centroids):
    attr_count, width_x, width_y, width_z = attributes.shape
    voxels = width_x * width_y * width_z
    flat = attributes.reshape(attr_count, voxels)
    values = flat.astype(jnp.float32)
    squares = jnp.sum(values * values, axis=0)
    centroids = start_centroids
    memberships = None
    for step in range(UPDATES):
        cb = centroids.astype(jnp.bfloat16)
        cross = jnp.dot(cb, flat, preferred_element_type=jnp.float32)
        csq = jnp.sum(centroids * centroids, axis=1)
        dist = squares[None, :] - 2.0 * cross + csq[:, None] + 1.0
        inverse = 1.0 / dist
        raw = inverse / jnp.sum(inverse, axis=0, keepdims=True)
        rounded = raw.astype(jnp.bfloat16).reshape(-1, width_x, width_y, width_z)
        box = smooth(rounded).reshape(-1, voxels)
        product = raw * box
        memberships = product / jnp.sum(product, axis=0, keepdims=True)
        weights = (memberships * memberships).astype(jnp.bfloat16)
        numer = lax.dot_general(
            weights, flat, (((1,), (1,)), ((), ())), preferred_element_type=jnp.float32
        )
        denom = jnp.sum(weights.astype(jnp.float32), axis=1)
        numer, denom = total_sums(numer, denom)
        centroids = numer / denom[:, None]
    return (centroids, memberships.reshape(-1, width_x, width_y, width_z))


def solution(mesh):
    placed = (P(None, "gx", "gy", "gz"), P())
    return jax.shard_map(
        per_device,
        mesh=mesh,
        in_specs=placed,
        out_specs=(P(), P(None, "gx", "gy", "gz")),
        check_vma=False,
    )
```

profile of v0, /device:TPU:1, one launch (start us, length us, event | category | flops | bytes accessed | tf_op | source)
XLA Modules:
  0.0 258.0 jit_solution(10573396135532194739)
XLA Ops:
  0.6 0.8 multiply_reduce_fusion.2
  1.5 1.2 multiply_reduce_fusion
  2.6 1.6 divide_reduce_fusion.1
  4.3 1.0 copy-done.2
  5.6 4.5 %collective-permute-start = (bf16[32,2,8,128]{3,2,1,0:T(8,128)(2,1)S(1)}, bf16[32,2,8,128]{3,2,1,0:T(8,128)(2,1)S(1)}, u32[]{:S(2)}, u32[]{:S(2)}) collective-permute-start(bf16[32,2,8,128]{3,2,1,0:T(8,128)(2,1)S(1)} %get-tuple-element.24), channel_id=1, source_target_pairs={{0,32},{32,64},{64,96},{96,128},{128,160},{160,192},{192,224},{1,3... | collective-permute-start | bytes 393224 | tf_op jit(solution)/shard_map/ppermute | solution.py:17
  10.1 1.9 collective-permute-start.1
  12.1 4.2 %collective-permute-done.1 = bf16[32,2,8,128]{3,2,1,0:T(8,128)(2,1)S(1)} collective-permute-done((bf16[32,2,8,128]{3,2,1,0:T(8,128)(2,1)S(1)}, bf16[32,2,8,128]{3,2,1,0:T(8,128)(2,1)S(1)}, u32[]{:S(2)}, u32[]{:S(2)}) %collective-permute-start.1) | collective-permute-done | bytes 131104 | tf_op jit(solution)/shard_map/ppermute | solution.py:19
  16.7 3.9 %collective-permute-start.2 = (bf16[32,12,2,128]{3,0,2,1:T(8,128)(2,1)S(1)}, bf16[32,12,2,128]{3,0,2,1:T(8,128)(2,1)}, u32[]{:S(2)}, u32[]{:S(2)}) collective-permute-start(bf16[32,12,2,128]{3,0,2,1:T(8,128)(2,1)S(1)} %copy.46), channel_id=1, source_target_pairs={{0,8},{8,16},{16,24},{1,9},{9,17},{17,25},{2,10},{10,18},{18,26},{... | collective-permute-start | bytes 589832 | tf_op jit(solution)/shard_map/ppermute | solution.py:17
  20.6 1.3 collective-permute-start.3
  21.9 3.0 %copy.31 = bf16[32,12,8,128]{0,3,2,1:T(8,128)(2,1)S(1)} copy(bf16[32,12,8,128]{3,2,1,0:T(8,128)(2,1)} %copy-done.6) | data formatting | bytes 1572864 | tf_op jit(solution)/shard_map/concatenate | solution.py:15
  24.9 2.1 copy.30
  27.2 2.1 copy.32
  29.3 2.2 pad_maximum_fusion
  31.5 2.1 copy-done
  33.7 1.3 collective-permute-start.5
  35.0 4.8 %collective-permute-start.4 = (bf16[32,12,12,2]{0,3,2,1:T(2,128)(2,1)S(1)}, bf16[32,12,12,2]{0,3,2,1:T(2,128)(2,1)}, u32[]{:S(2)}, u32[]{:S(2)}) collective-permute-start(bf16[32,12,12,2]{0,3,2,1:T(2,128)(2,1)S(1)} %get-tuple-element.14), channel_id=1, source_target_pairs={{0,1},{1,2},{2,3},{3,4},{4,5},{5,6},{6,7},{8,9},{9,10},{10,11},{11... | collective-permute-start | bytes 55304 | tf_op jit(solution)/shard_map/ppermute | solution.py:17
  39.8 3.8 %copy.34 = bf16[32,12,12,128]{3,0,2,1:T(8,128)(2,1)S(1)} copy(bf16[32,12,12,128]{0,3,2,1:T(8,128)(2,1)} %copy-done) | data formatting | bytes 2359296 | tf_op jit(solution)/shard_map/concatenate | solution.py:15
  43.6 1.0 copy.35
  44.6 1.8 copy.33
  46.4 1.3 maximum_convert_fusion
  47.7 2.5 slice_add_fusion.4
  50.7 0.6 copy.36
  51.9 0.8 fusion.13
  52.7 0.8 convert_reduce_fusion.1
  54.0 79.0 %all-reduce.1 = (f32[32,32]{1,0:T(8,128)S(1)}, f32[32]{0:T(128)S(1)}) all-reduce(f32[32,32]{1,0:T(8,128)S(1)} %fusion.9, f32[32]{0:T(128)S(1)} %get-tuple-element.10), channel_id=1, replica_groups=mesh['gx'=8,'gy'=4,'gz'=8] {'gx','gy','gz'}, use_global_device_ids=true, to_apply=%region_4.0 | all-reduce | flops 1056 | bytes 8448 | tf_op jit(solution)/shard_map/psum | solution.py:41
  133.8 1.0 copy-done.4
  135.1 2.6 collective-permute-start.6
  137.7 1.9 collective-permute-start.7
  139.7 4.2 %collective-permute-done.7 = bf16[32,2,8,128]{3,2,1,0:T(8,128)(2,1)S(1)} collective-permute-done((bf16[32,2,8,128]{3,2,1,0:T(8,128)(2,1)S(1)}, bf16[32,2,8,128]{3,2,1,0:T(8,128)(2,1)S(1)}, u32[]{:S(2)}, u32[]{:S(2)}) %collective-permute-start.7) | collective-permute-done | bytes 131104 | tf_op jit(solution)/shard_map/ppermute | solution.py:19
  144.3 2.4 collective-permute-start.8
  146.7 1.5 collective-permute-start.9
  148.2 3.0 %copy.40 = bf16[32,12,8,128]{0,3,2,1:T(8,128)(2,1)S(1)} copy(bf16[32,12,8,128]{3,2,1,0:T(8,128)(2,1)} %copy-done.7) | data formatting | bytes 1572864 | tf_op jit(solution)/shard_map/concatenate | solution.py:15
  151.2 2.1 copy.39
  153.3 2.1 copy.41
  155.5 2.2 pad_maximum_fusion.1
  157.7 2.1 copy-done.1
  159.9 1.3 collective-permute-start.11
  161.2 4.8 %collective-permute-start.10 = (bf16[32,12,12,2]{0,3,2,1:T(2,128)(2,1)S(1)}, bf16[32,12,12,2]{0,3,2,1:T(2,128)(2,1)}, u32[]{:S(2)}, u32[]{:S(2)}) collective-permute-start(bf16[32,12,12,2]{0,3,2,1:T(2,128)(2,1)S(1)} %get-tuple-element.12), channel_id=1, source_target_pairs={{0,1},{1,2},{2,3},{3,4},{4,5},{5,6},{6,7},{8,9},{9,10},{10,11},{11... | collective-permute-start | bytes 55304 | tf_op jit(solution)/shard_map/ppermute | solution.py:17
  166.0 3.8 %copy.43 = bf16[32,12,12,128]{3,0,2,1:T(8,128)(2,1)S(1)} copy(bf16[32,12,12,128]{0,3,2,1:T(8,128)(2,1)} %copy-done.1) | data formatting | bytes 2359296 | tf_op jit(solution)/shard_map/concatenate | solution.py:15
  169.8 1.0 copy.44
  170.8 1.8 copy.42
  172.6 1.3 maximum_convert_fusion.1
  173.9 2.5 slice_add_fusion
  176.9 0.6 copy.45
  178.1 0.8 fusion.20
  179.6 1.2 copy.55
  180.8 76.5 %all-reduce = (f32[32,32]{1,0:T(8,128)S(1)}, f32[32]{0:T(128)S(1)}) all-reduce(f32[32,32]{1,0:T(8,128)S(1)} %fusion.6, f32[32]{0:T(128)S(1)} %get-tuple-element.6), channel_id=1, replica_groups=mesh['gx'=8,'gy'=4,'gz'=8] {'gx','gy','gz'}, use_global_device_ids=true, to_apply=%region_10.0 | all-reduce | flops 1056 | bytes 8448 | tf_op jit(solution)/shard_map/psum | solution.py:41
  257.4 0.7 broadcast_divide_fusion.1
  (67 shorter events, 5.9 us)
Async XLA Ops:
  2.6 1.6 copy-start.14
  4.3 1.0 copy-start.2
  4.3 7.7 %copy-start.10 = (f32[8192]{0:T(1024)}, f32[8192]{0:T(1024)S(1)}, u32[]{:S(2)}) copy-start(f32[8192]{0:T(1024)S(1)} %get-tuple-element.25) | copy-start | bytes 98308
  5.6 6.5 %collective-permute-start = (bf16[32,2,8,128]{3,2,1,0:T(8,128)(2,1)S(1)}, bf16[32,2,8,128]{3,2,1,0:T(8,128)(2,1)S(1)}, u32[]{:S(2)}, u32[]{:S(2)}) collective-permute-start(bf16[32,2,8,128]{3,2,1,0:T(8,128)(2,1)S(1)} %get-tuple-element.24), channel_id=1, source_target_pairs={{0,32},{32,64},{64,96},{96,128},{128,160},{160,192},{192,224},{1,3... | collective-permute-start | bytes 393224 | tf_op jit(solution)/shard_map/ppermute | solution.py:17
  10.1 6.3 %collective-permute-start.1 = (bf16[32,2,8,128]{3,2,1,0:T(8,128)(2,1)S(1)}, bf16[32,2,8,128]{3,2,1,0:T(8,128)(2,1)S(1)}, u32[]{:S(2)}, u32[]{:S(2)}) collective-permute-start(bf16[32,2,8,128]{3,2,1,0:T(8,128)(2,1)S(1)} %get-tuple-element.23), channel_id=1, source_target_pairs={{32,0},{64,32},{96,64},{128,96},{160,128},{192,160},{224,192},{33,... | collective-permute-start | bytes 393224 | tf_op jit(solution)/shard_map/ppermute | solution.py:19
  16.4 4.2 %copy-start.6 = (bf16[32,12,8,128]{3,2,1,0:T(8,128)(2,1)}, bf16[32,12,8,128]{3,2,1,0:T(8,128)(2,1)S(1)}, u32[]{:S(2)}) copy-start(bf16[32,12,8,128]{3,2,1,0:T(8,128)(2,1)S(1)} %constant_dynamic-update-slice_fusion) | copy-start | bytes 2359300
  16.7 8.2 %collective-permute-start.2 = (bf16[32,12,2,128]{3,0,2,1:T(8,128)(2,1)S(1)}, bf16[32,12,2,128]{3,0,2,1:T(8,128)(2,1)}, u32[]{:S(2)}, u32[]{:S(2)}) collective-permute-start(bf16[32,12,2,128]{3,0,2,1:T(8,128)(2,1)S(1)} %copy.46), channel_id=1, source_target_pairs={{0,8},{8,16},{16,24},{1,9},{9,17},{17,25},{2,10},{10,18},{18,26},{... | collective-permute-start | bytes 589832 | tf_op jit(solution)/shard_map/ppermute | solution.py:17
  20.6 6.5 %collective-permute-start.3 = (bf16[32,12,2,128]{3,0,2,1:T(8,128)(2,1)S(1)}, bf16[32,12,2,128]{3,0,2,1:T(8,128)(2,1)}, u32[]{:S(2)}, u32[]{:S(2)}) collective-permute-start(bf16[32,12,2,128]{3,0,2,1:T(8,128)(2,1)S(1)} %copy.47), channel_id=1, source_target_pairs={{8,0},{16,8},{24,16},{9,1},{17,9},{25,17},{10,2},{18,10},{26,18},{... | collective-permute-start | bytes 589832 | tf_op jit(solution)/shard_map/ppermute | solution.py:19
  31.5 2.1 copy-start
  33.7 9.9 %collective-permute-start.5 = (bf16[32,12,12,2]{0,3,2,1:T(2,128)(2,1)S(1)}, bf16[32,12,12,2]{0,3,2,1:T(2,128)(2,1)S(1)}, u32[]{:S(2)}, u32[]{:S(2)}) collective-permute-start(bf16[32,12,12,2]{0,3,2,1:T(2,128)(2,1)S(1)} %get-tuple-element.15), channel_id=1, source_target_pairs={{1,0},{2,1},{3,2},{4,3},{5,4},{6,5},{7,6},{9,8},{10,9},{11,10},{12... | collective-permute-start | bytes 55304 | tf_op jit(solution)/shard_map/ppermute | solution.py:19
  35.0 9.6 %collective-permute-start.4 = (bf16[32,12,12,2]{0,3,2,1:T(2,128)(2,1)S(1)}, bf16[32,12,12,2]{0,3,2,1:T(2,128)(2,1)}, u32[]{:S(2)}, u32[]{:S(2)}) collective-permute-start(bf16[32,12,12,2]{0,3,2,1:T(2,128)(2,1)S(1)} %get-tuple-element.14), channel_id=1, source_target_pairs={{0,1},{1,2},{2,3},{3,4},{4,5},{5,6},{6,7},{8,9},{9,10},{10,11},{11... | collective-permute-start | bytes 55304 | tf_op jit(solution)/shard_map/ppermute | solution.py:17
  50.5 0.8 copy-start.11
  50.7 1.2 copy-start.3
  51.9 1.6 copy-start.8
  52.7 80.5 %copy-start.15 = (f32[8,8,128]{2,1,0:T(8,128)S(1)}, f32[8,8,128]{2,1,0:T(8,128)}, u32[]{:S(2)}) copy-start(f32[8,8,128]{2,1,0:T(8,128)} %copy-done.14) | copy-start | bytes 98308
  133.8 1.0 copy-start.4
  133.8 5.8 %copy-start.12 = (f32[8192]{0:T(1024)}, f32[8192]{0:T(1024)S(1)}, u32[]{:S(2)}) copy-start(f32[8192]{0:T(1024)S(1)} %get-tuple-element.27) | copy-start | bytes 98308
  135.1 4.5 %collective-permute-start.6 = (bf16[32,2,8,128]{3,2,1,0:T(8,128)(2,1)S(1)}, bf16[32,2,8,128]{3,2,1,0:T(8,128)(2,1)S(1)}, u32[]{:S(2)}, u32[]{:S(2)}) collective-permute-start(bf16[32,2,8,128]{3,2,1,0:T(8,128)(2,1)S(1)} %get-tuple-element.22), channel_id=1, source_target_pairs={{0,32},{32,64},{64,96},{96,128},{128,160},{160,192},{192,224},{1,3... | collective-permute-start | bytes 393224 | tf_op jit(solution)/shard_map/ppermute | solution.py:17
  137.7 6.3 %collective-permute-start.7 = (bf16[32,2,8,128]{3,2,1,0:T(8,128)(2,1)S(1)}, bf16[32,2,8,128]{3,2,1,0:T(8,128)(2,1)S(1)}, u32[]{:S(2)}, u32[]{:S(2)}) collective-permute-start(bf16[32,2,8,128]{3,2,1,0:T(8,128)(2,1)S(1)} %get-tuple-element.21), channel_id=1, source_target_pairs={{32,0},{64,32},{96,64},{128,96},{160,128},{192,160},{224,192},{33,... | collective-permute-start | bytes 393224 | tf_op jit(solution)/shard_map/ppermute | solution.py:19
  144.0 2.7 %copy-start.7 = (bf16[32,12,8,128]{3,2,1,0:T(8,128)(2,1)}, bf16[32,12,8,128]{3,2,1,0:T(8,128)(2,1)S(1)}, u32[]{:S(2)}) copy-start(bf16[32,12,8,128]{3,2,1,0:T(8,128)(2,1)S(1)} %constant_dynamic-update-slice_fusion.3) | copy-start | bytes 2359300
  144.3 7.0 %collective-permute-start.8 = (bf16[32,12,2,128]{3,0,2,1:T(8,128)(2,1)S(1)}, bf16[32,12,2,128]{3,0,2,1:T(8,128)(2,1)}, u32[]{:S(2)}, u32[]{:S(2)}) collective-permute-start(bf16[32,12,2,128]{3,0,2,1:T(8,128)(2,1)S(1)} %copy.48), channel_id=1, source_target_pairs={{0,8},{8,16},{16,24},{1,9},{9,17},{17,25},{2,10},{10,18},{18,26},{... | collective-permute-start | bytes 589832 | tf_op jit(solution)/shard_map/ppermute | solution.py:17
  146.7 6.6 %collective-permute-start.9 = (bf16[32,12,2,128]{3,0,2,1:T(8,128)(2,1)S(1)}, bf16[32,12,2,128]{3,0,2,1:T(8,128)(2,1)}, u32[]{:S(2)}, u32[]{:S(2)}) collective-permute-start(bf16[32,12,2,128]{3,0,2,1:T(8,128)(2,1)S(1)} %copy.49), channel_id=1, source_target_pairs={{8,0},{16,8},{24,16},{9,1},{17,9},{25,17},{10,2},{18,10},{26,18},{... | collective-permute-start | bytes 589832 | tf_op jit(solution)/shard_map/ppermute | solution.py:19
  157.7 2.1 copy-start.1
  159.9 9.9 %collective-permute-start.11 = (bf16[32,12,12,2]{0,3,2,1:T(2,128)(2,1)S(1)}, bf16[32,12,12,2]{0,3,2,1:T(2,128)(2,1)S(1)}, u32[]{:S(2)}, u32[]{:S(2)}) collective-permute-start(bf16[32,12,12,2]{0,3,2,1:T(2,128)(2,1)S(1)} %get-tuple-element.13), channel_id=1, source_target_pairs={{1,0},{2,1},{3,2},{4,3},{5,4},{6,5},{7,6},{9,8},{10,9},{11,10},{12... | collective-permute-start | bytes 55304 | tf_op jit(solution)/shard_map/ppermute | solution.py:19
  161.2 9.6 %collective-permute-start.10 = (bf16[32,12,12,2]{0,3,2,1:T(2,128)(2,1)S(1)}, bf16[32,12,12,2]{0,3,2,1:T(2,128)(2,1)}, u32[]{:S(2)}, u32[]{:S(2)}) collective-permute-start(bf16[32,12,12,2]{0,3,2,1:T(2,128)(2,1)S(1)} %get-tuple-element.12), channel_id=1, source_target_pairs={{0,1},{1,2},{2,3},{3,4},{4,5},{5,6},{6,7},{8,9},{9,10},{10,11},{11... | collective-permute-start | bytes 55304 | tf_op jit(solution)/shard_map/ppermute | solution.py:17
  176.7 0.8 copy-start.13
  176.9 1.2 copy-start.5
  178.1 1.1 copy-start.9
where the time goes:
time: 259 us; the launch traced here: 258 us
  blocking collectives  156 us (60%)
  local copies, waits for them, and re-layouts  38.7 us (15%)
  starting transfers between devices  32.2 us (12%)
  other arithmetic  18.6 us (7%)
  waiting for transfers between devices  8.62 us (3%)
  matrix products  3.14 us (1%)
    psum x2, blocking collectives, total_sums(): return lax.psum((numer, denom), ('gx', 'gy', 'gz'))  156 us
    ppermute x6, starting transfers between devices, extended(): lax.ppermute(tail, axis, [(i, (i + 1) % count) for i in range(ends)])  23 us
    concatenate x6, local copies, waits for them, and re-layouts, extended(): jnp.concatenate([lax.ppermute(tail, axis, [(i, (i + 1) % count) for i in...  13.6 us
    ppermute x6, starting transfers between devices, extended(): lax.ppermute(head, axis, [((i + 1) % count, i) for i in range(ends)])  9.25 us
    unnamed x43, local copies, waits for them, and re-layouts  9.09 us
    ppermute x6, waiting for transfers between devices, extended(): lax.ppermute(head, axis, [((i + 1) % count, i) for i in range(ends)])  8.6 us
    ppermute x4, local copies, waits for them, and re-layouts, extended(): lax.ppermute(tail, axis, [(i, (i + 1) % count) for i in range(ends)])  7.86 us
    ppermute x4, local copies, waits for them, and re-layouts, extended(): lax.ppermute(head, axis, [((i + 1) % count, i) for i in range(ends)])  6.15 us
  transfers between devices with their start and end apart: 12, of which 3 were waited for; matrix products, arithmetic and copies ran while one was open for 8% of the time, Pallas kernels for 0%

commit v1 on v0

v1 whole, which is shorter than its diff:
```python
import functools
import jax
import jax.numpy as jnp
import numpy as np
from jax import lax
from jax.experimental import pallas as pl
from jax.experimental.pallas import tpu as pltpu
from jax.sharding import Mesh, PartitionSpec as P

UPDATES = 2
F = 32
W = 8
E = W + 4
ZT = 12
BF16 = jnp.bfloat16
F32 = jnp.float32
XS = ("cx", "core")


def z_tiles():
    out = []
    for dy in (0, -1, 1):
        for half in (0, 1):
            out.append((0, dy, half))
    for dx, half in ((-1, 1), (1, 0)):
        for dy in (0, -1, 1):
            out.append((dx, dy, half))
    return out


def halo_matrix():
    src = []
    for dx, dy, half in z_tiles():
        for j in range(32):
            c = half * 32 + j
            for t in range(4):
                src.append((dx * W + c // W, dy * W + c % W, (-2, -1, 128, 129)[t]))
    src = np.array(src)
    dst = []
    for c in range(W * W):
        for t in range(4):
            dst.append((c // W, c % W, (126, 127, 0, 1)[t]))
    dst = np.array(dst)
    near = (np.abs(src[:, None, :] - dst[None, :, :]) <= 2).all(-1)
    return near.astype(np.float32)


def band_matrix():
    z = np.arange(128)
    return (np.abs(z[:, None] - z[None, :]) <= 2).astype(np.float32)


def recip(x):
    r = pl.reciprocal(x, approx=True)
    return r * (2.0 - x * r)


def unpack_centroids(packed):
    return jnp.concatenate([packed[:, 32 * g:32 * g + 32] for g in range(4)], axis=0)


def pack_rows(wide):
    return jnp.concatenate([wide[8 * g:8 * g + 8] for g in range(4)], axis=1)


def update_kernel(text, zt, cent, edge, smat, band, memb, part, inv_s, win_s):
    c = unpack_centroids(cent[0:8, :] / cent[8:16, :])
    cbm2 = (-2.0 * c.astype(BF16).astype(F32)).astype(BF16)
    csq1 = jnp.broadcast_to(jnp.sum(c * c, axis=1, keepdims=True) + 1.0, (F, 128))
    xlo, xhi, ylo, yhi, zlo, zhi = [edge[i] for i in range(6)]

    def inverse(a):
        af = a.astype(F32)
        sq = jnp.sum(af * af, axis=0, keepdims=True)
        cross = jnp.dot(cbm2, a, preferred_element_type=F32)
        n = a.shape[1] // 128
        parts = []
        for i in range(n):
            s = slice(128 * i, 128 * i + 128)
            parts.append(recip(cross[:, s] + csq1 + sq[:, s]))
        return parts

    def normalised(inv, mask):
        return (inv * (recip(jnp.sum(inv, axis=0, keepdims=True)) * mask)).astype(BF16)

    def front(X, carry):
        mx = jnp.where(X < 2, xlo, jnp.where(X >= W + 2, xhi, 1.0))
        rounded = []
        for Y in range(0, E, 2):
            pair = jnp.concatenate([text[X * E + Y], text[X * E + Y + 1]], axis=1)
            my = ylo if Y < 2 else (yhi if Y >= W + 2 else None)
            m = mx if my is None else mx * my
            for i, inv in enumerate(inverse(pair)):
                if 2 <= Y < W + 2:
                    inv_s[X * W + Y + i - 2] = inv
                rounded.append(normalised(inv, m))
        rows = jnp.concatenate(rounded, axis=0)
        z = jnp.dot(rows, band[...], preferred_element_type=F32)
        cols = [z[32 * Y:32 * Y + 32] for Y in range(E)]
        p = [cols[Y] + cols[Y + 1] for Y in range(E - 1)]
        for y in range(W):
            win_s[X * W + y] = p[y] + p[y + 2] + cols[y + 4]
        return carry

    lax.fori_loop(0, E, front, 0)

    lane = lax.broadcasted_iota(jnp.int32, (1, 128), 1)
    mz = jnp.where(lane % 4 < 2, zlo, zhi)
    rz = []
    for i, (dx, dy, half) in enumerate(z_tiles()):
        m = mz
        if dx:
            m = m * (xlo if dx < 0 else xhi)
        if dy:
            m = m * (ylo if dy < 0 else yhi)
        rz.append(normalised(inverse(zt[i])[0], m))
    halo = jnp.dot(jnp.concatenate(rz, axis=1), smat[...], preferred_element_type=F32)
    halves = [halo[:, :128], halo[:, 128:]]
    ends = (lane < 2) | (lane >= 126)

    numer = jnp.zeros((F, F), F32)
    denom = jnp.zeros((F, 128), F32)
    for x in range(W):
        ws, ts = [], []
        for y in range(W):
            i = x * W + y
            box = win_s[i]
            for d in range(1, 5):
                box = box + win_s[i + d * W]
            h = pltpu.roll(halves[i // 32], (126 - 4 * (i % 32)) % 128, 1)
            box = box + jnp.where(ends, h, 0.0)
            prod = inv_s[i + 2 * W] * box
            m = prod * recip(jnp.sum(prod, axis=0, keepdims=True))
            memb[i] = m
            w = (m * m).astype(BF16)
            denom = denom + w.astype(F32)
            ws.append(w)
            ts.append(text[(x + 2) * E + y + 2])
        numer = numer + lax.dot_general(
            jnp.concatenate(ws, axis=1), jnp.concatenate(ts, axis=1),
            (((1,), (1,)), ((), ())), preferred_element_type=F32)
    total = jnp.broadcast_to(jnp.sum(denom, axis=1, keepdims=True), (F, F))
    part[0:8, :] = pack_rows(numer)
    part[8:16, :] = pack_rows(total)


def update(text, zt, cent, edge):
    vmem = pl.BlockSpec(memory_space=pltpu.VMEM)
    return pl.pallas_call(
        update_kernel,
        out_shape=(
            jax.ShapeDtypeStruct((W * W, F, 128), F32),
            jax.ShapeDtypeStruct((16, 128), F32),
        ),
        in_specs=[vmem, vmem, vmem, pl.BlockSpec(memory_space=pltpu.SMEM), vmem, vmem],
        out_specs=(vmem, vmem),
        scratch_shapes=[
            pltpu.VMEM((E * W, F, 128), F32),
            pltpu.VMEM((E * W, F, 128), F32),
        ],
        compiler_params=pltpu.CompilerParams(vmem_limit_bytes=40 << 20),
    )(text, zt, cent, edge, jnp.asarray(halo_matrix(), BF16), jnp.asarray(band_matrix(), BF16))


def both_ways(up, down, axes, count):
    lo = lax.ppermute(up, axes, [(i, (i + 1) % count) for i in range(count)])
    hi = lax.ppermute(down, axes, [((i + 1) % count, i) for i in range(count)])
    return lo, hi


def gather_sum(part, axes, count):
    every = lax.all_to_all(jnp.broadcast_to(part[None], (count,) + part.shape), axes, 0, 0)
    return jnp.sum(every, axis=0)


def total_sums(part):
    part = part + lax.ppermute(part, "core", [(0, 1), (1, 0)])
    part = gather_sum(part, ("cx", "gy"), 16)
    return gather_sum(part, ("gz",), 8)


def packed_ends(cols):
    ends = jnp.concatenate([cols[:, :, 126:], cols[:, :, :2]], axis=2)
    return ends.reshape(2, 32, F, 4).transpose(0, 2, 1, 3).reshape(2, F, 128)


def extended(attributes):
    own = attributes.transpose(1, 2, 0, 3)
    ends = packed_ends(own.reshape(W * W, F, 128))
    zlo, zhi = both_ways(ends, ends, "gz", 8)
    lane = lax.broadcasted_iota(jnp.int32, ends.shape, 2)
    zown = jnp.where(lane % 4 < 2, zlo, zhi)

    def y_slice(s):
        return jnp.concatenate([own[:, s].reshape(2 * W, F, 128), zown])

    ylo, yhi = both_ways(y_slice(slice(W - 2, W)), y_slice(slice(0, 2)), "gy", 4)
    zy = [zown, ylo[2 * W:], yhi[2 * W:]]
    middle = jnp.concatenate(
        [ylo[:2 * W].reshape(W, 2, F, 128), own, yhi[:2 * W].reshape(W, 2, F, 128)], axis=1)

    def x_slice(s, half):
        return jnp.concatenate(
            [middle[s].reshape(2 * E, F, 128)] + [z[half:half + 1] for z in zy])

    xlo, xhi = both_ways(x_slice(slice(W - 2, W), 1), x_slice(slice(0, 2), 0), XS, 8)
    text = jnp.concatenate([xlo[:2 * E], middle.reshape(W * E, F, 128), xhi[:2 * E]])
    zt = jnp.concatenate(zy + [xlo[2 * E:], xhi[2 * E:]])
    return text, zt


def edges():
    gx, gy, gz = lax.axis_index(XS), lax.axis_index("gy"), lax.axis_index("gz")
    return jnp.stack([gx > 0, gx < 7, gy > 0, gy < 3, gz > 0, gz < 7]).astype(F32)


def per_device(attributes, start_centroids):
    text, zt = extended(attributes)
    edge = edges()
    packed = jnp.concatenate([start_centroids[8 * g:8 * g + 8] for g in range(4)], axis=1)
    cent = jnp.concatenate([packed, jnp.ones_like(packed)])
    for _ in range(UPDATES):
        memb, part = update(text, zt, cent, edge)
        cent = total_sums(part)
    packed = cent[:8] / cent[8:]
    centroids = jnp.concatenate([packed[:, 32 * g:32 * g + 32] for g in range(4)], axis=0)
    return centroids, memb.reshape(W, W, F, 128).transpose(2, 0, 1, 3)


def solution(mesh):
    split = Mesh(np.asarray(mesh.devices).reshape(4, 2, 4, 8), ("cx", "core", "gy", "gz"))
    placed = (P(None, XS, "gy", "gz"), P())
    return jax.shard_map(
        per_device,
        mesh=split,
        in_specs=placed,
        out_specs=(P(), P(None, XS, "gy", "gz")),
        check_vma=False,
    )
```

time: 259 us -> 94.9 us (0.37)
  blocking collectives: 156 us -> 36 us
  local copies, waits for them, and re-layouts: 38.7 us -> 7.06 us
  other arithmetic: 18.6 us -> 1.66 us
  Pallas kernels: 0 us -> 13 us
  starting transfers between devices: 32.2 us -> 19.7 us
  waiting for transfers between devices: 8.62 us -> 16 us
  matrix products: 3.14 us -> 0 us
    psum x2 -> x0, blocking collectives: 156 us -> none  [total_sums(): return lax.psum((numer, denom), ('gx', 'gy', 'gz'))]
    all_to_all x0 -> x3, blocking collectives: none -> 36 us  [gather_sum(): lax.all_to_all(jnp.broadcast_to(part[None], (count,) + part.shape), axes,...]
    ppermute x12 -> x8, starting transfers between devices: 32.2 us -> 16.3 us  [the longest x3 7.87 us: both_ways(): lo = lax.ppermute(up, axes, [(i, (i + 1) % count) for i in range(count)])]
    ppermute x8 -> x0, local copies, waits for them, and re-layouts: 14 us -> none  [the longest x4 7.86 us: extended(): lax.ppermute(tail, axis, [(i, (i + 1) % count) for i in range(ends)])]
    concatenate x6 -> x2, local copies, waits for them, and re-layouts: 13.6 us -> 0.52 us  [the longest x1 0.51 us: extended(): jnp.concatenate([ylo[:2 * W].reshape(W, 2, F, 128), own, yhi[:2 * W].resh...]
    pallas_call x0 -> x2, Pallas kernels: none -> 13 us  [update(): pl.pallas_call(update_kernel, out_shape=(jax.ShapeDtypeStruct((W * W, F,...]
    unnamed x43 -> x13, local copies, waits for them, and re-layouts: 9.09 us -> 1.57 us
    add x6 -> x2, other arithmetic: 5.91 us -> 0.01 us  [total_sums(): part = part + lax.ppermute(part, 'core', [(0, 1), (1, 0)])]
  transfers between devices with their start and end apart: 12 -> 9, of which waited for: 3 -> 7; matrix products, arithmetic and copies ran while one was open for 8% -> 2% of each run, Pallas kernels for 0% -> 0%
where the time goes in v1:
time: 94.9 us; the launch traced here: 94.3 us
  blocking collectives  36 us (38%)
  starting transfers between devices  19.7 us (21%)
  waiting for transfers between devices  16 us (17%)
  Pallas kernels  13 us (14%)
  local copies, waits for them, and re-layouts  7.06 us (7%)
  other arithmetic  1.66 us (2%)
    all_to_all x3, blocking collectives, gather_sum(): lax.all_to_all(jnp.broadcast_to(part[None], (count,) + part.shape), axes,...  36 us
    pallas_call x2, Pallas kernels, update(): pl.pallas_call(update_kernel, out_shape=(jax.ShapeDtypeStruct((W * W, F,...  13 us
    ppermute x3, starting transfers between devices, both_ways(): lo = lax.ppermute(up, axes, [(i, (i + 1) % count) for i in range(count)])  7.87 us
    ppermute x3, waiting for transfers between devices, both_ways(): lo = lax.ppermute(up, axes, [(i, (i + 1) % count) for i in range(count)])  5.68 us
    all_to_all x1, waiting for transfers between devices, gather_sum(): lax.all_to_all(jnp.broadcast_to(part[None], (count,) + part.shape), axes,...  5.67 us
    ppermute x3, starting transfers between devices, both_ways(): hi = lax.ppermute(down, axes, [((i + 1) % count, i) for i in range(count)])  5.57 us
    all_to_all x1, starting transfers between devices, gather_sum(): lax.all_to_all(jnp.broadcast_to(part[None], (count,) + part.shape), axes,...  3.35 us
    ppermute x2, starting transfers between devices, total_sums(): part = part + lax.ppermute(part, 'core', [(0, 1), (1, 0)])  2.91 us
  transfers between devices with their start and end apart: 9, of which 7 were waited for; matrix products, arithmetic and copies ran while one was open for 2% of the time, Pallas kernels for 0%

profile of v1, /device:TPU:1, one launch (start us, length us, event | category | flops | bytes accessed | tf_op | source)
XLA Modules:
  0.0 94.3 jit_solution(14136805099947959738)
XLA Ops:
  0.6 1.6 %fusion.4 = (bf16[64,32,2]{2,0,1:T(8,128)(2,1)S(1)}, bf16[64,32,2]{2,0,1:T(8,128)(2,1)S(1)}) fusion(bf16[64,32,128]{2,0,1:T(8,128)(2,1)} %bitcast.25), kind=kLoop, calls=%fused_computation.26 | loop fusion | bytes 32768 | tf_op jit(solution)/shard_map/slice | solution.py:183
  2.2 0.0 copy-start.2
  2.2 0.0 copy-start.3
  2.2 0.3 copy.42
  2.5 0.3 copy.43
  2.8 0.1 reshape.43
  2.9 0.1 copy.32
  3.1 0.1 copy.33
  3.1 2.5 %collective-permute-start = (bf16[2,32,128]{2,1,0:T(8,128)(2,1)S(1)}, bf16[2,32,128]{2,1,0:T(8,128)(2,1)S(1)}, u32[]{:S(2)}, u32[]{:S(2)}) collective-permute-start(bf16[2,32,128]{2,1,0:T(8,128)(2,1)S(1)} %copy.33), channel_id=1, source_target_pairs={{0,1},{1,2},{2,3},{3,4},{4,5},{5,6},{6,7},{7,0},{8,9},{9,10},{10,1... | collective-permute-start | bytes 49160 | tf_op jit(solution)/shard_map/ppermute | solution.py:166
  5.7 4.0 %collective-permute-start.1 = (bf16[2,32,128]{2,1,0:T(8,128)(2,1)S(1)}, bf16[2,32,128]{2,1,0:T(8,128)(2,1)S(1)}, u32[]{:S(2)}, u32[]{:S(2)}) collective-permute-start(bf16[2,32,128]{2,1,0:T(8,128)(2,1)S(1)} %copy.33), channel_id=1, source_target_pairs={{1,0},{2,1},{3,2},{4,3},{5,4},{6,5},{7,6},{0,7},{9,8},{10,9},{11,1... | collective-permute-start | bytes 49160 | tf_op jit(solution)/shard_map/ppermute | solution.py:167
  9.7 0.2 fusion.3
  9.9 0.1 select_maximum_fusion.cent
  10.1 0.1 stack.27
  10.2 0.5 collective-permute-done
  10.7 0.0 collective-permute-done.1
  10.8 1.4 %collective-permute-start.2 = (bf16[18,32,128]{2,1,0:T(8,128)(2,1)S(1)}, bf16[18,32,128]{2,1,0:T(8,128)(2,1)S(1)}, u32[]{:S(2)}, u32[]{:S(2)}) collective-permute-start(bf16[18,32,128]{2,1,0:T(8,128)(2,1)S(1)} %get-tuple-element.26), channel_id=1, source_target_pairs={{0,8},{8,16},{16,24},{24,0},{1,9},{9,17},{17,25},{25,1},{2,10},{10... | collective-permute-start | bytes 442376 | tf_op jit(solution)/shard_map/ppermute | solution.py:166
  12.2 1.5 %collective-permute-start.3 = (bf16[18,32,128]{2,1,0:T(8,128)(2,1)S(1)}, bf16[18,32,128]{2,1,0:T(8,128)(2,1)S(1)}, u32[]{:S(2)}, u32[]{:S(2)}) collective-permute-start(bf16[18,32,128]{2,1,0:T(8,128)(2,1)S(1)} %get-tuple-element.27), channel_id=1, source_target_pairs={{8,0},{16,8},{24,16},{0,24},{9,1},{17,9},{25,17},{1,25},{10,2},{18... | collective-permute-start | bytes 442376 | tf_op jit(solution)/shard_map/ppermute | solution.py:167
  13.7 2.4 %collective-permute-done.2 = bf16[18,32,128]{2,1,0:T(8,128)(2,1)S(1)} collective-permute-done((bf16[18,32,128]{2,1,0:T(8,128)(2,1)S(1)}, bf16[18,32,128]{2,1,0:T(8,128)(2,1)S(1)}, u32[]{:S(2)}, u32[]{:S(2)}) %collective-permute-start.2) | collective-permute-done | bytes 147488 | tf_op jit(solution)/shard_map/ppermute | solution.py:166
  16.1 0.1 copy.36
  16.2 0.0 collective-permute-done.3
  16.3 0.1 copy.37
  16.4 0.6 pad_maximum_fusion.1
  17.0 0.5 copy.39
  17.6 0.1 copy.38
  17.7 4.0 %collective-permute-start.4 = (bf16[27,32,128]{2,1,0:T(8,128)(2,1)S(1)}, bf16[27,32,128]{2,1,0:T(8,128)(2,1)S(1)}, u32[]{:S(2)}, u32[]{:S(2)}) collective-permute-start(bf16[27,32,128]{2,1,0:T(8,128)(2,1)S(1)} %pad_maximum_fusion.2), channel_id=1, source_target_pairs={{0,32},{32,64},{64,96},{96,128},{128,160},{160,192},{192,224},{224... | collective-permute-start | bytes 663560 | tf_op jit(solution)/shard_map/ppermute | solution.py:166
  21.7 0.1 copy.40
  21.8 0.0 collective-permute-start.5
  21.9 2.7 %collective-permute-done.4 = bf16[27,32,128]{2,1,0:T(8,128)(2,1)S(1)} collective-permute-done((bf16[27,32,128]{2,1,0:T(8,128)(2,1)S(1)}, bf16[27,32,128]{2,1,0:T(8,128)(2,1)S(1)}, u32[]{:S(2)}, u32[]{:S(2)}) %collective-permute-start.4) | collective-permute-done | bytes 221216 | tf_op jit(solution)/shard_map/ppermute | solution.py:166
  24.6 2.6 %collective-permute-done.5 = bf16[27,32,128]{2,1,0:T(8,128)(2,1)S(1)} collective-permute-done((bf16[27,32,128]{2,1,0:T(8,128)(2,1)S(1)}, bf16[27,32,128]{2,1,0:T(8,128)(2,1)S(1)}, u32[]{:S(2)}, u32[]{:S(2)}) %collective-permute-start.5) | collective-permute-done | bytes 221216 | tf_op jit(solution)/shard_map/ppermute | solution.py:167
  27.2 0.0 copy-start
  27.2 0.0 copy-start.1
  27.2 0.1 pad_maximum_fusion.text
  27.4 0.9 copy-done
  28.3 6.9 %shard_map.77 = (f32[64,32,128]{2,1,0:T(8,128)}, f32[16,128]{1,0:T(8,128)S(1)}) custom-call(bf16[144,32,128]{2,1,0:T(8,128)(2,1)S(1)} %pad_maximum_fusion.text, bf16[12,32,128]{2,1,0:T(8,128)(2,1)S(1)} %slice_dynamic-update-slice_fusion.zt, f32[16,128]{1,0:T(8,128)S(1)} %select_maximum_fusion.cent, f32[6]{0:T(128)S(1)} %convert_element_type.3.edge, ...), custom_call_target="tpu_custom_call" | custom-call | tf_op jit(solution)/shard_map/pallas_call | solution.py:149
  35.3 0.0 collective-permute-start.6
  35.3 1.2 %collective-permute-done.6 = f32[16,128]{1,0:T(8,128)S(1)} collective-permute-done((f32[16,128]{1,0:T(8,128)S(1)}, f32[16,128]{1,0:T(8,128)S(1)}, u32[]{:S(2)}, u32[]{:S(2)}) %collective-permute-start.6) | collective-permute-done | bytes 8224 | tf_op jit(solution)/shard_map/ppermute | solution.py:177
  36.5 12.9 %all_to_all.20 = f32[16,16,128]{2,1,0:T(8,128)S(1)} all-to-all(f32[16,16,128]{2,1,0:T(8,128)S(1)} %broadcast_in_dim.8), channel_id=1, replica_groups=mesh['cx'=4,'core'=2,'gy'=4,'gz'=8] {'cx','gy'}, dimensions={0} | all-to-all | bytes 262144 | tf_op jit(solution)/shard_map/all_to_all | solution.py:172
  49.4 13.3 %all_to_all.21 = f32[8,16,128]{2,1,0:T(8,128)S(1)} all-to-all(f32[8,16,128]{2,1,0:T(8,128)S(1)} %broadcast_in_dim.9), channel_id=1, replica_groups=mesh['cx'=4,'core'=2,'gy'=4,'gz'=8] {'gz'}, dimensions={0} | all-to-all | bytes 131072 | tf_op jit(solution)/shard_map/all_to_all | solution.py:172
  62.7 6.1 %shard_map.78 = (f32[64,32,128]{2,1,0:T(8,128)S(1)}, f32[16,128]{1,0:T(8,128)S(1)}) custom-call(bf16[144,32,128]{2,1,0:T(8,128)(2,1)S(1)} %pad_maximum_fusion.text, bf16[12,32,128]{2,1,0:T(8,128)(2,1)S(1)} %slice_dynamic-update-slice_fusion.zt, f32[16,128]{1,0:T(8,128)S(1)} %reduce_sum.37.cent, f32[6]{0:T(128)S(1)} %convert_element_type.3.edge, ...), custom_call_target="tpu_custom_call" | custom-call | tf_op jit(solution)/shard_map/pallas_call | solution.py:149
  68.8 2.9 %collective-permute-start.7 = (f32[16,128]{1,0:T(8,128)S(1)}, f32[16,128]{1,0:T(8,128)S(1)}, u32[]{:S(2)}, u32[]{:S(2)}) collective-permute-start(f32[16,128]{1,0:T(8,128)S(1)} %get-tuple-element.6), channel_id=1, source_target_pairs={{0,32},{32,0},{1,33},{33,1},{2,34},{34,2},{3,35},{35,3},{4,36},{36... | collective-permute-start | bytes 24584 | tf_op jit(solution)/shard_map/ppermute | solution.py:177
  71.7 0.8 collective-permute-done.7
  72.6 9.8 %all_to_all.22 = f32[16,16,128]{2,1,0:T(8,128)S(1)} all-to-all(f32[16,16,128]{2,1,0:T(8,128)S(1)} %broadcast_in_dim.10), channel_id=1, replica_groups=mesh['cx'=4,'core'=2,'gy'=4,'gz'=8] {'cx','gy'}, dimensions={0} | all-to-all | bytes 262144 | tf_op jit(solution)/shard_map/all_to_all | solution.py:172
  82.4 0.6 broadcast_in_dim.11
  83.0 3.3 %all-to-all-start.3 = ((f32[8,16,128]{2,1,0:T(8,128)}), f32[8,16,128]{2,1,0:T(8,128)S(1)}, u32[]{:S(2)}, u32[]{:S(2)}) async-start(f32[8,16,128]{2,1,0:T(8,128)} %broadcast_in_dim.11), calls=%async_computation.3 | async-start | bytes 131072 | tf_op jit(solution)/shard_map/all_to_all | solution.py:172
  86.4 1.6 %copy.45 = f32[8,8,32,128]{3,1,0,2:T(8,128)} copy(f32[8,8,32,128]{3,2,1,0:T(8,128)S(1)} %bitcast.24) | data formatting | bytes 2097152 | tf_op jit(solution)/shard_map/reshape | solution.py:227
  88.0 5.7 %all-to-all-done.3 = f32[8,16,128]{2,1,0:T(8,128)S(1)} async-done(((f32[8,16,128]{2,1,0:T(8,128)}), f32[8,16,128]{2,1,0:T(8,128)S(1)}, u32[]{:S(2)}, u32[]{:S(2)}) %all-to-all-start.3) | async-done | bytes 65568 | tf_op jit(solution)/shard_map/all_to_all | solution.py:172
  93.6 0.1 fusion.9
  93.7 0.6 pad_maximum_fusion.7
  (36 shorter events, 0.5 us)
Async XLA Ops:
  2.2 7.5 %copy-start.2 = (bf16[32,8,8,128]{3,2,1,0:T(8,128)(2,1)S(1)}, bf16[32,8,8,128]{3,2,1,0:T(8,128)(2,1)}, u32[]{:S(2)}) copy-start(bf16[32,8,8,128]{3,2,1,0:T(8,128)(2,1)} %param.6) | copy-start | bytes 1572868
  2.2 7.7 %copy-start.3 = (f32[32,32]{1,0:T(8,128)S(1)}, f32[32,32]{1,0:T(8,128)}, u32[]{:S(2)}) copy-start(f32[32,32]{1,0:T(8,128)} %param.7) | copy-start | bytes 12292
  3.1 7.6 %collective-permute-start = (bf16[2,32,128]{2,1,0:T(8,128)(2,1)S(1)}, bf16[2,32,128]{2,1,0:T(8,128)(2,1)S(1)}, u32[]{:S(2)}, u32[]{:S(2)}) collective-permute-start(bf16[2,32,128]{2,1,0:T(8,128)(2,1)S(1)} %copy.33), channel_id=1, source_target_pairs={{0,1},{1,2},{2,3},{3,4},{4,5},{5,6},{6,7},{7,0},{8,9},{9,10},{10,1... | collective-permute-start | bytes 49160 | tf_op jit(solution)/shard_map/ppermute | solution.py:166
  5.7 5.1 %collective-permute-start.1 = (bf16[2,32,128]{2,1,0:T(8,128)(2,1)S(1)}, bf16[2,32,128]{2,1,0:T(8,128)(2,1)S(1)}, u32[]{:S(2)}, u32[]{:S(2)}) collective-permute-start(bf16[2,32,128]{2,1,0:T(8,128)(2,1)S(1)} %copy.33), channel_id=1, source_target_pairs={{1,0},{2,1},{3,2},{4,3},{5,4},{6,5},{7,6},{0,7},{9,8},{10,9},{11,1... | collective-permute-start | bytes 49160 | tf_op jit(solution)/shard_map/ppermute | solution.py:167
  10.8 5.3 %collective-permute-start.2 = (bf16[18,32,128]{2,1,0:T(8,128)(2,1)S(1)}, bf16[18,32,128]{2,1,0:T(8,128)(2,1)S(1)}, u32[]{:S(2)}, u32[]{:S(2)}) collective-permute-start(bf16[18,32,128]{2,1,0:T(8,128)(2,1)S(1)} %get-tuple-element.26), channel_id=1, source_target_pairs={{0,8},{8,16},{16,24},{24,0},{1,9},{9,17},{17,25},{25,1},{2,10},{10... | collective-permute-start | bytes 442376 | tf_op jit(solution)/shard_map/ppermute | solution.py:166
  12.2 4.1 %collective-permute-start.3 = (bf16[18,32,128]{2,1,0:T(8,128)(2,1)S(1)}, bf16[18,32,128]{2,1,0:T(8,128)(2,1)S(1)}, u32[]{:S(2)}, u32[]{:S(2)}) collective-permute-start(bf16[18,32,128]{2,1,0:T(8,128)(2,1)S(1)} %get-tuple-element.27), channel_id=1, source_target_pairs={{8,0},{16,8},{24,16},{0,24},{9,1},{17,9},{25,17},{1,25},{10,2},{18... | collective-permute-start | bytes 442376 | tf_op jit(solution)/shard_map/ppermute | solution.py:167
  17.7 6.8 %collective-permute-start.4 = (bf16[27,32,128]{2,1,0:T(8,128)(2,1)S(1)}, bf16[27,32,128]{2,1,0:T(8,128)(2,1)S(1)}, u32[]{:S(2)}, u32[]{:S(2)}) collective-permute-start(bf16[27,32,128]{2,1,0:T(8,128)(2,1)S(1)} %pad_maximum_fusion.2), channel_id=1, source_target_pairs={{0,32},{32,64},{64,96},{96,128},{128,160},{160,192},{192,224},{224... | collective-permute-start | bytes 663560 | tf_op jit(solution)/shard_map/ppermute | solution.py:166
  21.8 5.4 %collective-permute-start.5 = (bf16[27,32,128]{2,1,0:T(8,128)(2,1)S(1)}, bf16[27,32,128]{2,1,0:T(8,128)(2,1)S(1)}, u32[]{:S(2)}, u32[]{:S(2)}) collective-permute-start(bf16[27,32,128]{2,1,0:T(8,128)(2,1)S(1)} %pad_maximum_fusion.3), channel_id=1, source_target_pairs={{32,0},{64,32},{96,64},{128,96},{160,128},{192,160},{224,192},{0,2... | collective-permute-start | bytes 663560 | tf_op jit(solution)/shard_map/ppermute | solution.py:167
  27.2 1.1 %copy-start = (bf16[1536,256]{1,0:T(8,128)(2,1)S(1)}, bf16[1536,256]{1,0:T(8,128)(2,1)}, u32[]{:S(2)}) copy-start(bf16[1536,256]{1,0:T(8,128)(2,1)} %constant.49.clone.smat) | copy-start | bytes 2359300
  27.2 1.1 %copy-start.1 = (bf16[128,128]{1,0:T(8,128)(2,1)S(1)}, bf16[128,128]{1,0:T(8,128)(2,1)}, u32[]{:S(2)}) copy-start(bf16[128,128]{1,0:T(8,128)(2,1)} %constant.50.clone.band) | copy-start | bytes 98308
  35.3 1.2 %collective-permute-start.6 = (f32[16,128]{1,0:T(8,128)S(1)}, f32[16,128]{1,0:T(8,128)S(1)}, u32[]{:S(2)}, u32[]{:S(2)}) collective-permute-start(f32[16,128]{1,0:T(8,128)S(1)} %get-tuple-element.5), channel_id=1, source_target_pairs={{0,32},{32,0},{1,33},{33,1},{2,34},{34,2},{3,35},{35,3},{4,36},{36... | collective-permute-start | bytes 24584 | tf_op jit(solution)/shard_map/ppermute | solution.py:177
  68.8 3.7 %collective-permute-start.7 = (f32[16,128]{1,0:T(8,128)S(1)}, f32[16,128]{1,0:T(8,128)S(1)}, u32[]{:S(2)}, u32[]{:S(2)}) collective-permute-start(f32[16,128]{1,0:T(8,128)S(1)} %get-tuple-element.6), channel_id=1, source_target_pairs={{0,32},{32,0},{1,33},{33,1},{2,34},{34,2},{3,35},{35,3},{4,36},{36... | collective-permute-start | bytes 24584 | tf_op jit(solution)/shard_map/ppermute | solution.py:177
  83.0 10.6 %all-to-all-start.3 = ((f32[8,16,128]{2,1,0:T(8,128)}), f32[8,16,128]{2,1,0:T(8,128)S(1)}, u32[]{:S(2)}, u32[]{:S(2)}) async-start(f32[8,16,128]{2,1,0:T(8,128)} %broadcast_in_dim.11), calls=%async_computation.3 | async-start | bytes 131072 | tf_op jit(solution)/shard_map/all_to_all | solution.py:172

commit v2 on v1

--- a/solution.py
+++ b/solution.py
@@ -1,4 +1,3 @@
-import functools
 import jax
 import jax.numpy as jnp
 import numpy as np
@@ -55,16 +54,27 @@
     return r * (2.0 - x * r)
 
 
-def unpack_centroids(packed):
-    return jnp.concatenate([packed[:, 32 * g:32 * g + 32] for g in range(4)], axis=0)
+def unpacked_centroids(sums):
+    lane = lax.broadcasted_iota(jnp.int32, (8, 128), 1)
+    row = lax.broadcasted_iota(jnp.int32, (8, 128), 0)
+    denom = jnp.broadcast_to(sums[8:9, :], (8, 128))
+    parts = []
+    for g in range(4):
+        d = jnp.sum(jnp.where(lane == row + 8 * g, denom, 0.0), axis=1, keepdims=True)
+        parts.append(sums[0:8, 32 * g:32 * g + 32] / d)
+    return jnp.concatenate(parts, axis=0)
 
 
 def pack_rows(wide):
     return jnp.concatenate([wide[8 * g:8 * g + 8] for g in range(4)], axis=1)
 
 
+def dot_lanes(a, b):
+    return lax.dot_general(a, b, (((1,), (1,)), ((), ())), preferred_element_type=F32)
+
+
 def update_kernel(text, zt, cent, edge, smat, band, memb, part, inv_s, win_s):
-    c = unpack_centroids(cent[0:8, :] / cent[8:16, :])
+    c = unpacked_centroids(cent)
     cbm2 = (-2.0 * c.astype(BF16).astype(F32)).astype(BF16)
     csq1 = jnp.broadcast_to(jnp.sum(c * c, axis=1, keepdims=True) + 1.0, (F, 128))
     xlo, xhi, ylo, yhi, zlo, zhi = [edge[i] for i in range(6)]
@@ -83,8 +93,8 @@
     def normalised(inv, mask):
         return (inv * (recip(jnp.sum(inv, axis=0, keepdims=True)) * mask)).astype(BF16)
 
-    def front(X, carry):
-        mx = jnp.where(X < 2, xlo, jnp.where(X >= W + 2, xhi, 1.0))
+    def front(X):
+        mx = xlo if X < 2 else (xhi if X >= W + 2 else 1.0)
         rounded = []
         for Y in range(0, E, 2):
             pair = jnp.concatenate([text[X * E + Y], text[X * E + Y + 1]], axis=1)
@@ -100,9 +110,9 @@
         p = [cols[Y] + cols[Y + 1] for Y in range(E - 1)]
         for y in range(W):
             win_s[X * W + y] = p[y] + p[y + 2] + cols[y + 4]
-        return carry
-
-    lax.fori_loop(0, E, front, 0)
+
+    for X in range(E):
+        front(X)
 
     lane = lax.broadcasted_iota(jnp.int32, (1, 128), 1)
     mz = jnp.where(lane % 4 < 2, zlo, zhi)
@@ -119,7 +129,8 @@
     ends = (lane < 2) | (lane >= 126)
 
     numer = jnp.zeros((F, F), F32)
-    denom = jnp.zeros((F, 128), F32)
+    denom = jnp.zeros((8, F), F32)
+    ones = jnp.ones((8, W * 128), BF16)
     for x in range(W):
         ws, ts = [], []
         for y in range(W):
@@ -133,15 +144,13 @@
             m = prod * recip(jnp.sum(prod, axis=0, keepdims=True))
             memb[i] = m
             w = (m * m).astype(BF16)
-            denom = denom + w.astype(F32)
             ws.append(w)
             ts.append(text[(x + 2) * E + y + 2])
-        numer = numer + lax.dot_general(
-            jnp.concatenate(ws, axis=1), jnp.concatenate(ts, axis=1),
-            (((1,), (1,)), ((), ())), preferred_element_type=F32)
-    total = jnp.broadcast_to(jnp.sum(denom, axis=1, keepdims=True), (F, F))
+        w = jnp.concatenate(ws, axis=1)
+        numer = numer + dot_lanes(w, jnp.concatenate(ts, axis=1))
+        denom = denom + dot_lanes(ones, w)
     part[0:8, :] = pack_rows(numer)
-    part[8:16, :] = pack_rows(total)
+    part[8:9, :] = jnp.concatenate([denom[0:1]] * 4, axis=1)
 
 
 def update(text, zt, cent, edge):
@@ -150,7 +159,7 @@
         update_kernel,
         out_shape=(
             jax.ShapeDtypeStruct((W * W, F, 128), F32),
-            jax.ShapeDtypeStruct((16, 128), F32),
+            jax.ShapeDtypeStruct((9, 128), F32),
         ),
         in_specs=[vmem, vmem, vmem, pl.BlockSpec(memory_space=pltpu.SMEM), vmem, vmem],
         out_specs=(vmem, vmem),
@@ -174,9 +183,10 @@
 
 
 def total_sums(part):
+    part = part.reshape(9, 1, 128)
     part = part + lax.ppermute(part, "core", [(0, 1), (1, 0)])
-    part = gather_sum(part, ("cx", "gy"), 16)
-    return gather_sum(part, ("gz",), 8)
+    part = gather_sum(part, ("gz",), 8)
+    return gather_sum(part, ("cx", "gy"), 16).reshape(9, 128)
 
 
 def packed_ends(cols):
@@ -218,12 +228,12 @@
     text, zt = extended(attributes)
     edge = edges()
     packed = jnp.concatenate([start_centroids[8 * g:8 * g + 8] for g in range(4)], axis=1)
-    cent = jnp.concatenate([packed, jnp.ones_like(packed)])
+    cent = jnp.concatenate([packed, jnp.ones((1, 128), F32)])
     for _ in range(UPDATES):
         memb, part = update(text, zt, cent, edge)
         cent = total_sums(part)
-    packed = cent[:8] / cent[8:]
-    centroids = jnp.concatenate([packed[:, 32 * g:32 * g + 32] for g in range(4)], axis=0)
+    numer = cent[:8].reshape(8, 4, 32).transpose(1, 0, 2).reshape(F, F)
+    centroids = numer / cent[8, :F][:, None]
     return centroids, memb.reshape(W, W, F, 128).transpose(2, 0, 1, 3)
 
 

time: 94.9 us -> 88.5 us (0.933)
  Pallas kernels: 13 us -> 8.06 us
  blocking collectives: 36 us -> 34.9 us
    pallas_call x2, Pallas kernels: 13 us -> 8.06 us  [update(): pl.pallas_call(update_kernel, out_shape=(jax.ShapeDtypeStruct((W * W, F,...]
    all_to_all x3, blocking collectives: 36 us -> 34.9 us  [gather_sum(): lax.all_to_all(jnp.broadcast_to(part[None], (count,) + part.shape), axes,...]
  transfers between devices with their start and end apart: 9 -> 9, of which waited for: 7 -> 7; matrix products, arithmetic and copies ran while one was open for 2% -> 3% of each run, Pallas kernels for 0% -> 0%
where the time goes in v2:
time: 88.5 us; the launch traced here: 88 us
  blocking collectives  34.9 us (39%)
  starting transfers between devices  20.1 us (23%)
  waiting for transfers between devices  15.2 us (17%)
  Pallas kernels  8.06 us (9%)
  local copies, waits for them, and re-layouts  7.04 us (8%)
  other arithmetic  1.85 us (2%)
  between operations  0.95 us (1%)
    all_to_all x3, blocking collectives, gather_sum(): lax.all_to_all(jnp.broadcast_to(part[None], (count,) + part.shape), axes,...  34.9 us
    pallas_call x2, Pallas kernels, update(): pl.pallas_call(update_kernel, out_shape=(jax.ShapeDtypeStruct((W * W, F,...  8.06 us
    ppermute x3, starting transfers between devices, both_ways(): lo = lax.ppermute(up, axes, [(i, (i + 1) % count) for i in range(count)])  7.87 us
    ppermute x3, waiting for transfers between devices, both_ways(): lo = lax.ppermute(up, axes, [(i, (i + 1) % count) for i in range(count)])  5.68 us
    ppermute x3, starting transfers between devices, both_ways(): hi = lax.ppermute(down, axes, [((i + 1) % count, i) for i in range(count)])  5.57 us
    all_to_all x1, waiting for transfers between devices, gather_sum(): lax.all_to_all(jnp.broadcast_to(part[None], (count,) + part.shape), axes,...  4.88 us
    all_to_all x1, starting transfers between devices, gather_sum(): lax.all_to_all(jnp.broadcast_to(part[None], (count,) + part.shape), axes,...  3.5 us
    ppermute x2, starting transfers between devices, total_sums(): part = part + lax.ppermute(part, 'core', [(0, 1), (1, 0)])  3.12 us
  transfers between devices with their start and end apart: 9, of which 7 were waited for; matrix products, arithmetic and copies ran while one was open for 3% of the time, Pallas kernels for 0%

profile of v2, /device:TPU:1, one launch (start us, length us, event | category | flops | bytes accessed | tf_op | source)
XLA Modules:
  0.0 88.0 jit_solution(2961584229951090886)
XLA Ops:
  0.6 1.4 %fusion.4 = (bf16[64,32,2]{2,0,1:T(8,128)(2,1)S(1)}, bf16[64,32,2]{2,0,1:T(8,128)(2,1)S(1)}) fusion(bf16[64,32,128]{2,0,1:T(8,128)(2,1)} %bitcast.40), kind=kLoop, calls=%fused_computation.28 | loop fusion | bytes 32768 | tf_op jit(solution)/shard_map/slice | solution.py:193
  2.1 0.0 copy-start.2
  2.1 0.0 copy-start.3
  2.1 0.3 copy.67
  2.4 0.3 copy.68
  2.7 0.1 reshape.78
  2.8 0.1 copy.48
  2.9 0.1 copy.49
  3.0 2.5 %collective-permute-start = (bf16[2,32,128]{2,1,0:T(8,128)(2,1)S(1)}, bf16[2,32,128]{2,1,0:T(8,128)(2,1)S(1)}, u32[]{:S(2)}, u32[]{:S(2)}) collective-permute-start(bf16[2,32,128]{2,1,0:T(8,128)(2,1)S(1)} %copy.49), channel_id=1, source_target_pairs={{0,1},{1,2},{2,3},{3,4},{4,5},{5,6},{6,7},{7,0},{8,9},{9,10},{10,1... | collective-permute-start | bytes 49160 | tf_op jit(solution)/shard_map/ppermute | solution.py:175
  5.5 4.0 %collective-permute-start.1 = (bf16[2,32,128]{2,1,0:T(8,128)(2,1)S(1)}, bf16[2,32,128]{2,1,0:T(8,128)(2,1)S(1)}, u32[]{:S(2)}, u32[]{:S(2)}) collective-permute-start(bf16[2,32,128]{2,1,0:T(8,128)(2,1)S(1)} %copy.49), channel_id=1, source_target_pairs={{1,0},{2,1},{3,2},{4,3},{5,4},{6,5},{7,6},{0,7},{9,8},{10,9},{11,1... | collective-permute-start | bytes 49160 | tf_op jit(solution)/shard_map/ppermute | solution.py:176
  9.6 0.2 fusion.3
  9.8 0.1 select_maximum_fusion.cent
  9.9 0.1 stack.27
  10.1 0.5 collective-permute-done
  10.7 1.4 %collective-permute-start.2 = (bf16[18,32,128]{2,1,0:T(8,128)(2,1)S(1)}, bf16[18,32,128]{2,1,0:T(8,128)(2,1)S(1)}, u32[]{:S(2)}, u32[]{:S(2)}) collective-permute-start(bf16[18,32,128]{2,1,0:T(8,128)(2,1)S(1)} %get-tuple-element.26), channel_id=1, source_target_pairs={{0,8},{8,16},{16,24},{24,0},{1,9},{9,17},{17,25},{25,1},{2,10},{10... | collective-permute-start | bytes 442376 | tf_op jit(solution)/shard_map/ppermute | solution.py:175
  12.0 1.5 %collective-permute-start.3 = (bf16[18,32,128]{2,1,0:T(8,128)(2,1)S(1)}, bf16[18,32,128]{2,1,0:T(8,128)(2,1)S(1)}, u32[]{:S(2)}, u32[]{:S(2)}) collective-permute-start(bf16[18,32,128]{2,1,0:T(8,128)(2,1)S(1)} %get-tuple-element.27), channel_id=1, source_target_pairs={{8,0},{16,8},{24,16},{0,24},{9,1},{17,9},{25,17},{1,25},{10,2},{18... | collective-permute-start | bytes 442376 | tf_op jit(solution)/shard_map/ppermute | solution.py:176
  13.6 2.4 %collective-permute-done.2 = bf16[18,32,128]{2,1,0:T(8,128)(2,1)S(1)} collective-permute-done((bf16[18,32,128]{2,1,0:T(8,128)(2,1)S(1)}, bf16[18,32,128]{2,1,0:T(8,128)(2,1)S(1)}, u32[]{:S(2)}, u32[]{:S(2)}) %collective-permute-start.2) | collective-permute-done | bytes 147488 | tf_op jit(solution)/shard_map/ppermute | solution.py:175
  16.0 0.1 copy.52
  16.2 0.1 copy.53
  16.3 0.6 pad_maximum_fusion.1
  16.9 0.5 copy.55
  17.4 0.1 copy.54
  17.6 4.0 %collective-permute-start.4 = (bf16[27,32,128]{2,1,0:T(8,128)(2,1)S(1)}, bf16[27,32,128]{2,1,0:T(8,128)(2,1)S(1)}, u32[]{:S(2)}, u32[]{:S(2)}) collective-permute-start(bf16[27,32,128]{2,1,0:T(8,128)(2,1)S(1)} %pad_maximum_fusion.2), channel_id=1, source_target_pairs={{0,32},{32,64},{64,96},{96,128},{128,160},{160,192},{192,224},{224... | collective-permute-start | bytes 663560 | tf_op jit(solution)/shard_map/ppermute | solution.py:175
  21.6 0.1 copy.56
  21.7 0.0 collective-permute-start.5
  21.8 2.7 %collective-permute-done.4 = bf16[27,32,128]{2,1,0:T(8,128)(2,1)S(1)} collective-permute-done((bf16[27,32,128]{2,1,0:T(8,128)(2,1)S(1)}, bf16[27,32,128]{2,1,0:T(8,128)(2,1)S(1)}, u32[]{:S(2)}, u32[]{:S(2)}) %collective-permute-start.4) | collective-permute-done | bytes 221216 | tf_op jit(solution)/shard_map/ppermute | solution.py:175
  24.5 2.6 %collective-permute-done.5 = bf16[27,32,128]{2,1,0:T(8,128)(2,1)S(1)} collective-permute-done((bf16[27,32,128]{2,1,0:T(8,128)(2,1)S(1)}, bf16[27,32,128]{2,1,0:T(8,128)(2,1)S(1)}, u32[]{:S(2)}, u32[]{:S(2)}) %collective-permute-start.5) | collective-permute-done | bytes 221216 | tf_op jit(solution)/shard_map/ppermute | solution.py:176
  27.1 0.0 copy-start
  27.1 0.0 copy-start.1
  27.1 0.1 pad_maximum_fusion.text
  27.3 0.9 %copy-done = bf16[1536,256]{1,0:T(8,128)(2,1)S(1)} copy-done((bf16[1536,256]{1,0:T(8,128)(2,1)S(1)}, bf16[1536,256]{1,0:T(8,128)(2,1)}, u32[]{:S(2)}) %copy-start) | copy-done | bytes 786456
  28.2 4.4 %shard_map.77 = (f32[64,32,128]{2,1,0:T(8,128)}, f32[9,128]{1,0:T(8,128)S(1)}) custom-call(bf16[144,32,128]{2,1,0:T(8,128)(2,1)S(1)} %pad_maximum_fusion.text, bf16[12,32,128]{2,1,0:T(8,128)(2,1)S(1)} %slice_dynamic-update-slice_fusion.zt, f32[9,128]{1,0:T(8,128)S(1)} %select_maximum_fusion.cent, f32[6]{0:T(128)S(1)} %convert_element_type.3.edge, ...), custom_call_target="tpu_custom_call" | custom-call | tf_op jit(solution)/shard_map/pallas_call | solution.py:158
  32.6 0.0 collective-permute-start.6
  32.6 1.2 %collective-permute-done.6 = f32[9,1,128]{2,0,1:T(8,128)S(1)} collective-permute-done((f32[9,1,128]{2,0,1:T(8,128)S(1)}, f32[9,1,128]{2,0,1:T(8,128)S(1)}, u32[]{:S(2)}, u32[]{:S(2)}) %collective-permute-start.6) | collective-permute-done | bytes 4640 | tf_op jit(solution)/shard_map/ppermute | solution.py:187
  33.8 12.8 %all_to_all.20 = f32[8,9,1,128]{3,2,1,0:T(1,128)S(1)} all-to-all(f32[8,9,1,128]{3,2,1,0:T(1,128)S(1)} %broadcast_in_dim.13), channel_id=1, replica_groups=mesh['cx'=4,'core'=2,'gy'=4,'gz'=8] {'gz'}, dimensions={0} | all-to-all | bytes 73728 | tf_op jit(solution)/shard_map/all_to_all | solution.py:181
  46.7 12.7 %all_to_all.21 = f32[16,9,1,128]{3,2,1,0:T(1,128)S(1)} all-to-all(f32[16,9,1,128]{3,2,1,0:T(1,128)S(1)} %broadcast_in_dim.14), channel_id=1, replica_groups=mesh['cx'=4,'core'=2,'gy'=4,'gz'=8] {'cx','gy'}, dimensions={0} | all-to-all | bytes 147456 | tf_op jit(solution)/shard_map/all_to_all | solution.py:181
  59.5 0.1 reduce_sum.37.cent
  59.5 3.7 %shard_map.78 = (f32[64,32,128]{2,1,0:T(8,128)S(1)}, f32[9,128]{1,0:T(8,128)S(1)}) custom-call(bf16[144,32,128]{2,1,0:T(8,128)(2,1)S(1)} %pad_maximum_fusion.text, bf16[12,32,128]{2,1,0:T(8,128)(2,1)S(1)} %slice_dynamic-update-slice_fusion.zt, f32[9,128]{1,0:T(8,128)S(1)} %reduce_sum.37.cent, f32[6]{0:T(128)S(1)} %convert_element_type.3.edge, ...), custom_call_target="tpu_custom_call" | custom-call | tf_op jit(solution)/shard_map/pallas_call | solution.py:158
  63.2 3.1 %collective-permute-start.7 = (f32[9,1,128]{2,0,1:T(8,128)S(1)}, f32[9,1,128]{2,0,1:T(8,128)S(1)}, u32[]{:S(2)}, u32[]{:S(2)}) collective-permute-start(f32[9,1,128]{2,0,1:T(8,128)S(1)} %bitcast.38), channel_id=1, source_target_pairs={{0,32},{32,0},{1,33},{33,1},{2,34},{34,2},{3,35},{35,3},{4,36},{36... | collective-permute-start | bytes 13832 | tf_op jit(solution)/shard_map/ppermute | solution.py:187
  66.3 0.8 collective-permute-done.7
  67.2 9.3 %all_to_all.22 = f32[8,9,1,128]{3,2,1,0:T(1,128)S(1)} all-to-all(f32[8,9,1,128]{3,2,1,0:T(1,128)S(1)} %broadcast_in_dim.16), channel_id=1, replica_groups=mesh['cx'=4,'core'=2,'gy'=4,'gz'=8] {'gz'}, dimensions={0} | all-to-all | bytes 73728 | tf_op jit(solution)/shard_map/all_to_all | solution.py:181
  76.5 0.7 broadcast_in_dim.34
  77.2 3.5 %all-to-all-start.3 = ((f32[16,9,1,128]{3,2,1,0:T(1,128)}), f32[16,9,1,128]{3,2,1,0:T(1,128)S(1)}, u32[]{:S(2)}, u32[]{:S(2)}) async-start(f32[16,9,1,128]{3,2,1,0:T(1,128)} %broadcast_in_dim.34), calls=%async_computation.3 | async-start | bytes 147456 | tf_op jit(solution)/shard_map/all_to_all | solution.py:181
  80.7 1.6 %copy.73 = f32[8,8,32,128]{3,1,0,2:T(8,128)} copy(f32[8,8,32,128]{3,2,1,0:T(8,128)S(1)} %bitcast.37) | data formatting | bytes 2097152 | tf_op jit(solution)/shard_map/reshape | solution.py:237
  82.3 4.9 %all-to-all-done.3 = f32[16,9,1,128]{3,2,1,0:T(1,128)S(1)} async-done(((f32[16,9,1,128]{3,2,1,0:T(1,128)}), f32[16,9,1,128]{3,2,1,0:T(1,128)S(1)}, u32[]{:S(2)}, u32[]{:S(2)}) %all-to-all-start.3) | async-done | bytes 73760 | tf_op jit(solution)/shard_map/all_to_all | solution.py:181
  87.1 0.1 reduce_sum.39
  87.2 0.1 reshape.88
  87.3 0.7 bitcast_divide_fusion
  (37 shorter events, 0.5 us)
Async XLA Ops:
  2.1 7.5 %copy-start.2 = (bf16[32,8,8,128]{3,2,1,0:T(8,128)(2,1)S(1)}, bf16[32,8,8,128]{3,2,1,0:T(8,128)(2,1)}, u32[]{:S(2)}) copy-start(bf16[32,8,8,128]{3,2,1,0:T(8,128)(2,1)} %param.6) | copy-start | bytes 1572868
  2.1 7.7 %copy-start.3 = (f32[32,32]{1,0:T(8,128)S(1)}, f32[32,32]{1,0:T(8,128)}, u32[]{:S(2)}) copy-start(f32[32,32]{1,0:T(8,128)} %param.7) | copy-start | bytes 12292
  3.0 7.6 %collective-permute-start = (bf16[2,32,128]{2,1,0:T(8,128)(2,1)S(1)}, bf16[2,32,128]{2,1,0:T(8,128)(2,1)S(1)}, u32[]{:S(2)}, u32[]{:S(2)}) collective-permute-start(bf16[2,32,128]{2,1,0:T(8,128)(2,1)S(1)} %copy.49), channel_id=1, source_target_pairs={{0,1},{1,2},{2,3},{3,4},{4,5},{5,6},{6,7},{7,0},{8,9},{9,10},{10,1... | collective-permute-start | bytes 49160 | tf_op jit(solution)/shard_map/ppermute | solution.py:175
  5.5 5.1 %collective-permute-start.1 = (bf16[2,32,128]{2,1,0:T(8,128)(2,1)S(1)}, bf16[2,32,128]{2,1,0:T(8,128)(2,1)S(1)}, u32[]{:S(2)}, u32[]{:S(2)}) collective-permute-start(bf16[2,32,128]{2,1,0:T(8,128)(2,1)S(1)} %copy.49), channel_id=1, source_target_pairs={{1,0},{2,1},{3,2},{4,3},{5,4},{6,5},{7,6},{0,7},{9,8},{10,9},{11,1... | collective-permute-start | bytes 49160 | tf_op jit(solution)/shard_map/ppermute | solution.py:176
  10.7 5.3 %collective-permute-start.2 = (bf16[18,32,128]{2,1,0:T(8,128)(2,1)S(1)}, bf16[18,32,128]{2,1,0:T(8,128)(2,1)S(1)}, u32[]{:S(2)}, u32[]{:S(2)}) collective-permute-start(bf16[18,32,128]{2,1,0:T(8,128)(2,1)S(1)} %get-tuple-element.26), channel_id=1, source_target_pairs={{0,8},{8,16},{16,24},{24,0},{1,9},{9,17},{17,25},{25,1},{2,10},{10... | collective-permute-start | bytes 442376 | tf_op jit(solution)/shard_map/ppermute | solution.py:175
  12.0 4.1 %collective-permute-start.3 = (bf16[18,32,128]{2,1,0:T(8,128)(2,1)S(1)}, bf16[18,32,128]{2,1,0:T(8,128)(2,1)S(1)}, u32[]{:S(2)}, u32[]{:S(2)}) collective-permute-start(bf16[18,32,128]{2,1,0:T(8,128)(2,1)S(1)} %get-tuple-element.27), channel_id=1, source_target_pairs={{8,0},{16,8},{24,16},{0,24},{9,1},{17,9},{25,17},{1,25},{10,2},{18... | collective-permute-start | bytes 442376 | tf_op jit(solution)/shard_map/ppermute | solution.py:176
  17.6 6.8 %collective-permute-start.4 = (bf16[27,32,128]{2,1,0:T(8,128)(2,1)S(1)}, bf16[27,32,128]{2,1,0:T(8,128)(2,1)S(1)}, u32[]{:S(2)}, u32[]{:S(2)}) collective-permute-start(bf16[27,32,128]{2,1,0:T(8,128)(2,1)S(1)} %pad_maximum_fusion.2), channel_id=1, source_target_pairs={{0,32},{32,64},{64,96},{96,128},{128,160},{160,192},{192,224},{224... | collective-permute-start | bytes 663560 | tf_op jit(solution)/shard_map/ppermute | solution.py:175
  21.7 5.4 %collective-permute-start.5 = (bf16[27,32,128]{2,1,0:T(8,128)(2,1)S(1)}, bf16[27,32,128]{2,1,0:T(8,128)(2,1)S(1)}, u32[]{:S(2)}, u32[]{:S(2)}) collective-permute-start(bf16[27,32,128]{2,1,0:T(8,128)(2,1)S(1)} %pad_maximum_fusion.3), channel_id=1, source_target_pairs={{32,0},{64,32},{96,64},{128,96},{160,128},{192,160},{224,192},{0,2... | collective-permute-start | bytes 663560 | tf_op jit(solution)/shard_map/ppermute | solution.py:176
  27.1 1.1 %copy-start = (bf16[1536,256]{1,0:T(8,128)(2,1)S(1)}, bf16[1536,256]{1,0:T(8,128)(2,1)}, u32[]{:S(2)}) copy-start(bf16[1536,256]{1,0:T(8,128)(2,1)} %constant.49.clone.smat) | copy-start | bytes 2359300
  27.1 1.1 %copy-start.1 = (bf16[128,128]{1,0:T(8,128)(2,1)S(1)}, bf16[128,128]{1,0:T(8,128)(2,1)}, u32[]{:S(2)}) copy-start(bf16[128,128]{1,0:T(8,128)(2,1)} %constant.50.clone.band) | copy-start | bytes 98308
  32.6 1.2 %collective-permute-start.6 = (f32[9,1,128]{2,0,1:T(8,128)S(1)}, f32[9,1,128]{2,0,1:T(8,128)S(1)}, u32[]{:S(2)}, u32[]{:S(2)}) collective-permute-start(f32[9,1,128]{2,0,1:T(8,128)S(1)} %bitcast.39), channel_id=1, source_target_pairs={{0,32},{32,0},{1,33},{33,1},{2,34},{34,2},{3,35},{35,3},{4,36},{36... | collective-permute-start | bytes 13832 | tf_op jit(solution)/shard_map/ppermute | solution.py:187
  63.2 3.9 %collective-permute-start.7 = (f32[9,1,128]{2,0,1:T(8,128)S(1)}, f32[9,1,128]{2,0,1:T(8,128)S(1)}, u32[]{:S(2)}, u32[]{:S(2)}) collective-permute-start(f32[9,1,128]{2,0,1:T(8,128)S(1)} %bitcast.38), channel_id=1, source_target_pairs={{0,32},{32,0},{1,33},{33,1},{2,34},{34,2},{3,35},{35,3},{4,36},{36... | collective-permute-start | bytes 13832 | tf_op jit(solution)/shard_map/ppermute | solution.py:187
  77.2 10.0 %all-to-all-start.3 = ((f32[16,9,1,128]{3,2,1,0:T(1,128)}), f32[16,9,1,128]{3,2,1,0:T(1,128)S(1)}, u32[]{:S(2)}, u32[]{:S(2)}) async-start(f32[16,9,1,128]{3,2,1,0:T(1,128)} %broadcast_in_dim.34), calls=%async_computation.3 | async-start | bytes 147456 | tf_op jit(solution)/shard_map/all_to_all | solution.py:181

commit v3 on v0

v3 whole, which is shorter than its diff:
```python
import jax
import jax.numpy as jnp
import numpy as np
from jax import lax
from jax.experimental import pallas as pl
from jax.experimental.pallas import tpu as pltpu
from jax.sharding import Mesh, PartitionSpec as P

F = 32
W = 8
E = W + 4
COLS = W * W
BF16 = jnp.bfloat16
F32 = jnp.float32
XS = ("cx", "core")
OUTER = (0, 1, W - 2, W - 1)
INNER = tuple(range(2, W - 2))


def z_tiles():
    near = [(0, dy, half) for dy in (0, -1, 1) for half in (0, 1)]
    far = [(dx, dy, half) for dx, half in ((-1, 1), (1, 0)) for dy in (0, -1, 1)]
    return near, far


def halo_matrix(tiles):
    src = []
    for dx, dy, half in tiles:
        for c in range(half * 32, half * 32 + 32):
            for t in range(4):
                src.append((dx * W + c // W, dy * W + c % W, (-2, -1, 128, 129)[t]))
    dst = [(c // W, c % W, (126, 127, 0, 1)[t]) for c in range(COLS) for t in range(4)]
    gap = np.abs(np.array(src)[:, None, :] - np.array(dst)[None, :, :])
    return (gap <= 2).all(-1).astype(np.float32)


def band_matrix():
    z = np.arange(128)
    return (np.abs(z[:, None] - z[None, :]) <= 2).astype(np.float32)


def recip(x):
    r = pl.reciprocal(x, approx=True)
    return r * (2.0 - x * r)


def dot_lanes(a, b):
    return lax.dot_general(a, b, (((1,), (1,)), ((), ())), preferred_element_type=F32)


def unpacked_centroids(sums):
    lane = lax.broadcasted_iota(jnp.int32, (8, 128), 1)
    row = lax.broadcasted_iota(jnp.int32, (8, 128), 0)
    denom = jnp.broadcast_to(sums[8:9, :], (8, 128))
    parts = []
    for g in range(4):
        d = jnp.sum(jnp.where(lane == row + 8 * g, denom, 0.0), axis=1, keepdims=True)
        parts.append(sums[0:8, 32 * g:32 * g + 32] / d)
    return jnp.concatenate(parts, axis=0)


def store_sums(part, numer, denom):
    part[0:8, :] = jnp.concatenate([numer[8 * g:8 * g + 8] for g in range(4)], axis=1)
    part[8:9, :] = jnp.concatenate([denom[0:1]] * 4, axis=1)


def prepare_kernel(attr, own, ends, rows):
    rows[...] = attr[...].astype(F32).reshape(F * COLS, 128)
    lane = lax.broadcasted_iota(jnp.int32, (1, 128), 1) // 4
    for half in range(2):
        acc = jnp.zeros((F, 128), F32)
        for j in range(32):
            c = half * 32 + j
            col = rows[pl.ds(c, F, stride=COLS), :]
            own[c] = col.astype(BF16)
            acc = jnp.where(lane == j, pltpu.roll(col, (4 * j + 2) % 128, 1), acc)
        ends[half] = acc.astype(BF16)


class Step:
    def __init__(self, cent, edge, band):
        c = unpacked_centroids(cent)
        self.cbm2 = (-2.0 * c.astype(BF16).astype(F32)).astype(BF16)
        self.csq1 = jnp.broadcast_to(jnp.sum(c * c, axis=1, keepdims=True) + 1.0, (F, 128))
        self.xlo, self.xhi, self.ylo, self.yhi, self.zlo, self.zhi = [edge[i] for i in range(6)]
        self.band = band
        self.lane = lax.broadcasted_iota(jnp.int32, (1, 128), 1)
        self.numer = jnp.zeros((F, F), F32)
        self.denom = jnp.zeros((8, F), F32)

    def inverse(self, a):
        af = a.astype(F32)
        sq = jnp.sum(af * af, axis=0, keepdims=True)
        cross = jnp.dot(self.cbm2, a, preferred_element_type=F32)
        return [
            recip(cross[:, s:s + 128] + self.csq1 + sq[:, s:s + 128])
            for s in range(0, a.shape[1], 128)
        ]

    def normalised(self, inv, mask):
        scale = recip(jnp.sum(inv, axis=0, keepdims=True))
        if mask is not None:
            scale = scale * mask
        return (inv * scale).astype(BF16)

    def front(self, X, column, keep):
        mx = self.xlo if X < 2 else (self.xhi if X >= W + 2 else None)
        rounded = []
        for Y in range(0, E, 2):
            my = self.ylo if Y < 2 else (self.yhi if Y >= W + 2 else None)
            m = mx if my is None else (my if mx is None else mx * my)
            pair = jnp.concatenate([column(X, Y), column(X, Y + 1)], axis=1)
            for i, inv in enumerate(self.inverse(pair)):
                if mx is None and my is None:
                    keep(Y + i - 2, inv)
                rounded.append(self.normalised(inv, m))
        z = jnp.dot(jnp.concatenate(rounded, axis=0), self.band[...], preferred_element_type=F32)
        cols = [z[F * Y:F * Y + F] for Y in range(E)]
        p = [cols[Y] + cols[Y + 1] for Y in range(E - 1)]
        return [p[y] + p[y + 2] + cols[y + 4] for y in range(W)]

    def halo(self, tiles, arrays, matrix):
        mz = jnp.where(self.lane % 4 < 2, self.zlo, self.zhi)
        rounded = []
        for (dx, dy, _), a in zip(tiles, arrays):
            m = mz
            if dx:
                m = m * (self.xlo if dx < 0 else self.xhi)
            if dy:
                m = m * (self.ylo if dy < 0 else self.yhi)
            rounded.append(self.normalised(self.inverse(a)[0], m))
        out = jnp.dot(jnp.concatenate(rounded, axis=1), matrix, preferred_element_type=F32)
        self.halves = out[:, :128], out[:, 128:]

    def halo_of(self, c):
        turned = pltpu.roll(self.halves[c // 32], (126 - 4 * (c % 32)) % 128, 1)
        return jnp.where((self.lane < 2) | (self.lane >= 126), turned, 0.0)

    def back(self, x, boxes, inv, own, memb=None):
        ws = []
        for y in range(W):
            prod = inv(y) * boxes[y]
            m = prod * recip(jnp.sum(prod, axis=0, keepdims=True))
            if memb is not None:
                memb[pl.ds(x * W + y, F, stride=COLS), :] = m
            ws.append((m * m).astype(BF16))
        w = jnp.concatenate(ws, axis=1)
        t = jnp.concatenate([own[x * W + y] for y in range(W)], axis=1)
        self.numer = self.numer + dot_lanes(w, t)
        self.denom = self.denom + dot_lanes(jnp.ones((8, W * 128), BF16), w)


def total(arrays):
    out = arrays[0]
    for a in arrays[1:]:
        out = out + a
    return out


def mid_column(own, ylo, yhi):
    def column(X, Y):
        x = X - 2
        if Y < 2:
            return ylo[x * 2 + Y]
        if Y >= W + 2:
            return yhi[x * 2 + Y - W - 2]
        return own[x * W + Y - 2]
    return column


def outer_column(xlo, xhi):
    def column(X, Y):
        ref, i = (xlo, X) if X < 2 else (xhi, X - W - 2)
        if Y < 2:
            return ref[16 + i * 2 + Y]
        if Y >= W + 2:
            return ref[20 + i * 2 + Y - W - 2]
        return ref[i * W + Y - 2]
    return column


def near_tiles(zown, ylo, yhi):
    return [zown[0], zown[1], ylo[16], ylo[17], yhi[16], yhi[17]]


def far_tiles(xlo, xhi):
    return [r[24 + i] for r in (xlo, xhi) for i in range(3)]


def inner_kernel(own, ylo, yhi, zown, cent, edge, band, near_hbm, box, kept, sums,
                 inv_s, win_s, near, sem):
    fetch = pltpu.make_async_copy(near_hbm, near, sem)
    fetch.start()
    step = Step(cent, edge, band)
    column = mid_column(own, ylo, yhi)
    for x in range(W):
        def keep(y, inv, x=x):
            if x in INNER:
                inv_s[(x - 2) * W + y] = inv
            else:
                kept[OUTER.index(x) * W + y] = inv
        for y, w in enumerate(step.front(x + 2, column, keep)):
            win_s[x * W + y] = w
    fetch.wait()
    step.halo(z_tiles()[0], near_tiles(zown, ylo, yhi), near[...])

    def mid_box(x, y):
        rows = range(max(x - 2, 0), min(x + 3, W))
        return total([win_s[r * W + y] for r in rows]) + step.halo_of(x * W + y)

    for x in INNER:
        step.back(x, [mid_box(x, y) for y in range(W)], lambda y: inv_s[(x - 2) * W + y], own)
    for i, x in enumerate(OUTER):
        for y in range(W):
            box[i * W + y] = mid_box(x, y)
    sums[0:F, :] = step.numer
    sums[F:F + 8, :] = step.denom


def outer_kernel(own, xlo, xhi, cent, edge, band, far_hbm, box, kept, sums, part,
                 win_s, far, sem):
    fetch = pltpu.make_async_copy(far_hbm, far, sem)
    fetch.start()
    step = Step(cent, edge, band)
    column = outer_column(xlo, xhi)
    rows = (0, 1, W + 2, W + 3)
    for i, X in enumerate(rows):
        for y, w in enumerate(step.front(X, column, None)):
            win_s[i * W + y] = w
    fetch.wait()
    step.halo(z_tiles()[1], far_tiles(xlo, xhi), far[...])
    for i, x in enumerate(OUTER):
        near = [n for n, X in enumerate(rows) if x <= X <= x + 4]
        boxes = [
            total([box[i * W + y]] + [win_s[n * W + y] for n in near]) + step.halo_of(x * W + y)
            for y in range(W)
        ]
        step.back(x, boxes, lambda y: kept[i * W + y], own)
    store_sums(part, step.numer + sums[0:F, :], step.denom + sums[F:F + 8, :])


def whole_kernel(own, ylo, yhi, xlo, xhi, zown, cent, edge, band, near_hbm, far_hbm, memb, part,
                 inv_s, win_s, matrix, sem):
    half = matrix.shape[0] // 2
    fetch = [
        pltpu.make_async_copy(near_hbm, matrix.at[0:half], sem.at[0]),
        pltpu.make_async_copy(far_hbm, matrix.at[half:2 * half], sem.at[1]),
    ]
    for f in fetch:
        f.start()
    step = Step(cent, edge, band)
    mid, outer = mid_column(own, ylo, yhi), outer_column(xlo, xhi)
    for X in range(E):
        def keep(y, inv, X=X):
            inv_s[(X - 2) * W + y] = inv
        for y, w in enumerate(step.front(X, mid if 2 <= X < W + 2 else outer, keep)):
            win_s[X * W + y] = w
    for f in fetch:
        f.wait()
    near, far = z_tiles()
    step.halo(near + far, near_tiles(zown, ylo, yhi) + far_tiles(xlo, xhi), matrix[...])
    for x in range(W):
        boxes = [
            total([win_s[X * W + y] for X in range(x, x + 5)]) + step.halo_of(x * W + y)
            for y in range(W)
        ]
        step.back(x, boxes, lambda y: inv_s[x * W + y], own, memb)
    store_sums(part, step.numer, step.denom)


VMEM = pl.BlockSpec(memory_space=pltpu.VMEM)
SMEM = pl.BlockSpec(memory_space=pltpu.SMEM)
ANY = pl.BlockSpec(memory_space=pl.ANY)


def call(kernel, out_shape, in_specs, scratch_shapes, flops, moved, args):
    return pl.pallas_call(
        kernel,
        out_shape=tuple(jax.ShapeDtypeStruct(s, t) for s, t in out_shape),
        in_specs=in_specs,
        out_specs=(VMEM,) * len(out_shape),
        scratch_shapes=scratch_shapes,
        compiler_params=pltpu.CompilerParams(vmem_limit_bytes=24 << 20),
        cost_estimate=pl.CostEstimate(flops=flops, bytes_accessed=moved, transcendentals=0),
    )(*args)


def columns(n, dtype=F32):
    return (n, F, 128), dtype


def prepare(attributes):
    return call(
        prepare_kernel, [columns(COLS, BF16), columns(2, BF16)], [VMEM],
        [pltpu.VMEM((F * COLS, 128), F32)], 10 ** 6, 1 << 20, (attributes,))


def inner_part(own, ylo, yhi, zown, cent, edge, band, near):
    return call(
        inner_kernel, [columns(4 * W), columns(4 * W), ((F + 8, F), F32)],
        [VMEM] * 5 + [SMEM, VMEM, ANY],
        [pltpu.VMEM(*columns(4 * W)), pltpu.VMEM(*columns(COLS)),
         pltpu.VMEM(near.shape, BF16), pltpu.SemaphoreType.DMA],
        5 * 10 ** 8, 3 << 20, (own, ylo, yhi, zown, cent, edge, band, near))


def outer_part(own, xlo, xhi, cent, edge, band, far, box, kept, sums):
    return call(
        outer_kernel, [((9, 128), F32)],
        [VMEM] * 4 + [SMEM, VMEM, ANY, VMEM, VMEM, VMEM],
        [pltpu.VMEM(*columns(4 * W)), pltpu.VMEM(far.shape, BF16), pltpu.SemaphoreType.DMA],
        2 * 10 ** 8, 2 << 20, (own, xlo, xhi, cent, edge, band, far, box, kept, sums))[0]


def whole_update(own, ylo, yhi, xlo, xhi, zown, cent, edge, band, near, far):
    return call(
        whole_kernel, [((F * COLS, 128), F32), ((9, 128), F32)],
        [VMEM] * 7 + [SMEM, VMEM, ANY, ANY],
        [pltpu.VMEM(*columns(COLS)), pltpu.VMEM(*columns(E * W)),
         pltpu.VMEM((2 * near.shape[0], near.shape[1]), BF16), pltpu.SemaphoreType.DMA((2,))],
        8 * 10 ** 8, 3 << 20, (own, ylo, yhi, xlo, xhi, zown, cent, edge, band, near, far))


def both_ways(up, down, axes, count):
    lo = lax.ppermute(up, axes, [(i, (i + 1) % count) for i in range(count)])
    hi = lax.ppermute(down, axes, [((i + 1) % count, i) for i in range(count)])
    return lo, hi


def gather_sum(part, axes, count):
    every = lax.all_to_all(jnp.broadcast_to(part[None], (count,) + part.shape), axes, 0, 0)
    return jnp.sum(every, axis=0)


def total_sums(part):
    part = part.reshape(9, 1, 128)
    part = part + lax.ppermute(part, "core", [(0, 1), (1, 0)])
    part = gather_sum(part, ("gz",), 8)
    return gather_sum(part, ("cx", "gy"), 16).reshape(9, 128)


def edges():
    gx, gy, gz = lax.axis_index(XS), lax.axis_index("gy"), lax.axis_index("gz")
    return jnp.stack([gx > 0, gx < 7, gy > 0, gy < 3, gz > 0, gz < 7]).astype(F32)


def per_device(attributes, start_centroids):
    edge = edges()
    band = jnp.asarray(band_matrix(), BF16)
    near, far = [jnp.asarray(halo_matrix(t), BF16) for t in z_tiles()]
    packed = start_centroids.reshape(4, 8, F).transpose(1, 0, 2).reshape(8, 128)
    cent = jnp.concatenate([packed, jnp.ones((1, 128), F32)])

    own, ends = prepare(attributes)
    zlo, zhi = both_ways(ends, ends, "gz", 8)
    lane = lax.broadcasted_iota(jnp.int32, ends.shape, 2)
    zown = jnp.where(lane % 4 < 2, zlo, zhi)

    grid = own.reshape(W, W, F, 128)

    def y_slice(y):
        return jnp.concatenate([grid[:, y:y + 2].reshape(2 * W, F, 128), zown])

    ylo, yhi = both_ways(y_slice(W - 2), y_slice(0), "gy", 4)

    def x_slice(x, half):
        return jnp.concatenate(
            [own[x * W:x * W + 2 * W], ylo[2 * x:2 * x + 4], yhi[2 * x:2 * x + 4],
             zown[half:half + 1], ylo[16 + half:17 + half], yhi[16 + half:17 + half]])

    xlo, xhi = both_ways(x_slice(W - 2, 1), x_slice(0, 0), XS, 8)

    box, kept, sums = inner_part(own, ylo, yhi, zown, cent, edge, band, near)
    part = outer_part(own, xlo, xhi, cent, edge, band, far, box, kept, sums)
    cent = total_sums(part)
    memb, part = whole_update(own, ylo, yhi, xlo, xhi, zown, cent, edge, band, near, far)
    cent = total_sums(part)
    numer = cent[:8].reshape(8, 4, F).transpose(1, 0, 2).reshape(F, F)
    return numer / cent[8, :F][:, None], memb.reshape(F, W, W, 128)


def solution(mesh):
    split = Mesh(np.asarray(mesh.devices).reshape(4, 2, 4, 8), ("cx", "core", "gy", "gz"))
    return jax.shard_map(
        per_device,
        mesh=split,
        in_specs=(P(None, XS, "gy", "gz"), P()),
        out_specs=(P(), P(None, XS, "gy", "gz")),
        check_vma=False,
    )
```

time: 259 us -> 83.2 us (0.32)
  blocking collectives: 156 us -> 39.9 us
  local copies, waits for them, and re-layouts: 38.7 us -> 2.81 us
  other arithmetic: 18.6 us -> 0.93 us
  starting transfers between devices: 32.2 us -> 18.1 us
  Pallas kernels: 0 us -> 11.9 us
  matrix products: 3.14 us -> 0 us
    psum x2 -> x0, blocking collectives: 156 us -> none  [total_sums(): return lax.psum((numer, denom), ('gx', 'gy', 'gz'))]
    all_to_all x0 -> x4, blocking collectives: none -> 39.9 us  [gather_sum(): lax.all_to_all(jnp.broadcast_to(part[None], (count,) + part.shape), axes,...]
    ppermute x12 -> x8, starting transfers between devices: 32.2 us -> 18.1 us  [the longest x3 11.6 us: both_ways(): hi = lax.ppermute(down, axes, [((i + 1) % count, i) for i in range(count)])]
    ppermute x8 -> x0, local copies, waits for them, and re-layouts: 14 us -> none  [the longest x4 7.86 us: extended(): lax.ppermute(tail, axis, [(i, (i + 1) % count) for i in range(ends)])]
    concatenate x6 -> x2, local copies, waits for them, and re-layouts: 13.6 us -> 0.02 us  [the longest x1 0.01 us: x_slice(): jnp.concatenate([own[x * W:x * W + 2 * W], ylo[2 * x:2 * x + 4], yhi[2 *...]
    pallas_call x0 -> x4, Pallas kernels: none -> 11.9 us  [call(): pl.pallas_call(kernel, out_shape=tuple((jax.ShapeDtypeStruct(s, t) for s,...]
    unnamed x43 -> x15, local copies, waits for them, and re-layouts: 9.09 us -> 2.37 us
    add x6 -> x0, other arithmetic: 5.91 us -> none  [window_sum(): total = total + lax.slice_in_dim(padded, shift, shift + count, axis=dim)]
  transfers between devices with their start and end apart: 12 -> 8, of which waited for: 3 -> 6; matrix products, arithmetic and copies ran while one was open for 8% -> 0% of each run, Pallas kernels for 0% -> 4%
where the time goes in v3:
time: 83.2 us; the launch traced here: 82.4 us
  blocking collectives  39.9 us (48%)
  starting transfers between devices  18.1 us (22%)
  Pallas kernels  11.9 us (14%)
  waiting for transfers between devices  7.94 us (10%)
  local copies, waits for them, and re-layouts  2.81 us (3%)
  other arithmetic  0.93 us (1%)
    all_to_all x4, blocking collectives, gather_sum(): lax.all_to_all(jnp.broadcast_to(part[None], (count,) + part.shape), axes,...  39.9 us
    pallas_call x4, Pallas kernels, call(): pl.pallas_call(kernel, out_shape=tuple((jax.ShapeDtypeStruct(s, t) for s,...  11.9 us
    ppermute x3, starting transfers between devices, both_ways(): hi = lax.ppermute(down, axes, [((i + 1) % count, i) for i in range(count)])  11.6 us
    ppermute x3, waiting for transfers between devices, both_ways(): lo = lax.ppermute(up, axes, [(i, (i + 1) % count) for i in range(count)])  5.35 us
    ppermute x2, starting transfers between devices, total_sums(): part = part + lax.ppermute(part, 'core', [(0, 1), (1, 0)])  4.09 us
    ppermute x3, starting transfers between devices, both_ways(): lo = lax.ppermute(up, axes, [(i, (i + 1) % count) for i in range(count)])  2.5 us
    unnamed x15, local copies, waits for them, and re-layouts  2.37 us
  transfers between devices with their start and end apart: 8, of which 6 were waited for; matrix products, arithmetic and copies ran while one was open for 0% of the time, Pallas kernels for 4%

profile of v3, /device:TPU:1, one launch (start us, length us, event | category | flops | bytes accessed | tf_op | source)
XLA Modules:
  0.0 82.4 jit_solution(1539080376655823806)
XLA Ops:
  0.6 0.0 copy-start
  0.6 1.0 %copy-done = bf16[32,8,8,128]{3,2,1,0:T(8,128)(2,1)S(1)} copy-done((bf16[32,8,8,128]{3,2,1,0:T(8,128)(2,1)S(1)}, bf16[32,8,8,128]{3,2,1,0:T(8,128)(2,1)}, u32[]{:S(2)}) %copy-start) | copy-done | bytes 524312
  1.7 0.8 shard_map.68
  2.4 6.5 %collective-permute-start.1 = (bf16[2,32,128]{2,1,0:T(8,128)(2,1)S(1)}, bf16[2,32,128]{2,1,0:T(8,128)(2,1)S(1)}, u32[]{:S(2)}, u32[]{:S(2)}) collective-permute-start(bf16[2,32,128]{2,1,0:T(8,128)(2,1)S(1)} %get-tuple-element.10), channel_id=1, source_target_pairs={{1,0},{2,1},{3,2},{4,3},{5,4},{6,5},{7,6},{0,7},{9,8},{10,9},{11,1... | collective-permute-start | bytes 49160 | tf_op jit(solution)/shard_map/ppermute | solution.py:326
  8.9 0.0 collective-permute-start
  9.0 0.8 %collective-permute-done.1 = bf16[2,32,128]{2,1,0:T(8,128)(2,1)S(1)} collective-permute-done((bf16[2,32,128]{2,1,0:T(8,128)(2,1)S(1)}, bf16[2,32,128]{2,1,0:T(8,128)(2,1)S(1)}, u32[]{:S(2)}, u32[]{:S(2)}) %collective-permute-start.1) | collective-permute-done | bytes 16416 | tf_op jit(solution)/shard_map/ppermute | solution.py:326
  9.8 2.9 %collective-permute-done = bf16[2,32,128]{2,1,0:T(8,128)(2,1)S(1)} collective-permute-done((bf16[2,32,128]{2,1,0:T(8,128)(2,1)S(1)}, bf16[2,32,128]{2,1,0:T(8,128)(2,1)S(1)}, u32[]{:S(2)}, u32[]{:S(2)}) %collective-permute-start) | collective-permute-done | bytes 16416 | tf_op jit(solution)/shard_map/ppermute | solution.py:325
  12.8 0.0 copy-start.3
  12.8 1.4 %collective-permute-start.2 = (bf16[18,32,128]{2,1,0:T(8,128)(2,1)S(1)}, bf16[18,32,128]{2,1,0:T(8,128)(2,1)S(1)}, u32[]{:S(2)}, u32[]{:S(2)}) collective-permute-start(bf16[18,32,128]{2,1,0:T(8,128)(2,1)S(1)} %get-tuple-element.31), channel_id=1, source_target_pairs={{0,8},{8,16},{16,24},{24,0},{1,9},{9,17},{17,25},{25,1},{2,10},{10... | collective-permute-start | bytes 442376 | tf_op jit(solution)/shard_map/ppermute | solution.py:325
  14.2 1.5 %collective-permute-start.3 = (bf16[18,32,128]{2,1,0:T(8,128)(2,1)S(1)}, bf16[18,32,128]{2,1,0:T(8,128)(2,1)S(1)}, u32[]{:S(2)}, u32[]{:S(2)}) collective-permute-start(bf16[18,32,128]{2,1,0:T(8,128)(2,1)S(1)} %get-tuple-element.30), channel_id=1, source_target_pairs={{8,0},{16,8},{24,16},{0,24},{9,1},{17,9},{25,17},{1,25},{10,2},{18... | collective-permute-start | bytes 442376 | tf_op jit(solution)/shard_map/ppermute | solution.py:326
  15.7 2.4 %collective-permute-done.2.ylo = bf16[18,32,128]{2,1,0:T(8,128)(2,1)S(1)} collective-permute-done((bf16[18,32,128]{2,1,0:T(8,128)(2,1)S(1)}, bf16[18,32,128]{2,1,0:T(8,128)(2,1)S(1)}, u32[]{:S(2)}, u32[]{:S(2)}) %collective-permute-start.2) | collective-permute-done | bytes 147488 | tf_op jit(solution)/shard_map/ppermute | solution.py:325
  18.1 0.1 collective-permute-done.3.yhi
  18.3 3.5 %collective-permute-start.5 = (bf16[27,32,128]{2,1,0:T(8,128)(2,1)S(1)}, bf16[27,32,128]{2,1,0:T(8,128)(2,1)S(1)}, u32[]{:S(2)}, u32[]{:S(2)}) collective-permute-start(bf16[27,32,128]{2,1,0:T(8,128)(2,1)S(1)} %get-tuple-element.20), channel_id=1, source_target_pairs={{32,0},{64,32},{96,64},{128,96},{160,128},{192,160},{224,192},{0,2... | collective-permute-start | bytes 663560 | tf_op jit(solution)/shard_map/ppermute | solution.py:326
  21.8 1.1 %collective-permute-start.4 = (bf16[27,32,128]{2,1,0:T(8,128)(2,1)S(1)}, bf16[27,32,128]{2,1,0:T(8,128)(2,1)S(1)}, u32[]{:S(2)}, u32[]{:S(2)}) collective-permute-start(bf16[27,32,128]{2,1,0:T(8,128)(2,1)S(1)} %get-tuple-element.21), channel_id=1, source_target_pairs={{0,32},{32,64},{64,96},{96,128},{128,160},{160,192},{192,224},{224... | collective-permute-start | bytes 663560 | tf_op jit(solution)/shard_map/ppermute | solution.py:325
  23.0 0.0 copy-start.4
  23.0 0.1 stack.27
  23.1 0.6 copy-done.4
  23.7 0.0 copy-start.2
  23.7 0.1 reshape.65
  23.8 0.0 copy-done.3
  23.8 0.7 copy-done.2
  24.4 0.0 copy-start.1
  24.4 2.9 %shard_map.69 = (f32[32,32,128]{2,1,0:T(8,128)S(1)}, f32[32,32,128]{2,1,0:T(8,128)S(1)}, f32[40,32]{1,0:T(8,128)S(1)}) custom-call(bf16[64,32,128]{2,1,0:T(8,128)(2,1)S(1)} %get-tuple-element.9.own, bf16[18,32,128]{2,1,0:T(8,128)(2,1)S(1)} %collective-permute-done.2.ylo, bf16[18,32,128]{2,1,0:T(8,128)(2,1)S(1)} %collective-permute-done.3.yhi, ...), custom_call_target="tpu_custom_call" | custom-call | flops 500000000 | bytes 3145728 | tf_op jit(solution)/shard_map/pallas_call | solution.py:277
  27.4 0.0 collective-permute-done.5.xhi
  27.4 0.0 collective-permute-done.4.xlo
  27.4 0.0 copy-done.1
  27.4 2.4 %shard_map.70 = f32[9,128]{1,0:T(8,128)S(1)} custom-call(bf16[64,32,128]{2,1,0:T(8,128)(2,1)S(1)} %get-tuple-element.9.own, bf16[27,32,128]{2,1,0:T(8,128)(2,1)S(1)} %collective-permute-done.4.xlo, bf16[27,32,128]{2,1,0:T(8,128)(2,1)S(1)} %collective-permute-done.5.xhi, f32[9,128]{1,0:T(8,128)S(1)} %concatenate.19.cent, f32[6]{0:T(128)S(1)} %convert_element_type.3.edge, ...), custom_call_target="tpu_custom_call" | custom-call | flops 200000000 | bytes 2097152 | tf_op jit(solution)/shard_map/pallas_call | solution.py:277
  29.8 1.1 %collective-permute-start.6 = (f32[9,1,128]{2,0,1:T(8,128)S(1)}, f32[9,1,128]{2,0,1:T(8,128)S(1)}, u32[]{:S(2)}, u32[]{:S(2)}) collective-permute-start(f32[9,1,128]{2,0,1:T(8,128)S(1)} %bitcast.28), channel_id=1, source_target_pairs={{0,32},{32,0},{1,33},{33,1},{2,34},{34,2},{3,35},{35,3},{4,36},{36... | collective-permute-start | bytes 13832 | tf_op jit(solution)/shard_map/ppermute | solution.py:337
  30.9 0.8 %collective-permute-done.6 = f32[9,1,128]{2,0,1:T(8,128)S(1)} collective-permute-done((f32[9,1,128]{2,0,1:T(8,128)S(1)}, f32[9,1,128]{2,0,1:T(8,128)S(1)}, u32[]{:S(2)}, u32[]{:S(2)}) %collective-permute-start.6) | collective-permute-done | bytes 4640 | tf_op jit(solution)/shard_map/ppermute | solution.py:337
  31.8 9.3 %all_to_all.20 = f32[8,9,1,128]{3,2,1,0:T(1,128)S(1)} all-to-all(f32[8,9,1,128]{3,2,1,0:T(1,128)S(1)} %broadcast_in_dim.13), channel_id=1, replica_groups=mesh['cx'=4,'core'=2,'gy'=4,'gz'=8] {'gz'}, dimensions={0} | all-to-all | bytes 73728 | tf_op jit(solution)/shard_map/all_to_all | solution.py:331
  41.1 11.8 %all_to_all.21 = f32[16,9,1,128]{3,2,1,0:T(1,128)S(1)} all-to-all(f32[16,9,1,128]{3,2,1,0:T(1,128)S(1)} %broadcast_in_dim.14), channel_id=1, replica_groups=mesh['cx'=4,'core'=2,'gy'=4,'gz'=8] {'cx','gy'}, dimensions={0} | all-to-all | bytes 147456 | tf_op jit(solution)/shard_map/all_to_all | solution.py:331
  52.9 0.1 reduce_sum.37.cent
  53.0 5.8 %shard_map.71 = (f32[2048,128]{1,0:T(8,128)}, f32[9,128]{1,0:T(8,128)S(1)}) custom-call(bf16[64,32,128]{2,1,0:T(8,128)(2,1)S(1)} %get-tuple-element.9.own, bf16[18,32,128]{2,1,0:T(8,128)(2,1)S(1)} %collective-permute-done.2.ylo, bf16[18,32,128]{2,1,0:T(8,128)(2,1)S(1)} %collective-permute-done.3.yhi, bf16[27,32,128]{2,1,0:T(8,128)(2,1)S(1)} %collective-permute-done.4.xlo, ...), custom_call_target="tpu_custom_call" | custom-call | flops 800000000 | bytes 3145728 | tf_op jit(solution)/shard_map/pallas_call | solution.py:277
  58.8 3.0 %collective-permute-start.7 = (f32[9,1,128]{2,0,1:T(8,128)S(1)}, f32[9,1,128]{2,0,1:T(8,128)S(1)}, u32[]{:S(2)}, u32[]{:S(2)}) collective-permute-start(f32[9,1,128]{2,0,1:T(8,128)S(1)} %bitcast.29), channel_id=1, source_target_pairs={{0,32},{32,0},{1,33},{33,1},{2,34},{34,2},{3,35},{35,3},{4,36},{36... | collective-permute-start | bytes 13832 | tf_op jit(solution)/shard_map/ppermute | solution.py:337
  61.8 0.8 %collective-permute-done.7 = f32[9,1,128]{2,0,1:T(8,128)S(1)} collective-permute-done((f32[9,1,128]{2,0,1:T(8,128)S(1)}, f32[9,1,128]{2,0,1:T(8,128)S(1)}, u32[]{:S(2)}, u32[]{:S(2)}) %collective-permute-start.7) | collective-permute-done | bytes 4640 | tf_op jit(solution)/shard_map/ppermute | solution.py:337
  62.6 9.3 %all_to_all.22 = f32[8,9,1,128]{3,2,1,0:T(1,128)S(1)} all-to-all(f32[8,9,1,128]{3,2,1,0:T(1,128)S(1)} %broadcast_in_dim.16), channel_id=1, replica_groups=mesh['cx'=4,'core'=2,'gy'=4,'gz'=8] {'gz'}, dimensions={0} | all-to-all | bytes 73728 | tf_op jit(solution)/shard_map/all_to_all | solution.py:331
  72.0 9.5 %all_to_all.23 = f32[16,9,1,128]{3,2,1,0:T(1,128)S(1)} all-to-all(f32[16,9,1,128]{3,2,1,0:T(1,128)S(1)} %broadcast_in_dim.34), channel_id=1, replica_groups=mesh['cx'=4,'core'=2,'gy'=4,'gz'=8] {'cx','gy'}, dimensions={0} | all-to-all | bytes 147456 | tf_op jit(solution)/shard_map/all_to_all | solution.py:331
  81.5 0.1 reduce_sum.39
  81.6 0.1 reshape.68
  81.7 0.7 bitcast_divide_fusion
  (24 shorter events, 0.4 us)
Async XLA Ops:
  0.6 1.0 %copy-start = (bf16[32,8,8,128]{3,2,1,0:T(8,128)(2,1)S(1)}, bf16[32,8,8,128]{3,2,1,0:T(8,128)(2,1)}, u32[]{:S(2)}) copy-start(bf16[32,8,8,128]{3,2,1,0:T(8,128)(2,1)} %attr.1) | copy-start | bytes 1572868
  2.4 7.3 %collective-permute-start.1 = (bf16[2,32,128]{2,1,0:T(8,128)(2,1)S(1)}, bf16[2,32,128]{2,1,0:T(8,128)(2,1)S(1)}, u32[]{:S(2)}, u32[]{:S(2)}) collective-permute-start(bf16[2,32,128]{2,1,0:T(8,128)(2,1)S(1)} %get-tuple-element.10), channel_id=1, source_target_pairs={{1,0},{2,1},{3,2},{4,3},{5,4},{6,5},{7,6},{0,7},{9,8},{10,9},{11,1... | collective-permute-start | bytes 49160 | tf_op jit(solution)/shard_map/ppermute | solution.py:326
  8.9 3.8 %collective-permute-start = (bf16[2,32,128]{2,1,0:T(8,128)(2,1)S(1)}, bf16[2,32,128]{2,1,0:T(8,128)(2,1)S(1)}, u32[]{:S(2)}, u32[]{:S(2)}) collective-permute-start(bf16[2,32,128]{2,1,0:T(8,128)(2,1)S(1)} %get-tuple-element.10), channel_id=1, source_target_pairs={{0,1},{1,2},{2,3},{3,4},{4,5},{5,6},{6,7},{7,0},{8,9},{9,10},{10,1... | collective-permute-start | bytes 49160 | tf_op jit(solution)/shard_map/ppermute | solution.py:325
  12.8 11.0 %copy-start.3 = (bf16[768,256]{1,0:T(8,128)(2,1)S(1)}, bf16[768,256]{1,0:T(8,128)(2,1)}, u32[]{:S(2)}) copy-start(bf16[768,256]{1,0:T(8,128)(2,1)} %constant.52.clone.near_hbm) | copy-start | bytes 1179652
  12.8 5.3 %collective-permute-start.2 = (bf16[18,32,128]{2,1,0:T(8,128)(2,1)S(1)}, bf16[18,32,128]{2,1,0:T(8,128)(2,1)S(1)}, u32[]{:S(2)}, u32[]{:S(2)}) collective-permute-start(bf16[18,32,128]{2,1,0:T(8,128)(2,1)S(1)} %get-tuple-element.31), channel_id=1, source_target_pairs={{0,8},{8,16},{16,24},{24,0},{1,9},{9,17},{17,25},{25,1},{2,10},{10... | collective-permute-start | bytes 442376 | tf_op jit(solution)/shard_map/ppermute | solution.py:325
  14.2 4.1 %collective-permute-start.3 = (bf16[18,32,128]{2,1,0:T(8,128)(2,1)S(1)}, bf16[18,32,128]{2,1,0:T(8,128)(2,1)S(1)}, u32[]{:S(2)}, u32[]{:S(2)}) collective-permute-start(bf16[18,32,128]{2,1,0:T(8,128)(2,1)S(1)} %get-tuple-element.30), channel_id=1, source_target_pairs={{8,0},{16,8},{24,16},{0,24},{9,1},{17,9},{25,17},{1,25},{10,2},{18... | collective-permute-start | bytes 442376 | tf_op jit(solution)/shard_map/ppermute | solution.py:326
  18.3 9.1 %collective-permute-start.5 = (bf16[27,32,128]{2,1,0:T(8,128)(2,1)S(1)}, bf16[27,32,128]{2,1,0:T(8,128)(2,1)S(1)}, u32[]{:S(2)}, u32[]{:S(2)}) collective-permute-start(bf16[27,32,128]{2,1,0:T(8,128)(2,1)S(1)} %get-tuple-element.20), channel_id=1, source_target_pairs={{32,0},{64,32},{96,64},{128,96},{160,128},{192,160},{224,192},{0,2... | collective-permute-start | bytes 663560 | tf_op jit(solution)/shard_map/ppermute | solution.py:326
  21.8 5.6 %collective-permute-start.4 = (bf16[27,32,128]{2,1,0:T(8,128)(2,1)S(1)}, bf16[27,32,128]{2,1,0:T(8,128)(2,1)S(1)}, u32[]{:S(2)}, u32[]{:S(2)}) collective-permute-start(bf16[27,32,128]{2,1,0:T(8,128)(2,1)S(1)} %get-tuple-element.21), channel_id=1, source_target_pairs={{0,32},{32,64},{64,96},{96,128},{128,160},{160,192},{192,224},{224... | collective-permute-start | bytes 663560 | tf_op jit(solution)/shard_map/ppermute | solution.py:325
  23.0 0.7 copy-start.4
  23.7 0.8 copy-start.2
  24.4 3.0 %copy-start.1 = (bf16[768,256]{1,0:T(8,128)(2,1)S(1)}, bf16[768,256]{1,0:T(8,128)(2,1)}, u32[]{:S(2)}) copy-start(bf16[768,256]{1,0:T(8,128)(2,1)} %constant.53.clone.far_hbm) | copy-start | bytes 1179652
  29.8 1.9 %collective-permute-start.6 = (f32[9,1,128]{2,0,1:T(8,128)S(1)}, f32[9,1,128]{2,0,1:T(8,128)S(1)}, u32[]{:S(2)}, u32[]{:S(2)}) collective-permute-start(f32[9,1,128]{2,0,1:T(8,128)S(1)} %bitcast.28), channel_id=1, source_target_pairs={{0,32},{32,0},{1,33},{33,1},{2,34},{34,2},{3,35},{35,3},{4,36},{36... | collective-permute-start | bytes 13832 | tf_op jit(solution)/shard_map/ppermute | solution.py:337
  58.8 3.8 %collective-permute-start.7 = (f32[9,1,128]{2,0,1:T(8,128)S(1)}, f32[9,1,128]{2,0,1:T(8,128)S(1)}, u32[]{:S(2)}, u32[]{:S(2)}) collective-permute-start(f32[9,1,128]{2,0,1:T(8,128)S(1)} %bitcast.29), channel_id=1, source_target_pairs={{0,32},{32,0},{1,33},{33,1},{2,34},{34,2},{3,35},{35,3},{4,36},{36... | collective-permute-start | bytes 13832 | tf_op jit(solution)/shard_map/ppermute | solution.py:337

commit v4 on v3

--- a/solution.py
+++ b/solution.py
@@ -75,6 +75,19 @@
             own[c] = col.astype(BF16)
             acc = jnp.where(lane == j, pltpu.roll(col, (4 * j + 2) % 128, 1), acc)
         ends[half] = acc.astype(BF16)
+
+
+def turned8(v):
+    row = lax.broadcasted_iota(jnp.int32, (8, 128), 0)
+    v = list(v)
+    for s in (4, 2, 1):
+        low = (row & s) == 0
+        for i in range(8):
+            if not i & s:
+                a, b = v[i], v[i + s]
+                v[i] = jnp.where(low, a, pltpu.roll(b, s, 0))
+                v[i + s] = jnp.where(low, pltpu.roll(a, 8 - s, 0), b)
+    return v
 
 
 class Step:
@@ -129,21 +142,24 @@
             if dy:
                 m = m * (self.ylo if dy < 0 else self.yhi)
             rounded.append(self.normalised(self.inverse(a)[0], m))
-        out = jnp.dot(jnp.concatenate(rounded, axis=1), matrix, preferred_element_type=F32)
-        self.halves = out[:, :128], out[:, 128:]
-
-    def halo_of(self, c):
-        turned = pltpu.roll(self.halves[c // 32], (126 - 4 * (c % 32)) % 128, 1)
+        return jnp.dot(jnp.concatenate(rounded, axis=1), matrix[...], preferred_element_type=F32)
+
+    def halo_of(self, windows, c):
+        half = windows[:, c // 32 * 128:c // 32 * 128 + 128]
+        turned = pltpu.roll(half, (126 - 4 * (c % 32)) % 128, 1)
         return jnp.where((self.lane < 2) | (self.lane >= 126), turned, 0.0)
 
     def back(self, x, boxes, inv, own, memb=None):
-        ws = []
+        ws, ms = [], []
         for y in range(W):
             prod = inv(y) * boxes[y]
             m = prod * recip(jnp.sum(prod, axis=0, keepdims=True))
-            if memb is not None:
-                memb[pl.ds(x * W + y, F, stride=COLS), :] = m
+            ms.append(m)
             ws.append((m * m).astype(BF16))
+        if memb is not None:
+            for g in range(4):
+                for k, rows in enumerate(turned8([m[8 * g:8 * g + 8] for m in ms])):
+                    memb[8 * g + k, x] = rows
         w = jnp.concatenate(ws, axis=1)
         t = jnp.concatenate([own[x * W + y] for y in range(W)], axis=1)
         self.numer = self.numer + dot_lanes(w, t)
@@ -187,12 +203,10 @@
     return [r[24 + i] for r in (xlo, xhi) for i in range(3)]
 
 
-def inner_kernel(own, ylo, yhi, zown, cent, edge, band, near_hbm, box, kept, sums,
-                 inv_s, win_s, near, sem):
-    fetch = pltpu.make_async_copy(near_hbm, near, sem)
-    fetch.start()
+def inner_kernel(own, ylo, yhi, zown, cent, edge, band, near, box, kept, sums, inv_s, win_s):
     step = Step(cent, edge, band)
     column = mid_column(own, ylo, yhi)
+    windows = step.halo(z_tiles()[0], near_tiles(zown, ylo, yhi), near)
     for x in range(W):
         def keep(y, inv, x=x):
             if x in INNER:
@@ -201,12 +215,10 @@
                 kept[OUTER.index(x) * W + y] = inv
         for y, w in enumerate(step.front(x + 2, column, keep)):
             win_s[x * W + y] = w
-    fetch.wait()
-    step.halo(z_tiles()[0], near_tiles(zown, ylo, yhi), near[...])
 
     def mid_box(x, y):
         rows = range(max(x - 2, 0), min(x + 3, W))
-        return total([win_s[r * W + y] for r in rows]) + step.halo_of(x * W + y)
+        return total([win_s[r * W + y] for r in rows]) + step.halo_of(windows, x * W + y)
 
     for x in INNER:
         step.back(x, [mid_box(x, y) for y in range(W)], lambda y: inv_s[(x - 2) * W + y], own)
@@ -217,51 +229,37 @@
     sums[F:F + 8, :] = step.denom
 
 
-def outer_kernel(own, xlo, xhi, cent, edge, band, far_hbm, box, kept, sums, part,
-                 win_s, far, sem):
-    fetch = pltpu.make_async_copy(far_hbm, far, sem)
-    fetch.start()
+def outer_kernel(own, xlo, xhi, cent, edge, band, far, box, kept, sums, part, win_s):
     step = Step(cent, edge, band)
     column = outer_column(xlo, xhi)
     rows = (0, 1, W + 2, W + 3)
+    windows = step.halo(z_tiles()[1], far_tiles(xlo, xhi), far)
     for i, X in enumerate(rows):
         for y, w in enumerate(step.front(X, column, None)):
             win_s[i * W + y] = w
-    fetch.wait()
-    step.halo(z_tiles()[1], far_tiles(xlo, xhi), far[...])
     for i, x in enumerate(OUTER):
         near = [n for n, X in enumerate(rows) if x <= X <= x + 4]
         boxes = [
-            total([box[i * W + y]] + [win_s[n * W + y] for n in near]) + step.halo_of(x * W + y)
+            total([box[i * W + y]] + [win_s[n * W + y] for n in near]) + step.halo_of(windows, x * W + y)
             for y in range(W)
         ]
         step.back(x, boxes, lambda y: kept[i * W + y], own)
     store_sums(part, step.numer + sums[0:F, :], step.denom + sums[F:F + 8, :])
 
 
-def whole_kernel(own, ylo, yhi, xlo, xhi, zown, cent, edge, band, near_hbm, far_hbm, memb, part,
-                 inv_s, win_s, matrix, sem):
-    half = matrix.shape[0] // 2
-    fetch = [
-        pltpu.make_async_copy(near_hbm, matrix.at[0:half], sem.at[0]),
-        pltpu.make_async_copy(far_hbm, matrix.at[half:2 * half], sem.at[1]),
-    ]
-    for f in fetch:
-        f.start()
+def whole_kernel(own, ylo, yhi, xlo, xhi, zown, cent, edge, band, near, far, memb, part, inv_s, win_s):
     step = Step(cent, edge, band)
     mid, outer = mid_column(own, ylo, yhi), outer_column(xlo, xhi)
+    windows = step.halo(z_tiles()[0], near_tiles(zown, ylo, yhi), near)
+    windows = windows + step.halo(z_tiles()[1], far_tiles(xlo, xhi), far)
     for X in range(E):
         def keep(y, inv, X=X):
             inv_s[(X - 2) * W + y] = inv
         for y, w in enumerate(step.front(X, mid if 2 <= X < W + 2 else outer, keep)):
             win_s[X * W + y] = w
-    for f in fetch:
-        f.wait()
-    near, far = z_tiles()
-    step.halo(near + far, near_tiles(zown, ylo, yhi) + far_tiles(xlo, xhi), matrix[...])
     for x in range(W):
         boxes = [
-            total([win_s[X * W + y] for X in range(x, x + 5)]) + step.halo_of(x * W + y)
+            total([win_s[X * W + y] for X in range(x, x + 5)]) + step.halo_of(windows, x * W + y)
             for y in range(W)
         ]
         step.back(x, boxes, lambda y: inv_s[x * W + y], own, memb)
@@ -270,7 +268,6 @@
 
 VMEM = pl.BlockSpec(memory_space=pltpu.VMEM)
 SMEM = pl.BlockSpec(memory_space=pltpu.SMEM)
-ANY = pl.BlockSpec(memory_space=pl.ANY)
 
 
 def call(kernel, out_shape, in_specs, scratch_shapes, flops, moved, args):
@@ -298,26 +295,24 @@
 def inner_part(own, ylo, yhi, zown, cent, edge, band, near):
     return call(
         inner_kernel, [columns(4 * W), columns(4 * W), ((F + 8, F), F32)],
-        [VMEM] * 5 + [SMEM, VMEM, ANY],
-        [pltpu.VMEM(*columns(4 * W)), pltpu.VMEM(*columns(COLS)),
-         pltpu.VMEM(near.shape, BF16), pltpu.SemaphoreType.DMA],
+        [VMEM] * 5 + [SMEM, VMEM, VMEM],
+        [pltpu.VMEM(*columns(4 * W)), pltpu.VMEM(*columns(COLS))],
         5 * 10 ** 8, 3 << 20, (own, ylo, yhi, zown, cent, edge, band, near))
 
 
 def outer_part(own, xlo, xhi, cent, edge, band, far, box, kept, sums):
     return call(
         outer_kernel, [((9, 128), F32)],
-        [VMEM] * 4 + [SMEM, VMEM, ANY, VMEM, VMEM, VMEM],
-        [pltpu.VMEM(*columns(4 * W)), pltpu.VMEM(far.shape, BF16), pltpu.SemaphoreType.DMA],
+        [VMEM] * 4 + [SMEM] + [VMEM] * 5,
+        [pltpu.VMEM(*columns(4 * W))],
         2 * 10 ** 8, 2 << 20, (own, xlo, xhi, cent, edge, band, far, box, kept, sums))[0]
 
 
 def whole_update(own, ylo, yhi, xlo, xhi, zown, cent, edge, band, near, far):
     return call(
-        whole_kernel, [((F * COLS, 128), F32), ((9, 128), F32)],
-        [VMEM] * 7 + [SMEM, VMEM, ANY, ANY],
-        [pltpu.VMEM(*columns(COLS)), pltpu.VMEM(*columns(E * W)),
-         pltpu.VMEM((2 * near.shape[0], near.shape[1]), BF16), pltpu.SemaphoreType.DMA((2,))],
+        whole_kernel, [((F, W, W, 128), F32), ((9, 128), F32)],
+        [VMEM] * 7 + [SMEM] + [VMEM] * 3,
+        [pltpu.VMEM(*columns(COLS)), pltpu.VMEM(*columns(E * W))],
         8 * 10 ** 8, 3 << 20, (own, ylo, yhi, xlo, xhi, zown, cent, edge, band, near, far))
 
 
@@ -376,7 +371,7 @@
     memb, part = whole_update(own, ylo, yhi, xlo, xhi, zown, cent, edge, band, near, far)
     cent = total_sums(part)
     numer = cent[:8].reshape(8, 4, F).transpose(1, 0, 2).reshape(F, F)
-    return numer / cent[8, :F][:, None], memb.reshape(F, W, W, 128)
+    return numer / cent[8, :F][:, None], memb
 
 
 def solution(mesh):

time: 83.2 us -> 80.8 us (0.971)
  Pallas kernels: 11.9 us -> 9.13 us
    pallas_call x4, Pallas kernels: 11.9 us -> 9.13 us  [call(): pl.pallas_call(kernel, out_shape=tuple((jax.ShapeDtypeStruct(s, t) for s,...]
  transfers between devices with their start and end apart: 8 -> 8, of which waited for: 6 -> 6; matrix products, arithmetic and copies ran while one was open for 0% -> 0% of each run, Pallas kernels for 4% -> 3%
where the time goes in v4:
time: 80.8 us; the launch traced here: 80 us
  blocking collectives  39.7 us (49%)
  starting transfers between devices  18.7 us (23%)
  Pallas kernels  9.13 us (11%)
  waiting for transfers between devices  7.96 us (10%)
  local copies, waits for them, and re-layouts  2.81 us (3%)
  other arithmetic  0.93 us (1%)
    all_to_all x4, blocking collectives, gather_sum(): lax.all_to_all(jnp.broadcast_to(part[None], (count,) + part.shape), axes,...  39.7 us
    ppermute x3, starting transfers between devices, both_ways(): hi = lax.ppermute(down, axes, [((i + 1) % count, i) for i in range(count)])  11.6 us
    pallas_call x4, Pallas kernels, call(): pl.pallas_call(kernel, out_shape=tuple((jax.ShapeDtypeStruct(s, t) for s,...  9.13 us
    ppermute x3, waiting for transfers between devices, both_ways(): lo = lax.ppermute(up, axes, [(i, (i + 1) % count) for i in range(count)])  5.35 us
    ppermute x2, starting transfers between devices, total_sums(): part = part + lax.ppermute(part, 'core', [(0, 1), (1, 0)])  4.62 us
    ppermute x3, starting transfers between devices, both_ways(): lo = lax.ppermute(up, axes, [(i, (i + 1) % count) for i in range(count)])  2.5 us
    unnamed x15, local copies, waits for them, and re-layouts  2.37 us
    ppermute x2, waiting for transfers between devices, total_sums(): part = part + lax.ppermute(part, 'core', [(0, 1), (1, 0)])  1.66 us
  transfers between devices with their start and end apart: 8, of which 6 were waited for; matrix products, arithmetic and copies ran while one was open for 0% of the time, Pallas kernels for 3%

profile of v4, /device:TPU:1, one launch (start us, length us, event | category | flops | bytes accessed | tf_op | source)
XLA Modules:
  0.0 80.0 jit_solution(17917059147479036577)
XLA Ops:
  0.6 0.0 copy-start
  0.6 1.0 %copy-done = bf16[32,8,8,128]{3,2,1,0:T(8,128)(2,1)S(1)} copy-done((bf16[32,8,8,128]{3,2,1,0:T(8,128)(2,1)S(1)}, bf16[32,8,8,128]{3,2,1,0:T(8,128)(2,1)}, u32[]{:S(2)}) %copy-start) | copy-done | bytes 524312
  1.7 0.8 shard_map.68
  2.4 6.5 %collective-permute-start.1 = (bf16[2,32,128]{2,1,0:T(8,128)(2,1)S(1)}, bf16[2,32,128]{2,1,0:T(8,128)(2,1)S(1)}, u32[]{:S(2)}, u32[]{:S(2)}) collective-permute-start(bf16[2,32,128]{2,1,0:T(8,128)(2,1)S(1)} %get-tuple-element.10), channel_id=1, source_target_pairs={{1,0},{2,1},{3,2},{4,3},{5,4},{6,5},{7,6},{0,7},{9,8},{10,9},{11,1... | collective-permute-start | bytes 49160 | tf_op jit(solution)/shard_map/ppermute | solution.py:321
  8.9 0.0 collective-permute-start
  9.0 0.8 %collective-permute-done.1 = bf16[2,32,128]{2,1,0:T(8,128)(2,1)S(1)} collective-permute-done((bf16[2,32,128]{2,1,0:T(8,128)(2,1)S(1)}, bf16[2,32,128]{2,1,0:T(8,128)(2,1)S(1)}, u32[]{:S(2)}, u32[]{:S(2)}) %collective-permute-start.1) | collective-permute-done | bytes 16416 | tf_op jit(solution)/shard_map/ppermute | solution.py:321
  9.8 2.9 %collective-permute-done = bf16[2,32,128]{2,1,0:T(8,128)(2,1)S(1)} collective-permute-done((bf16[2,32,128]{2,1,0:T(8,128)(2,1)S(1)}, bf16[2,32,128]{2,1,0:T(8,128)(2,1)S(1)}, u32[]{:S(2)}, u32[]{:S(2)}) %collective-permute-start) | collective-permute-done | bytes 16416 | tf_op jit(solution)/shard_map/ppermute | solution.py:320
  12.8 0.0 copy-start.3
  12.8 1.4 %collective-permute-start.2 = (bf16[18,32,128]{2,1,0:T(8,128)(2,1)S(1)}, bf16[18,32,128]{2,1,0:T(8,128)(2,1)S(1)}, u32[]{:S(2)}, u32[]{:S(2)}) collective-permute-start(bf16[18,32,128]{2,1,0:T(8,128)(2,1)S(1)} %get-tuple-element.31), channel_id=1, source_target_pairs={{0,8},{8,16},{16,24},{24,0},{1,9},{9,17},{17,25},{25,1},{2,10},{10... | collective-permute-start | bytes 442376 | tf_op jit(solution)/shard_map/ppermute | solution.py:320
  14.2 1.5 %collective-permute-start.3 = (bf16[18,32,128]{2,1,0:T(8,128)(2,1)S(1)}, bf16[18,32,128]{2,1,0:T(8,128)(2,1)S(1)}, u32[]{:S(2)}, u32[]{:S(2)}) collective-permute-start(bf16[18,32,128]{2,1,0:T(8,128)(2,1)S(1)} %get-tuple-element.30), channel_id=1, source_target_pairs={{8,0},{16,8},{24,16},{0,24},{9,1},{17,9},{25,17},{1,25},{10,2},{18... | collective-permute-start | bytes 442376 | tf_op jit(solution)/shard_map/ppermute | solution.py:321
  15.7 2.4 %collective-permute-done.2.ylo = bf16[18,32,128]{2,1,0:T(8,128)(2,1)S(1)} collective-permute-done((bf16[18,32,128]{2,1,0:T(8,128)(2,1)S(1)}, bf16[18,32,128]{2,1,0:T(8,128)(2,1)S(1)}, u32[]{:S(2)}, u32[]{:S(2)}) %collective-permute-start.2) | collective-permute-done | bytes 147488 | tf_op jit(solution)/shard_map/ppermute | solution.py:320
  18.1 0.1 collective-permute-done.3.yhi
  18.3 3.5 %collective-permute-start.5 = (bf16[27,32,128]{2,1,0:T(8,128)(2,1)S(1)}, bf16[27,32,128]{2,1,0:T(8,128)(2,1)S(1)}, u32[]{:S(2)}, u32[]{:S(2)}) collective-permute-start(bf16[27,32,128]{2,1,0:T(8,128)(2,1)S(1)} %get-tuple-element.20), channel_id=1, source_target_pairs={{32,0},{64,32},{96,64},{128,96},{160,128},{192,160},{224,192},{0,2... | collective-permute-start | bytes 663560 | tf_op jit(solution)/shard_map/ppermute | solution.py:321
  21.8 1.1 %collective-permute-start.4 = (bf16[27,32,128]{2,1,0:T(8,128)(2,1)S(1)}, bf16[27,32,128]{2,1,0:T(8,128)(2,1)S(1)}, u32[]{:S(2)}, u32[]{:S(2)}) collective-permute-start(bf16[27,32,128]{2,1,0:T(8,128)(2,1)S(1)} %get-tuple-element.21), channel_id=1, source_target_pairs={{0,32},{32,64},{64,96},{96,128},{128,160},{160,192},{192,224},{224... | collective-permute-start | bytes 663560 | tf_op jit(solution)/shard_map/ppermute | solution.py:320
  23.0 0.0 copy-start.4
  23.0 0.1 stack.27
  23.1 0.6 copy-done.4
  23.7 0.0 copy-start.2
  23.7 0.1 reshape.62
  23.8 0.0 copy-done.3
  23.8 0.7 copy-done.2
  24.4 0.0 copy-start.1
  24.4 2.4 %shard_map.69 = (f32[32,32,128]{2,1,0:T(8,128)S(1)}, f32[32,32,128]{2,1,0:T(8,128)S(1)}, f32[40,32]{1,0:T(8,128)S(1)}) custom-call(bf16[64,32,128]{2,1,0:T(8,128)(2,1)S(1)} %get-tuple-element.9.own, bf16[18,32,128]{2,1,0:T(8,128)(2,1)S(1)} %collective-permute-done.2.ylo, bf16[18,32,128]{2,1,0:T(8,128)(2,1)S(1)} %collective-permute-done.3.yhi, ...), custom_call_target="tpu_custom_call" | custom-call | flops 500000000 | bytes 3145728 | tf_op jit(solution)/shard_map/pallas_call | solution.py:274
  26.8 0.0 collective-permute-done.5.xhi
  26.9 0.0 collective-permute-done.4.xlo
  26.9 0.0 copy-done.1
  26.9 1.8 %shard_map.70 = f32[9,128]{1,0:T(8,128)S(1)} custom-call(bf16[64,32,128]{2,1,0:T(8,128)(2,1)S(1)} %get-tuple-element.9.own, bf16[27,32,128]{2,1,0:T(8,128)(2,1)S(1)} %collective-permute-done.4.xlo, bf16[27,32,128]{2,1,0:T(8,128)(2,1)S(1)} %collective-permute-done.5.xhi, f32[9,128]{1,0:T(8,128)S(1)} %concatenate.19.cent, f32[6]{0:T(128)S(1)} %convert_element_type.3.edge, ...), custom_call_target="tpu_custom_call" | custom-call | flops 200000000 | bytes 2097152 | tf_op jit(solution)/shard_map/pallas_call | solution.py:274
  28.7 1.6 %collective-permute-start.6 = (f32[9,1,128]{2,0,1:T(8,128)S(1)}, f32[9,1,128]{2,0,1:T(8,128)S(1)}, u32[]{:S(2)}, u32[]{:S(2)}) collective-permute-start(f32[9,1,128]{2,0,1:T(8,128)S(1)} %bitcast.27), channel_id=1, source_target_pairs={{0,32},{32,0},{1,33},{33,1},{2,34},{34,2},{3,35},{35,3},{4,36},{36... | collective-permute-start | bytes 13832 | tf_op jit(solution)/shard_map/ppermute | solution.py:332
  30.3 0.8 %collective-permute-done.6 = f32[9,1,128]{2,0,1:T(8,128)S(1)} collective-permute-done((f32[9,1,128]{2,0,1:T(8,128)S(1)}, f32[9,1,128]{2,0,1:T(8,128)S(1)}, u32[]{:S(2)}, u32[]{:S(2)}) %collective-permute-start.6) | collective-permute-done | bytes 4640 | tf_op jit(solution)/shard_map/ppermute | solution.py:332
  31.2 9.3 %all_to_all.20 = f32[8,9,1,128]{3,2,1,0:T(1,128)S(1)} all-to-all(f32[8,9,1,128]{3,2,1,0:T(1,128)S(1)} %broadcast_in_dim.13), channel_id=1, replica_groups=mesh['cx'=4,'core'=2,'gy'=4,'gz'=8] {'gz'}, dimensions={0} | all-to-all | bytes 73728 | tf_op jit(solution)/shard_map/all_to_all | solution.py:326
  40.6 11.6 %all_to_all.21 = f32[16,9,1,128]{3,2,1,0:T(1,128)S(1)} all-to-all(f32[16,9,1,128]{3,2,1,0:T(1,128)S(1)} %broadcast_in_dim.14), channel_id=1, replica_groups=mesh['cx'=4,'core'=2,'gy'=4,'gz'=8] {'cx','gy'}, dimensions={0} | all-to-all | bytes 147456 | tf_op jit(solution)/shard_map/all_to_all | solution.py:326
  52.2 0.1 reduce_sum.37.cent
  52.2 4.1 %shard_map.71 = (f32[32,8,8,128]{3,2,1,0:T(8,128)}, f32[9,128]{1,0:T(8,128)S(1)}) custom-call(bf16[64,32,128]{2,1,0:T(8,128)(2,1)S(1)} %get-tuple-element.9.own, bf16[18,32,128]{2,1,0:T(8,128)(2,1)S(1)} %collective-permute-done.2.ylo, bf16[18,32,128]{2,1,0:T(8,128)(2,1)S(1)} %collective-permute-done.3.yhi, ...), custom_call_target="tpu_custom_call" | custom-call | flops 800000000 | bytes 3145728 | tf_op jit(solution)/shard_map/pallas_call | solution.py:274
  56.3 3.0 %collective-permute-start.7 = (f32[9,1,128]{2,0,1:T(8,128)S(1)}, f32[9,1,128]{2,0,1:T(8,128)S(1)}, u32[]{:S(2)}, u32[]{:S(2)}) collective-permute-start(f32[9,1,128]{2,0,1:T(8,128)S(1)} %bitcast.28), channel_id=1, source_target_pairs={{0,32},{32,0},{1,33},{33,1},{2,34},{34,2},{3,35},{35,3},{4,36},{36... | collective-permute-start | bytes 13832 | tf_op jit(solution)/shard_map/ppermute | solution.py:332
  59.4 0.8 %collective-permute-done.7 = f32[9,1,128]{2,0,1:T(8,128)S(1)} collective-permute-done((f32[9,1,128]{2,0,1:T(8,128)S(1)}, f32[9,1,128]{2,0,1:T(8,128)S(1)}, u32[]{:S(2)}, u32[]{:S(2)}) %collective-permute-start.7) | collective-permute-done | bytes 4640 | tf_op jit(solution)/shard_map/ppermute | solution.py:332
  60.2 9.3 %all_to_all.22 = f32[8,9,1,128]{3,2,1,0:T(1,128)S(1)} all-to-all(f32[8,9,1,128]{3,2,1,0:T(1,128)S(1)} %broadcast_in_dim.16), channel_id=1, replica_groups=mesh['cx'=4,'core'=2,'gy'=4,'gz'=8] {'gz'}, dimensions={0} | all-to-all | bytes 73728 | tf_op jit(solution)/shard_map/all_to_all | solution.py:326
  69.6 9.5 %all_to_all.23 = f32[16,9,1,128]{3,2,1,0:T(1,128)S(1)} all-to-all(f32[16,9,1,128]{3,2,1,0:T(1,128)S(1)} %broadcast_in_dim.34), channel_id=1, replica_groups=mesh['cx'=4,'core'=2,'gy'=4,'gz'=8] {'cx','gy'}, dimensions={0} | all-to-all | bytes 147456 | tf_op jit(solution)/shard_map/all_to_all | solution.py:326
  79.1 0.1 reduce_sum.39
  79.2 0.1 reshape.65
  79.3 0.7 bitcast_divide_fusion
  (24 shorter events, 0.4 us)
Async XLA Ops:
  0.6 1.0 %copy-start = (bf16[32,8,8,128]{3,2,1,0:T(8,128)(2,1)S(1)}, bf16[32,8,8,128]{3,2,1,0:T(8,128)(2,1)}, u32[]{:S(2)}) copy-start(bf16[32,8,8,128]{3,2,1,0:T(8,128)(2,1)} %attr.1) | copy-start | bytes 1572868
  2.4 7.3 %collective-permute-start.1 = (bf16[2,32,128]{2,1,0:T(8,128)(2,1)S(1)}, bf16[2,32,128]{2,1,0:T(8,128)(2,1)S(1)}, u32[]{:S(2)}, u32[]{:S(2)}) collective-permute-start(bf16[2,32,128]{2,1,0:T(8,128)(2,1)S(1)} %get-tuple-element.10), channel_id=1, source_target_pairs={{1,0},{2,1},{3,2},{4,3},{5,4},{6,5},{7,6},{0,7},{9,8},{10,9},{11,1... | collective-permute-start | bytes 49160 | tf_op jit(solution)/shard_map/ppermute | solution.py:321
  8.9 3.8 %collective-permute-start = (bf16[2,32,128]{2,1,0:T(8,128)(2,1)S(1)}, bf16[2,32,128]{2,1,0:T(8,128)(2,1)S(1)}, u32[]{:S(2)}, u32[]{:S(2)}) collective-permute-start(bf16[2,32,128]{2,1,0:T(8,128)(2,1)S(1)} %get-tuple-element.10), channel_id=1, source_target_pairs={{0,1},{1,2},{2,3},{3,4},{4,5},{5,6},{6,7},{7,0},{8,9},{9,10},{10,1... | collective-permute-start | bytes 49160 | tf_op jit(solution)/shard_map/ppermute | solution.py:320
  12.8 11.0 %copy-start.3 = (bf16[768,256]{1,0:T(8,128)(2,1)S(1)}, bf16[768,256]{1,0:T(8,128)(2,1)}, u32[]{:S(2)}) copy-start(bf16[768,256]{1,0:T(8,128)(2,1)} %constant.52.clone.near) | copy-start | bytes 1179652
  12.8 5.3 %collective-permute-start.2 = (bf16[18,32,128]{2,1,0:T(8,128)(2,1)S(1)}, bf16[18,32,128]{2,1,0:T(8,128)(2,1)S(1)}, u32[]{:S(2)}, u32[]{:S(2)}) collective-permute-start(bf16[18,32,128]{2,1,0:T(8,128)(2,1)S(1)} %get-tuple-element.31), channel_id=1, source_target_pairs={{0,8},{8,16},{16,24},{24,0},{1,9},{9,17},{17,25},{25,1},{2,10},{10... | collective-permute-start | bytes 442376 | tf_op jit(solution)/shard_map/ppermute | solution.py:320
  14.2 4.1 %collective-permute-start.3 = (bf16[18,32,128]{2,1,0:T(8,128)(2,1)S(1)}, bf16[18,32,128]{2,1,0:T(8,128)(2,1)S(1)}, u32[]{:S(2)}, u32[]{:S(2)}) collective-permute-start(bf16[18,32,128]{2,1,0:T(8,128)(2,1)S(1)} %get-tuple-element.30), channel_id=1, source_target_pairs={{8,0},{16,8},{24,16},{0,24},{9,1},{17,9},{25,17},{1,25},{10,2},{18... | collective-permute-start | bytes 442376 | tf_op jit(solution)/shard_map/ppermute | solution.py:321
  18.3 8.6 %collective-permute-start.5 = (bf16[27,32,128]{2,1,0:T(8,128)(2,1)S(1)}, bf16[27,32,128]{2,1,0:T(8,128)(2,1)S(1)}, u32[]{:S(2)}, u32[]{:S(2)}) collective-permute-start(bf16[27,32,128]{2,1,0:T(8,128)(2,1)S(1)} %get-tuple-element.20), channel_id=1, source_target_pairs={{32,0},{64,32},{96,64},{128,96},{160,128},{192,160},{224,192},{0,2... | collective-permute-start | bytes 663560 | tf_op jit(solution)/shard_map/ppermute | solution.py:321
  21.8 5.0 %collective-permute-start.4 = (bf16[27,32,128]{2,1,0:T(8,128)(2,1)S(1)}, bf16[27,32,128]{2,1,0:T(8,128)(2,1)S(1)}, u32[]{:S(2)}, u32[]{:S(2)}) collective-permute-start(bf16[27,32,128]{2,1,0:T(8,128)(2,1)S(1)} %get-tuple-element.21), channel_id=1, source_target_pairs={{0,32},{32,64},{64,96},{96,128},{128,160},{160,192},{192,224},{224... | collective-permute-start | bytes 663560 | tf_op jit(solution)/shard_map/ppermute | solution.py:320
  23.0 0.7 copy-start.4
  23.7 0.8 copy-start.2
  24.4 2.5 %copy-start.1 = (bf16[768,256]{1,0:T(8,128)(2,1)S(1)}, bf16[768,256]{1,0:T(8,128)(2,1)}, u32[]{:S(2)}) copy-start(bf16[768,256]{1,0:T(8,128)(2,1)} %constant.53.clone.far) | copy-start | bytes 1179652
  28.7 2.4 %collective-permute-start.6 = (f32[9,1,128]{2,0,1:T(8,128)S(1)}, f32[9,1,128]{2,0,1:T(8,128)S(1)}, u32[]{:S(2)}, u32[]{:S(2)}) collective-permute-start(f32[9,1,128]{2,0,1:T(8,128)S(1)} %bitcast.27), channel_id=1, source_target_pairs={{0,32},{32,0},{1,33},{33,1},{2,34},{34,2},{3,35},{35,3},{4,36},{36... | collective-permute-start | bytes 13832 | tf_op jit(solution)/shard_map/ppermute | solution.py:332
  56.3 3.9 %collective-permute-start.7 = (f32[9,1,128]{2,0,1:T(8,128)S(1)}, f32[9,1,128]{2,0,1:T(8,128)S(1)}, u32[]{:S(2)}, u32[]{:S(2)}) collective-permute-start(f32[9,1,128]{2,0,1:T(8,128)S(1)} %bitcast.28), channel_id=1, source_target_pairs={{0,32},{32,0},{1,33},{33,1},{2,34},{34,2},{3,35},{35,3},{4,36},{36... | collective-permute-start | bytes 13832 | tf_op jit(solution)/shard_map/ppermute | solution.py:332

commit v5 on v4

--- a/solution.py
+++ b/solution.py
@@ -35,8 +35,8 @@
 
 
 def band_matrix():
-    z = np.arange(128)
-    return (np.abs(z[:, None] - z[None, :]) <= 2).astype(np.float32)
+    gap = lax.broadcasted_iota(jnp.int32, (128, 128), 0) - lax.broadcasted_iota(jnp.int32, (128, 128), 1)
+    return jnp.where(jnp.abs(gap) <= 2, 1.0, 0.0).astype(BF16)
 
 
 def recip(x):
@@ -64,7 +64,9 @@
     part[8:9, :] = jnp.concatenate([denom[0:1]] * 4, axis=1)
 
 
-def prepare_kernel(attr, own, ends, rows):
+def prepare_kernel(attr, start, own, ends, cent, rows):
+    cent[0:8, :] = jnp.concatenate([start[8 * g:8 * g + 8, :] for g in range(4)], axis=1)
+    cent[8:9, :] = jnp.ones((1, 128), F32)
     rows[...] = attr[...].astype(F32).reshape(F * COLS, 128)
     lane = lax.broadcasted_iota(jnp.int32, (1, 128), 1) // 4
     for half in range(2):
@@ -91,12 +93,12 @@
 
 
 class Step:
-    def __init__(self, cent, edge, band):
+    def __init__(self, cent, edge):
         c = unpacked_centroids(cent)
         self.cbm2 = (-2.0 * c.astype(BF16).astype(F32)).astype(BF16)
         self.csq1 = jnp.broadcast_to(jnp.sum(c * c, axis=1, keepdims=True) + 1.0, (F, 128))
         self.xlo, self.xhi, self.ylo, self.yhi, self.zlo, self.zhi = [edge[i] for i in range(6)]
-        self.band = band
+        self.band = band_matrix()
         self.lane = lax.broadcasted_iota(jnp.int32, (1, 128), 1)
         self.numer = jnp.zeros((F, F), F32)
         self.denom = jnp.zeros((8, F), F32)
@@ -127,7 +129,7 @@
                 if mx is None and my is None:
                     keep(Y + i - 2, inv)
                 rounded.append(self.normalised(inv, m))
-        z = jnp.dot(jnp.concatenate(rounded, axis=0), self.band[...], preferred_element_type=F32)
+        z = jnp.dot(jnp.concatenate(rounded, axis=0), self.band, preferred_element_type=F32)
         cols = [z[F * Y:F * Y + F] for Y in range(E)]
         p = [cols[Y] + cols[Y + 1] for Y in range(E - 1)]
         return [p[y] + p[y + 2] + cols[y + 4] for y in range(W)]
@@ -195,18 +197,18 @@
     return column
 
 
-def near_tiles(zown, ylo, yhi):
-    return [zown[0], zown[1], ylo[16], ylo[17], yhi[16], yhi[17]]
+def near_tiles(*arrays):
+    return [a[half] for a in arrays for half in range(2)]
 
 
 def far_tiles(xlo, xhi):
     return [r[24 + i] for r in (xlo, xhi) for i in range(3)]
 
 
-def inner_kernel(own, ylo, yhi, zown, cent, edge, band, near, box, kept, sums, inv_s, win_s):
-    step = Step(cent, edge, band)
+def inner_kernel(own, ylo, yhi, zown, zylo, zyhi, cent, edge, near, box, kept, sums, inv_s, win_s):
+    step = Step(cent, edge)
     column = mid_column(own, ylo, yhi)
-    windows = step.halo(z_tiles()[0], near_tiles(zown, ylo, yhi), near)
+    windows = step.halo(z_tiles()[0], near_tiles(zown, zylo, zyhi), near)
     for x in range(W):
         def keep(y, inv, x=x):
             if x in INNER:
@@ -229,8 +231,8 @@
     sums[F:F + 8, :] = step.denom
 
 
-def outer_kernel(own, xlo, xhi, cent, edge, band, far, box, kept, sums, part, win_s):
-    step = Step(cent, edge, band)
+def outer_kernel(own, xlo, xhi, cent, edge, far, box, kept, sums, part, win_s):
+    step = Step(cent, edge)
     column = outer_column(xlo, xhi)
     rows = (0, 1, W + 2, W + 3)
     windows = step.halo(z_tiles()[1], far_tiles(xlo, xhi), far)
@@ -247,10 +249,10 @@
     store_sums(part, step.numer + sums[0:F, :], step.denom + sums[F:F + 8, :])
 
 
-def whole_kernel(own, ylo, yhi, xlo, xhi, zown, cent, edge, band, near, far, memb, part, inv_s, win_s):
-    step = Step(cent, edge, band)
+def whole_kernel(own, ylo, yhi, xlo, xhi, zown, zylo, zyhi, cent, edge, near, far, memb, part, inv_s, win_s):
+    step = Step(cent, edge)
     mid, outer = mid_column(own, ylo, yhi), outer_column(xlo, xhi)
-    windows = step.halo(z_tiles()[0], near_tiles(zown, ylo, yhi), near)
+    windows = step.halo(z_tiles()[0], near_tiles(zown, zylo, zyhi), near)
     windows = windows + step.halo(z_tiles()[1], far_tiles(xlo, xhi), far)
     for X in range(E):
         def keep(y, inv, X=X):
@@ -286,34 +288,34 @@
     return (n, F, 128), dtype
 
 
-def prepare(attributes):
+def prepare(attributes, start):
     return call(
-        prepare_kernel, [columns(COLS, BF16), columns(2, BF16)], [VMEM],
-        [pltpu.VMEM((F * COLS, 128), F32)], 10 ** 6, 1 << 20, (attributes,))
-
-
-def inner_part(own, ylo, yhi, zown, cent, edge, band, near):
+        prepare_kernel, [columns(COLS, BF16), columns(2, BF16), ((9, 128), F32)], [VMEM] * 2,
+        [pltpu.VMEM((F * COLS, 128), F32)], 10 ** 6, 1 << 20, (attributes, start))
+
+
+def inner_part(own, ylo, yhi, zown, zylo, zyhi, cent, edge, near):
     return call(
         inner_kernel, [columns(4 * W), columns(4 * W), ((F + 8, F), F32)],
-        [VMEM] * 5 + [SMEM, VMEM, VMEM],
+        [VMEM] * 7 + [SMEM, VMEM],
         [pltpu.VMEM(*columns(4 * W)), pltpu.VMEM(*columns(COLS))],
-        5 * 10 ** 8, 3 << 20, (own, ylo, yhi, zown, cent, edge, band, near))
-
-
-def outer_part(own, xlo, xhi, cent, edge, band, far, box, kept, sums):
+        5 * 10 ** 8, 3 << 20, (own, ylo, yhi, zown, zylo, zyhi, cent, edge, near))
+
+
+def outer_part(own, xlo, xhi, cent, edge, far, box, kept, sums):
     return call(
         outer_kernel, [((9, 128), F32)],
-        [VMEM] * 4 + [SMEM] + [VMEM] * 5,
+        [VMEM] * 4 + [SMEM] + [VMEM] * 4,
         [pltpu.VMEM(*columns(4 * W))],
-        2 * 10 ** 8, 2 << 20, (own, xlo, xhi, cent, edge, band, far, box, kept, sums))[0]
-
-
-def whole_update(own, ylo, yhi, xlo, xhi, zown, cent, edge, band, near, far):
+        2 * 10 ** 8, 2 << 20, (own, xlo, xhi, cent, edge, far, box, kept, sums))[0]
+
+
+def whole_update(own, ylo, yhi, xlo, xhi, zown, zylo, zyhi, cent, edge, near, far):
     return call(
         whole_kernel, [((F, W, W, 128), F32), ((9, 128), F32)],
-        [VMEM] * 7 + [SMEM] + [VMEM] * 3,
+        [VMEM] * 9 + [SMEM] + [VMEM] * 2,
         [pltpu.VMEM(*columns(COLS)), pltpu.VMEM(*columns(E * W))],
-        8 * 10 ** 8, 3 << 20, (own, ylo, yhi, xlo, xhi, zown, cent, edge, band, near, far))
+        8 * 10 ** 8, 3 << 20, (own, ylo, yhi, xlo, xhi, zown, zylo, zyhi, cent, edge, near, far))
 
 
 def both_ways(up, down, axes, count):
@@ -328,9 +330,7 @@
 
 
 def total_sums(part):
-    part = part.reshape(9, 1, 128)
-    part = part + lax.ppermute(part, "core", [(0, 1), (1, 0)])
-    part = gather_sum(part, ("gz",), 8)
+    part = gather_sum(part.reshape(9, 1, 128), ("core", "gz"), 16)
     return gather_sum(part, ("cx", "gy"), 16).reshape(9, 128)
 
 
@@ -341,34 +341,28 @@
 
 def per_device(attributes, start_centroids):
     edge = edges()
-    band = jnp.asarray(band_matrix(), BF16)
     near, far = [jnp.asarray(halo_matrix(t), BF16) for t in z_tiles()]
-    packed = start_centroids.reshape(4, 8, F).transpose(1, 0, 2).reshape(8, 128)
-    cent = jnp.concatenate([packed, jnp.ones((1, 128), F32)])
-
-    own, ends = prepare(attributes)
+    own, ends, cent = prepare(attributes, start_centroids)
     zlo, zhi = both_ways(ends, ends, "gz", 8)
     lane = lax.broadcasted_iota(jnp.int32, ends.shape, 2)
     zown = jnp.where(lane % 4 < 2, zlo, zhi)
 
     grid = own.reshape(W, W, F, 128)
-
-    def y_slice(y):
-        return jnp.concatenate([grid[:, y:y + 2].reshape(2 * W, F, 128), zown])
-
-    ylo, yhi = both_ways(y_slice(W - 2), y_slice(0), "gy", 4)
+    ylo, yhi = both_ways(
+        grid[:, W - 2:].reshape(2 * W, F, 128), grid[:, :2].reshape(2 * W, F, 128), "gy", 4)
+    zylo, zyhi = both_ways(zown, zown, "gy", 4)
 
     def x_slice(x, half):
         return jnp.concatenate(
             [own[x * W:x * W + 2 * W], ylo[2 * x:2 * x + 4], yhi[2 * x:2 * x + 4],
-             zown[half:half + 1], ylo[16 + half:17 + half], yhi[16 + half:17 + half]])
+             zown[half:half + 1], zylo[half:half + 1], zyhi[half:half + 1]])
 
     xlo, xhi = both_ways(x_slice(W - 2, 1), x_slice(0, 0), XS, 8)
 
-    box, kept, sums = inner_part(own, ylo, yhi, zown, cent, edge, band, near)
-    part = outer_part(own, xlo, xhi, cent, edge, band, far, box, kept, sums)
+    box, kept, sums = inner_part(own, ylo, yhi, zown, zylo, zyhi, cent, edge, near)
+    part = outer_part(own, xlo, xhi, cent, edge, far, box, kept, sums)
     cent = total_sums(part)
-    memb, part = whole_update(own, ylo, yhi, xlo, xhi, zown, cent, edge, band, near, far)
+    memb, part = whole_update(own, ylo, yhi, xlo, xhi, zown, zylo, zyhi, cent, edge, near, far)
     cent = total_sums(part)
     numer = cent[:8].reshape(8, 4, F).transpose(1, 0, 2).reshape(F, F)
     return numer / cent[8, :F][:, None], memb

time: 80.8 us -> 78.3 us (0.969)
  blocking collectives: 39.7 us -> 42.1 us
  waiting for transfers between devices: 7.96 us -> 5.92 us
  starting transfers between devices: 18.7 us -> 16.9 us
    ppermute x2 -> x0, starting transfers between devices: 4.62 us -> none  [total_sums(): part = part + lax.ppermute(part, 'core', [(0, 1), (1, 0)])]
    ppermute x3 -> x4, starting transfers between devices: 11.6 us -> 14.4 us  [both_ways(): hi = lax.ppermute(down, axes, [((i + 1) % count, i) for i in range(count)])]
    all_to_all x4, blocking collectives: 39.7 us -> 42.1 us  [gather_sum(): lax.all_to_all(jnp.broadcast_to(part[None], (count,) + part.shape), axes,...]
    ppermute x2 -> x0, waiting for transfers between devices: 1.66 us -> none  [total_sums(): part = part + lax.ppermute(part, 'core', [(0, 1), (1, 0)])]
    ppermute x3 -> x4, waiting for transfers between devices: 5.35 us -> 4.56 us  [both_ways(): lo = lax.ppermute(up, axes, [(i, (i + 1) % count) for i in range(count)])]
    unnamed x15 -> x13, local copies, waits for them, and re-layouts: 2.37 us -> 1.82 us
    ppermute x3 -> x4, starting transfers between devices: 2.5 us -> 2.5 us  [both_ways(): lo = lax.ppermute(up, axes, [(i, (i + 1) % count) for i in range(count)])]
  transfers between devices with their start and end apart: 8 -> 8, of which waited for: 6 -> 3; matrix products, arithmetic and copies ran while one was open for 0% -> 0% of each run, Pallas kernels for 3% -> 3%
where the time goes in v5:
time: 78.3 us; the launch traced here: 78 us
  blocking collectives  42.1 us (54%)
  starting transfers between devices  16.9 us (22%)
  Pallas kernels  9.17 us (12%)
  waiting for transfers between devices  5.92 us (8%)
  local copies, waits for them, and re-layouts  2.2 us (3%)
  other arithmetic  0.94 us (1%)
    all_to_all x4, blocking collectives, gather_sum(): lax.all_to_all(jnp.broadcast_to(part[None], (count,) + part.shape), axes,...  42.1 us
    ppermute x4, starting transfers between devices, both_ways(): hi = lax.ppermute(down, axes, [((i + 1) % count, i) for i in range(count)])  14.4 us
    pallas_call x4, Pallas kernels, call(): pl.pallas_call(kernel, out_shape=tuple((jax.ShapeDtypeStruct(s, t) for s,...  9.17 us
    ppermute x4, waiting for transfers between devices, both_ways(): lo = lax.ppermute(up, axes, [(i, (i + 1) % count) for i in range(count)])  4.56 us
    ppermute x4, starting transfers between devices, both_ways(): lo = lax.ppermute(up, axes, [(i, (i + 1) % count) for i in range(count)])  2.5 us
    unnamed x13, local copies, waits for them, and re-layouts  1.82 us
  transfers between devices with their start and end apart: 8, of which 3 were waited for; matrix products, arithmetic and copies ran while one was open for 0% of the time, Pallas kernels for 3%

profile of v5, /device:TPU:1, one launch (start us, length us, event | category | flops | bytes accessed | tf_op | source)
XLA Modules:
  0.0 78.0 jit_solution(16453945410667265481)
XLA Ops:
  0.6 0.0 copy-start
  0.6 1.0 %copy-done = bf16[32,8,8,128]{3,2,1,0:T(8,128)(2,1)S(1)} copy-done((bf16[32,8,8,128]{3,2,1,0:T(8,128)(2,1)S(1)}, bf16[32,8,8,128]{3,2,1,0:T(8,128)(2,1)}, u32[]{:S(2)}) %copy-start) | copy-done | bytes 524312
  1.7 0.0 copy-start.2
  1.7 0.7 copy-done.2
  2.4 0.8 %shard_map.59 = (bf16[64,32,128]{2,1,0:T(8,128)(2,1)S(1)}, bf16[2,32,128]{2,1,0:T(8,128)(2,1)S(1)}, f32[9,128]{1,0:T(8,128)S(1)}) custom-call(bf16[32,8,8,128]{3,2,1,0:T(8,128)(2,1)S(1)} %copy-done, f32[32,32]{1,0:T(8,128)S(1)} %copy-done.2), custom_call_target="tpu_custom_call" | custom-call | flops 1000000 | bytes 1048576 | tf_op jit(solution)/shard_map/pallas_call | solution.py:276
  3.2 6.5 %collective-permute-start.3 = (bf16[2,32,128]{2,1,0:T(8,128)(2,1)S(1)}, bf16[2,32,128]{2,1,0:T(8,128)(2,1)S(1)}, u32[]{:S(2)}, u32[]{:S(2)}) collective-permute-start(bf16[2,32,128]{2,1,0:T(8,128)(2,1)S(1)} %get-tuple-element.11), channel_id=1, source_target_pairs={{1,0},{2,1},{3,2},{4,3},{5,4},{6,5},{7,6},{0,7},{9,8},{10,9},{11,1... | collective-permute-start | bytes 49160 | tf_op jit(solution)/shard_map/ppermute | solution.py:323
  9.6 0.0 collective-permute-start.2
  9.7 1.4 %collective-permute-start = (bf16[16,32,128]{2,1,0:T(8,128)(2,1)S(1)}, bf16[16,32,128]{2,1,0:T(8,128)(2,1)S(1)}, u32[]{:S(2)}, u32[]{:S(2)}) collective-permute-start(bf16[16,32,128]{2,1,0:T(8,128)(2,1)S(1)} %bitcast.16), channel_id=1, source_target_pairs={{0,8},{8,16},{16,24},{24,0},{1,9},{9,17},{17,25},{25,1},{2,10},{10... | collective-permute-start | bytes 393224 | tf_op jit(solution)/shard_map/ppermute | solution.py:322
  11.0 1.5 %collective-permute-start.1 = (bf16[16,32,128]{2,1,0:T(8,128)(2,1)S(1)}, bf16[16,32,128]{2,1,0:T(8,128)(2,1)S(1)}, u32[]{:S(2)}, u32[]{:S(2)}) collective-permute-start(bf16[16,32,128]{2,1,0:T(8,128)(2,1)S(1)} %bitcast.15), channel_id=1, source_target_pairs={{8,0},{16,8},{24,16},{0,24},{9,1},{17,9},{25,17},{1,25},{10,2},{18... | collective-permute-start | bytes 393224 | tf_op jit(solution)/shard_map/ppermute | solution.py:323
  12.6 0.0 copy-start.3
  12.6 0.0 collective-permute-done.3
  12.6 0.8 %collective-permute-done.2 = bf16[2,32,128]{2,1,0:T(8,128)(2,1)S(1)} collective-permute-done((bf16[2,32,128]{2,1,0:T(8,128)(2,1)S(1)}, bf16[2,32,128]{2,1,0:T(8,128)(2,1)S(1)}, u32[]{:S(2)}, u32[]{:S(2)}) %collective-permute-start.2) | collective-permute-done | bytes 16416 | tf_op jit(solution)/shard_map/ppermute | solution.py:322
  13.5 2.8 %collective-permute-start.5 = (bf16[2,32,128]{2,1,0:T(8,128)(2,1)S(1)}, bf16[2,32,128]{2,1,0:T(8,128)(2,1)S(1)}, u32[]{:S(2)}, u32[]{:S(2)}) collective-permute-start(bf16[2,32,128]{2,1,0:T(8,128)(2,1)S(1)} %fusion.zown), channel_id=1, source_target_pairs={{8,0},{16,8},{24,16},{0,24},{9,1},{17,9},{25,17},{1,25},{10,2},{18... | collective-permute-start | bytes 49160 | tf_op jit(solution)/shard_map/ppermute | solution.py:323
  16.3 0.0 collective-permute-start.4
  16.3 0.0 collective-permute-done.ylo
  16.3 0.0 collective-permute-done.1.yhi
  16.3 3.7 %collective-permute-done.4.zylo = bf16[2,32,128]{2,1,0:T(8,128)(2,1)S(1)} collective-permute-done((bf16[2,32,128]{2,1,0:T(8,128)(2,1)S(1)}, bf16[2,32,128]{2,1,0:T(8,128)(2,1)S(1)}, u32[]{:S(2)}, u32[]{:S(2)}) %collective-permute-start.4) | collective-permute-done | bytes 16416 | tf_op jit(solution)/shard_map/ppermute | solution.py:322
  20.1 0.0 collective-permute-done.5.zyhi
  20.1 3.5 %collective-permute-start.7 = (bf16[27,32,128]{2,1,0:T(8,128)(2,1)S(1)}, bf16[27,32,128]{2,1,0:T(8,128)(2,1)S(1)}, u32[]{:S(2)}, u32[]{:S(2)}) collective-permute-start(bf16[27,32,128]{2,1,0:T(8,128)(2,1)S(1)} %get-tuple-element.26), channel_id=1, source_target_pairs={{32,0},{64,32},{96,64},{128,96},{160,128},{192,160},{224,192},{0,2... | collective-permute-start | bytes 663560 | tf_op jit(solution)/shard_map/ppermute | solution.py:323
  23.6 1.1 %collective-permute-start.6 = (bf16[27,32,128]{2,1,0:T(8,128)(2,1)S(1)}, bf16[27,32,128]{2,1,0:T(8,128)(2,1)S(1)}, u32[]{:S(2)}, u32[]{:S(2)}) collective-permute-start(bf16[27,32,128]{2,1,0:T(8,128)(2,1)S(1)} %get-tuple-element.27), channel_id=1, source_target_pairs={{0,32},{32,64},{64,96},{96,128},{128,160},{160,192},{192,224},{224... | collective-permute-start | bytes 663560 | tf_op jit(solution)/shard_map/ppermute | solution.py:322
  24.8 0.1 stack.27
  24.9 0.0 copy-done.3
  24.9 0.0 copy-start.1
  24.9 2.4 %shard_map.60 = (f32[32,32,128]{2,1,0:T(8,128)S(1)}, f32[32,32,128]{2,1,0:T(8,128)S(1)}, f32[40,32]{1,0:T(8,128)S(1)}) custom-call(bf16[64,32,128]{2,1,0:T(8,128)(2,1)S(1)} %get-tuple-element.10.own, bf16[16,32,128]{2,1,0:T(8,128)(2,1)S(1)} %collective-permute-done.ylo, bf16[16,32,128]{2,1,0:T(8,128)(2,1)S(1)} %collective-permute-done.1.yhi, ...), custom_call_target="tpu_custom_call" | custom-call | flops 500000000 | bytes 3145728 | tf_op jit(solution)/shard_map/pallas_call | solution.py:276
  27.3 1.3 %collective-permute-done.7.xhi = bf16[27,32,128]{2,1,0:T(8,128)(2,1)S(1)} collective-permute-done((bf16[27,32,128]{2,1,0:T(8,128)(2,1)S(1)}, bf16[27,32,128]{2,1,0:T(8,128)(2,1)S(1)}, u32[]{:S(2)}, u32[]{:S(2)}) %collective-permute-start.7) | collective-permute-done | bytes 221216 | tf_op jit(solution)/shard_map/ppermute | solution.py:323
  28.6 0.0 collective-permute-done.6.xlo
  28.6 0.0 copy-done.1
  28.7 1.8 %shard_map.61 = f32[9,128]{1,0:T(8,128)S(1)} custom-call(bf16[64,32,128]{2,1,0:T(8,128)(2,1)S(1)} %get-tuple-element.10.own, bf16[27,32,128]{2,1,0:T(8,128)(2,1)S(1)} %collective-permute-done.6.xlo, bf16[27,32,128]{2,1,0:T(8,128)(2,1)S(1)} %collective-permute-done.7.xhi, f32[9,128]{1,0:T(8,128)S(1)} %get-tuple-element.12.cent, ...), custom_call_target="tpu_custom_call" | custom-call | flops 200000000 | bytes 2097152 | tf_op jit(solution)/shard_map/pallas_call | solution.py:276
  30.5 11.4 %all_to_all.20 = f32[16,9,1,128]{3,2,1,0:T(1,128)S(1)} all-to-all(f32[16,9,1,128]{3,2,1,0:T(1,128)S(1)} %broadcast_in_dim.8), channel_id=1, replica_groups=mesh['cx'=4,'core'=2,'gy'=4,'gz'=8] {'core','gz'}, dimensions={0} | all-to-all | bytes 147456 | tf_op jit(solution)/shard_map/all_to_all | solution.py:328
  41.9 0.1 reduce_sum.36
  42.0 9.2 %all_to_all.21 = f32[16,9,1,128]{3,2,1,0:T(1,128)S(1)} all-to-all(f32[16,9,1,128]{3,2,1,0:T(1,128)S(1)} %broadcast_in_dim.9), channel_id=1, replica_groups=mesh['cx'=4,'core'=2,'gy'=4,'gz'=8] {'cx','gy'}, dimensions={0} | all-to-all | bytes 147456 | tf_op jit(solution)/shard_map/all_to_all | solution.py:328
  51.2 0.1 reduce_sum.37.cent
  51.3 4.1 %shard_map.62 = (f32[32,8,8,128]{3,2,1,0:T(8,128)}, f32[9,128]{1,0:T(8,128)S(1)}) custom-call(bf16[64,32,128]{2,1,0:T(8,128)(2,1)S(1)} %get-tuple-element.10.own, bf16[16,32,128]{2,1,0:T(8,128)(2,1)S(1)} %collective-permute-done.ylo, bf16[16,32,128]{2,1,0:T(8,128)(2,1)S(1)} %collective-permute-done.1.yhi, ...), custom_call_target="tpu_custom_call" | custom-call | flops 800000000 | bytes 3145728 | tf_op jit(solution)/shard_map/pallas_call | solution.py:276
  55.5 12.0 %all_to_all.22 = f32[16,9,1,128]{3,2,1,0:T(1,128)S(1)} all-to-all(f32[16,9,1,128]{3,2,1,0:T(1,128)S(1)} %broadcast_in_dim.10), channel_id=1, replica_groups=mesh['cx'=4,'core'=2,'gy'=4,'gz'=8] {'core','gz'}, dimensions={0} | all-to-all | bytes 147456 | tf_op jit(solution)/shard_map/all_to_all | solution.py:328
  67.5 0.1 reduce_sum.38
  67.6 9.5 %all_to_all.23 = f32[16,9,1,128]{3,2,1,0:T(1,128)S(1)} all-to-all(f32[16,9,1,128]{3,2,1,0:T(1,128)S(1)} %broadcast_in_dim.11), channel_id=1, replica_groups=mesh['cx'=4,'core'=2,'gy'=4,'gz'=8] {'cx','gy'}, dimensions={0} | all-to-all | bytes 147456 | tf_op jit(solution)/shard_map/all_to_all | solution.py:328
  77.1 0.1 reduce_sum.39
  77.2 0.1 reshape.49
  77.3 0.7 bitcast_divide_fusion
  (17 shorter events, 0.3 us)
Async XLA Ops:
  0.6 1.0 %copy-start = (bf16[32,8,8,128]{3,2,1,0:T(8,128)(2,1)S(1)}, bf16[32,8,8,128]{3,2,1,0:T(8,128)(2,1)}, u32[]{:S(2)}) copy-start(bf16[32,8,8,128]{3,2,1,0:T(8,128)(2,1)} %attr.1) | copy-start | bytes 1572868
  1.7 0.7 copy-start.2
  3.2 9.4 %collective-permute-start.3 = (bf16[2,32,128]{2,1,0:T(8,128)(2,1)S(1)}, bf16[2,32,128]{2,1,0:T(8,128)(2,1)S(1)}, u32[]{:S(2)}, u32[]{:S(2)}) collective-permute-start(bf16[2,32,128]{2,1,0:T(8,128)(2,1)S(1)} %get-tuple-element.11), channel_id=1, source_target_pairs={{1,0},{2,1},{3,2},{4,3},{5,4},{6,5},{7,6},{0,7},{9,8},{10,9},{11,1... | collective-permute-start | bytes 49160 | tf_op jit(solution)/shard_map/ppermute | solution.py:323
  9.6 3.8 %collective-permute-start.2 = (bf16[2,32,128]{2,1,0:T(8,128)(2,1)S(1)}, bf16[2,32,128]{2,1,0:T(8,128)(2,1)S(1)}, u32[]{:S(2)}, u32[]{:S(2)}) collective-permute-start(bf16[2,32,128]{2,1,0:T(8,128)(2,1)S(1)} %get-tuple-element.11), channel_id=1, source_target_pairs={{0,1},{1,2},{2,3},{3,4},{4,5},{5,6},{6,7},{7,0},{8,9},{9,10},{10,1... | collective-permute-start | bytes 49160 | tf_op jit(solution)/shard_map/ppermute | solution.py:322
  9.7 6.6 %collective-permute-start = (bf16[16,32,128]{2,1,0:T(8,128)(2,1)S(1)}, bf16[16,32,128]{2,1,0:T(8,128)(2,1)S(1)}, u32[]{:S(2)}, u32[]{:S(2)}) collective-permute-start(bf16[16,32,128]{2,1,0:T(8,128)(2,1)S(1)} %bitcast.16), channel_id=1, source_target_pairs={{0,8},{8,16},{16,24},{24,0},{1,9},{9,17},{17,25},{25,1},{2,10},{10... | collective-permute-start | bytes 393224 | tf_op jit(solution)/shard_map/ppermute | solution.py:322
  11.0 5.2 %collective-permute-start.1 = (bf16[16,32,128]{2,1,0:T(8,128)(2,1)S(1)}, bf16[16,32,128]{2,1,0:T(8,128)(2,1)S(1)}, u32[]{:S(2)}, u32[]{:S(2)}) collective-permute-start(bf16[16,32,128]{2,1,0:T(8,128)(2,1)S(1)} %bitcast.15), channel_id=1, source_target_pairs={{8,0},{16,8},{24,16},{0,24},{9,1},{17,9},{25,17},{1,25},{10,2},{18... | collective-permute-start | bytes 393224 | tf_op jit(solution)/shard_map/ppermute | solution.py:323
  12.6 12.3 %copy-start.3 = (bf16[768,256]{1,0:T(8,128)(2,1)S(1)}, bf16[768,256]{1,0:T(8,128)(2,1)}, u32[]{:S(2)}) copy-start(bf16[768,256]{1,0:T(8,128)(2,1)} %constant.47.clone.near) | copy-start | bytes 1179652
  13.5 6.6 %collective-permute-start.5 = (bf16[2,32,128]{2,1,0:T(8,128)(2,1)S(1)}, bf16[2,32,128]{2,1,0:T(8,128)(2,1)S(1)}, u32[]{:S(2)}, u32[]{:S(2)}) collective-permute-start(bf16[2,32,128]{2,1,0:T(8,128)(2,1)S(1)} %fusion.zown), channel_id=1, source_target_pairs={{8,0},{16,8},{24,16},{0,24},{9,1},{17,9},{25,17},{1,25},{10,2},{18... | collective-permute-start | bytes 49160 | tf_op jit(solution)/shard_map/ppermute | solution.py:323
  16.3 3.8 %collective-permute-start.4 = (bf16[2,32,128]{2,1,0:T(8,128)(2,1)S(1)}, bf16[2,32,128]{2,1,0:T(8,128)(2,1)S(1)}, u32[]{:S(2)}, u32[]{:S(2)}) collective-permute-start(bf16[2,32,128]{2,1,0:T(8,128)(2,1)S(1)} %fusion.zown), channel_id=1, source_target_pairs={{0,8},{8,16},{16,24},{24,0},{1,9},{9,17},{17,25},{25,1},{2,10},{10... | collective-permute-start | bytes 49160 | tf_op jit(solution)/shard_map/ppermute | solution.py:322
  20.1 8.6 %collective-permute-start.7 = (bf16[27,32,128]{2,1,0:T(8,128)(2,1)S(1)}, bf16[27,32,128]{2,1,0:T(8,128)(2,1)S(1)}, u32[]{:S(2)}, u32[]{:S(2)}) collective-permute-start(bf16[27,32,128]{2,1,0:T(8,128)(2,1)S(1)} %get-tuple-element.26), channel_id=1, source_target_pairs={{32,0},{64,32},{96,64},{128,96},{160,128},{192,160},{224,192},{0,2... | collective-permute-start | bytes 663560 | tf_op jit(solution)/shard_map/ppermute | solution.py:323
  23.6 5.0 %collective-permute-start.6 = (bf16[27,32,128]{2,1,0:T(8,128)(2,1)S(1)}, bf16[27,32,128]{2,1,0:T(8,128)(2,1)S(1)}, u32[]{:S(2)}, u32[]{:S(2)}) collective-permute-start(bf16[27,32,128]{2,1,0:T(8,128)(2,1)S(1)} %get-tuple-element.27), channel_id=1, source_target_pairs={{0,32},{32,64},{64,96},{96,128},{128,160},{160,192},{192,224},{224... | collective-permute-start | bytes 663560 | tf_op jit(solution)/shard_map/ppermute | solution.py:322
  24.9 3.8 %copy-start.1 = (bf16[768,256]{1,0:T(8,128)(2,1)S(1)}, bf16[768,256]{1,0:T(8,128)(2,1)}, u32[]{:S(2)}) copy-start(bf16[768,256]{1,0:T(8,128)(2,1)} %constant.48.clone.far) | copy-start | bytes 1179652

commit v6 on v5

--- a/solution.py
+++ b/solution.py
@@ -15,21 +15,22 @@
 XS = ("cx", "core")
 OUTER = (0, 1, W - 2, W - 1)
 INNER = tuple(range(2, W - 2))
-
-
-def z_tiles():
-    near = [(0, dy, half) for dy in (0, -1, 1) for half in (0, 1)]
-    far = [(dx, dy, half) for dx, half in ((-1, 1), (1, 0)) for dy in (0, -1, 1)]
-    return near, far
-
-
-def halo_matrix(tiles):
-    src = []
-    for dx, dy, half in tiles:
-        for c in range(half * 32, half * 32 + 32):
-            for t in range(4):
-                src.append((dx * W + c // W, dy * W + c % W, (-2, -1, 128, 129)[t]))
-    dst = [(c // W, c % W, (126, 127, 0, 1)[t]) for c in range(COLS) for t in range(4)]
+ROWS = (0, 1, W + 2, W + 3)
+
+
+def tile_columns():
+    def beyond(i):
+        return i - W if i >= W // 2 else i + W
+
+    own = [(c // W, c % W) for c in range(COLS)]
+    ys = [(x, beyond(y)) for x, y in own]
+    xs = [(beyond(j // W + (4 if j >= 16 else 0)), j % W) for j in range(32)]
+    return own + ys + xs + [(x, beyond(y)) for x, y in xs]
+
+
+def halo_matrix():
+    src = [(x, y, z) for x, y in tile_columns() for z in (-2, -1, 128, 129)]
+    dst = [(c // W, c % W, z) for c in range(COLS) for z in (126, 127, 0, 1)]
     gap = np.abs(np.array(src)[:, None, :] - np.array(dst)[None, :, :])
     return (gap <= 2).all(-1).astype(np.float32)
 
@@ -62,21 +63,6 @@
 def store_sums(part, numer, denom):
     part[0:8, :] = jnp.concatenate([numer[8 * g:8 * g + 8] for g in range(4)], axis=1)
     part[8:9, :] = jnp.concatenate([denom[0:1]] * 4, axis=1)
-
-
-def prepare_kernel(attr, start, own, ends, cent, rows):
-    cent[0:8, :] = jnp.concatenate([start[8 * g:8 * g + 8, :] for g in range(4)], axis=1)
-    cent[8:9, :] = jnp.ones((1, 128), F32)
-    rows[...] = attr[...].astype(F32).reshape(F * COLS, 128)
-    lane = lax.broadcasted_iota(jnp.int32, (1, 128), 1) // 4
-    for half in range(2):
-        acc = jnp.zeros((F, 128), F32)
-        for j in range(32):
-            c = half * 32 + j
-            col = rows[pl.ds(c, F, stride=COLS), :]
-            own[c] = col.astype(BF16)
-            acc = jnp.where(lane == j, pltpu.roll(col, (4 * j + 2) % 128, 1), acc)
-        ends[half] = acc.astype(BF16)
 
 
 def turned8(v):
@@ -90,6 +76,33 @@
                 v[i] = jnp.where(low, a, pltpu.roll(b, s, 0))
                 v[i + s] = jnp.where(low, pltpu.roll(a, 8 - s, 0), b)
     return v
+
+
+def prepare_kernel(attr_hbm, start_hbm, own, ends, cent, attr, start, sems):
+    fetch = [
+        pltpu.make_async_copy(attr_hbm.at[:, x:x + 4], attr.at[:, x:x + 4], sems.at[x // 4])
+        for x in range(0, W, 4)
+    ]
+    fetch.append(pltpu.make_async_copy(start_hbm, start, sems.at[2]))
+    for f in fetch:
+        f.start()
+    lane = lax.broadcasted_iota(jnp.int32, (1, 128), 1) // 4
+    for half in range(2):
+        acc = jnp.zeros((F, 128), F32)
+        fetch[half].wait()
+        for x in range(half * 4, half * 4 + 4):
+            wide = [attr[a, x].astype(F32) for a in range(F)]
+            groups = [turned8(wide[8 * g:8 * g + 8]) for g in range(4)]
+            for y in range(W):
+                c = x * W + y
+                j = c % 32
+                col = jnp.concatenate([groups[g][y] for g in range(4)], axis=0)
+                own[c] = col.astype(BF16)
+                acc = jnp.where(lane == j, pltpu.roll(col, (4 * j + 2) % 128, 1), acc)
+        ends[half] = acc.astype(BF16)
+    fetch[-1].wait()
+    cent[0:8, :] = jnp.concatenate([start[8 * g:8 * g + 8, :] for g in range(4)], axis=1)
+    cent[8:9, :] = jnp.ones((1, 128), F32)
 
 
 class Step:
@@ -134,17 +147,26 @@
         p = [cols[Y] + cols[Y + 1] for Y in range(E - 1)]
         return [p[y] + p[y + 2] + cols[y + 4] for y in range(W)]
 
-    def halo(self, tiles, arrays, matrix):
+    def halo(self, tiles, matrix, near):
+        j = self.lane // 4
         mz = jnp.where(self.lane % 4 < 2, self.zlo, self.zhi)
+        my = mz * jnp.where(j % W >= W // 2, self.ylo, self.yhi)
+        mx = jnp.where(j >= 16, self.xlo, self.xhi)
+        masks = [mz, mz, my, my] if near else [mz * mx, my * mx]
         rounded = []
-        for (dx, dy, _), a in zip(tiles, arrays):
-            m = mz
-            if dx:
-                m = m * (self.xlo if dx < 0 else self.xhi)
-            if dy:
-                m = m * (self.ylo if dy < 0 else self.yhi)
-            rounded.append(self.normalised(self.inverse(a)[0], m))
-        return jnp.dot(jnp.concatenate(rounded, axis=1), matrix[...], preferred_element_type=F32)
+        for i in range(0, len(tiles), 2):
+            pair = jnp.concatenate([tiles[i], tiles[i + 1]], axis=1)
+            for inv, m in zip(self.inverse(pair), masks[i:i + 2]):
+                rounded.append(self.normalised(inv, m))
+        return jnp.dot(jnp.concatenate(rounded, axis=1), matrix, preferred_element_type=F32)
+
+    def near_halo(self, zown, zy, matrix):
+        return self.halo([zown[0], zown[1], zy[0], zy[1]], matrix[0:4 * 128, :], True)
+
+    def far_halo(self, xlo, xhi, matrix):
+        tiles = [jnp.where(self.lane >= 64, xlo[2 * E + i].astype(F32), xhi[2 * E + i].astype(F32)).astype(BF16)
+                 for i in range(2)]
+        return self.halo(tiles, matrix[4 * 128:6 * 128, :], False)
 
     def halo_of(self, windows, c):
         half = windows[:, c // 32 * 128:c // 32 * 128 + 128]
@@ -197,18 +219,10 @@
     return column
 
 
-def near_tiles(*arrays):
-    return [a[half] for a in arrays for half in range(2)]
-
-
-def far_tiles(xlo, xhi):
-    return [r[24 + i] for r in (xlo, xhi) for i in range(3)]
-
-
-def inner_kernel(own, ylo, yhi, zown, zylo, zyhi, cent, edge, near, box, kept, sums, inv_s, win_s):
+def inner_kernel(own, ylo, yhi, zown, zy, matrix, cent, edge, box, kept, sums, inv_s, win_s):
     step = Step(cent, edge)
     column = mid_column(own, ylo, yhi)
-    windows = step.halo(z_tiles()[0], near_tiles(zown, zylo, zyhi), near)
+    windows = step.near_halo(zown, zy, matrix)
     for x in range(W):
         def keep(y, inv, x=x):
             if x in INNER:
@@ -231,29 +245,28 @@
     sums[F:F + 8, :] = step.denom
 
 
-def outer_kernel(own, xlo, xhi, cent, edge, far, box, kept, sums, part, win_s):
+def outer_kernel(own, xlo, xhi, matrix, cent, edge, box, kept, sums, part, win_s):
     step = Step(cent, edge)
     column = outer_column(xlo, xhi)
-    rows = (0, 1, W + 2, W + 3)
-    windows = step.halo(z_tiles()[1], far_tiles(xlo, xhi), far)
-    for i, X in enumerate(rows):
+    windows = step.far_halo(xlo, xhi, matrix)
+    for i, X in enumerate(ROWS):
         for y, w in enumerate(step.front(X, column, None)):
             win_s[i * W + y] = w
     for i, x in enumerate(OUTER):
-        near = [n for n, X in enumerate(rows) if x <= X <= x + 4]
+        near = [n for n, X in enumerate(ROWS) if x <= X <= x + 4]
         boxes = [
-            total([box[i * W + y]] + [win_s[n * W + y] for n in near]) + step.halo_of(windows, x * W + y)
+            total([box[i * W + y]] + [win_s[n * W + y] for n in near])
+            + step.halo_of(windows, x * W + y)
             for y in range(W)
         ]
         step.back(x, boxes, lambda y: kept[i * W + y], own)
     store_sums(part, step.numer + sums[0:F, :], step.denom + sums[F:F + 8, :])
 
 
-def whole_kernel(own, ylo, yhi, xlo, xhi, zown, zylo, zyhi, cent, edge, near, far, memb, part, inv_s, win_s):
+def whole_kernel(own, ylo, yhi, xlo, xhi, zown, zy, matrix, cent, edge, memb, part, inv_s, win_s):
     step = Step(cent, edge)
     mid, outer = mid_column(own, ylo, yhi), outer_column(xlo, xhi)
-    windows = step.halo(z_tiles()[0], near_tiles(zown, zylo, zyhi), near)
-    windows = windows + step.halo(z_tiles()[1], far_tiles(xlo, xhi), far)
+    windows = step.near_halo(zown, zy, matrix) + step.far_halo(xlo, xhi, matrix)
     for X in range(E):
         def keep(y, inv, X=X):
             inv_s[(X - 2) * W + y] = inv
@@ -269,6 +282,7 @@
 
 
 VMEM = pl.BlockSpec(memory_space=pltpu.VMEM)
+ANY = pl.BlockSpec(memory_space=pl.ANY)
 SMEM = pl.BlockSpec(memory_space=pltpu.SMEM)
 
 
@@ -290,32 +304,32 @@
 
 def prepare(attributes, start):
     return call(
-        prepare_kernel, [columns(COLS, BF16), columns(2, BF16), ((9, 128), F32)], [VMEM] * 2,
-        [pltpu.VMEM((F * COLS, 128), F32)], 10 ** 6, 1 << 20, (attributes, start))
-
-
-def inner_part(own, ylo, yhi, zown, zylo, zyhi, cent, edge, near):
+        prepare_kernel, [columns(COLS, BF16), columns(2, BF16), ((9, 128), F32)], [ANY] * 2,
+        [pltpu.VMEM(attributes.shape, BF16), pltpu.VMEM(start.shape, F32),
+         pltpu.SemaphoreType.DMA((3,))],
+        10 ** 6, 1 << 20,
+        [pltpu.with_memory_space_constraint(a, pltpu.HBM) for a in (attributes, start)])
+
+
+def inner_part(own, ylo, yhi, zown, zy, matrix, cent, edge):
     return call(
-        inner_kernel, [columns(4 * W), columns(4 * W), ((F + 8, F), F32)],
-        [VMEM] * 7 + [SMEM, VMEM],
+        inner_kernel, [columns(4 * W), columns(4 * W), ((F + 8, F), F32)], [VMEM] * 7 + [SMEM],
         [pltpu.VMEM(*columns(4 * W)), pltpu.VMEM(*columns(COLS))],
-        5 * 10 ** 8, 3 << 20, (own, ylo, yhi, zown, zylo, zyhi, cent, edge, near))
-
-
-def outer_part(own, xlo, xhi, cent, edge, far, box, kept, sums):
+        5 * 10 ** 8, 3 << 20, (own, ylo, yhi, zown, zy, matrix, cent, edge))
+
+
+def outer_part(own, xlo, xhi, matrix, cent, edge, box, kept, sums):
     return call(
-        outer_kernel, [((9, 128), F32)],
-        [VMEM] * 4 + [SMEM] + [VMEM] * 4,
+        outer_kernel, [((9, 128), F32)], [VMEM] * 5 + [SMEM] + [VMEM] * 3,
         [pltpu.VMEM(*columns(4 * W))],
-        2 * 10 ** 8, 2 << 20, (own, xlo, xhi, cent, edge, far, box, kept, sums))[0]
-
-
-def whole_update(own, ylo, yhi, xlo, xhi, zown, zylo, zyhi, cent, edge, near, far):
+        2 * 10 ** 8, 2 << 20, (own, xlo, xhi, matrix, cent, edge, box, kept, sums))[0]
+
+
+def whole_update(own, ylo, yhi, xlo, xhi, zown, zy, matrix, cent, edge):
     return call(
-        whole_kernel, [((F, W, W, 128), F32), ((9, 128), F32)],
-        [VMEM] * 9 + [SMEM] + [VMEM] * 2,
+        whole_kernel, [((F, W, W, 128), F32), ((9, 128), F32)], [VMEM] * 9 + [SMEM],
         [pltpu.VMEM(*columns(COLS)), pltpu.VMEM(*columns(E * W))],
-        8 * 10 ** 8, 3 << 20, (own, ylo, yhi, xlo, xhi, zown, zylo, zyhi, cent, edge, near, far))
+        8 * 10 ** 8, 3 << 20, (own, ylo, yhi, xlo, xhi, zown, zy, matrix, cent, edge))
 
 
 def both_ways(up, down, axes, count):
@@ -341,28 +355,28 @@
 
 def per_device(attributes, start_centroids):
     edge = edges()
-    near, far = [jnp.asarray(halo_matrix(t), BF16) for t in z_tiles()]
+    matrix = jnp.asarray(halo_matrix(), BF16)
+    lane = lax.broadcasted_iota(jnp.int32, (1, 1, 128), 2)
     own, ends, cent = prepare(attributes, start_centroids)
-    zlo, zhi = both_ways(ends, ends, "gz", 8)
-    lane = lax.broadcasted_iota(jnp.int32, ends.shape, 2)
-    zown = jnp.where(lane % 4 < 2, zlo, zhi)
-
     grid = own.reshape(W, W, F, 128)
     ylo, yhi = both_ways(
         grid[:, W - 2:].reshape(2 * W, F, 128), grid[:, :2].reshape(2 * W, F, 128), "gy", 4)
+    zlo, zhi = both_ways(ends, ends, "gz", 8)
+    zown = jnp.where(lane % 4 < 2, zlo, zhi)
     zylo, zyhi = both_ways(zown, zown, "gy", 4)
+    zy = jnp.where(lane // 4 % W >= W // 2, zylo, zyhi)
 
     def x_slice(x, half):
         return jnp.concatenate(
             [own[x * W:x * W + 2 * W], ylo[2 * x:2 * x + 4], yhi[2 * x:2 * x + 4],
-             zown[half:half + 1], zylo[half:half + 1], zyhi[half:half + 1]])
+             zown[half:half + 1], zy[half:half + 1]])
 
     xlo, xhi = both_ways(x_slice(W - 2, 1), x_slice(0, 0), XS, 8)
 
-    box, kept, sums = inner_part(own, ylo, yhi, zown, zylo, zyhi, cent, edge, near)
-    part = outer_part(own, xlo, xhi, cent, edge, far, box, kept, sums)
+    box, kept, sums = inner_part(own, ylo, yhi, zown, zy, matrix, cent, edge)
+    part = outer_part(own, xlo, xhi, matrix, cent, edge, box, kept, sums)
     cent = total_sums(part)
-    memb, part = whole_update(own, ylo, yhi, xlo, xhi, zown, zylo, zyhi, cent, edge, near, far)
+    memb, part = whole_update(own, ylo, yhi, xlo, xhi, zown, zy, matrix, cent, edge)
     cent = total_sums(part)
     numer = cent[:8].reshape(8, 4, F).transpose(1, 0, 2).reshape(F, F)
     return numer / cent[8, :F][:, None], memb

time: 78.3 us -> 76.9 us (0.982)
  local copies, waits for them, and re-layouts: 2.2 us -> 0.44 us
    unnamed x13 -> x6, local copies, waits for them, and re-layouts: 1.82 us -> 0.06 us
    ppermute x4, waiting for transfers between devices: 1.36 us -> 2.27 us  [both_ways(): hi = lax.ppermute(down, axes, [((i + 1) % count, i) for i in range(count)])]
    ppermute x4, waiting for transfers between devices: 4.56 us -> 3.75 us  [both_ways(): lo = lax.ppermute(up, axes, [(i, (i + 1) % count) for i in range(count)])]
  transfers between devices with their start and end apart: 8 -> 8, of which waited for: 3 -> 4; matrix products, arithmetic and copies ran while one was open for 0% -> 0% of each run, Pallas kernels for 3% -> 3%
where the time goes in v6:
time: 76.9 us; the launch traced here: 76.7 us
  blocking collectives  42.1 us (55%)
  starting transfers between devices  16.8 us (22%)
  Pallas kernels  9.59 us (12%)
  waiting for transfers between devices  6.02 us (8%)
  other arithmetic  0.95 us (1%)
    all_to_all x4, blocking collectives, gather_sum(): lax.all_to_all(jnp.broadcast_to(part[None], (count,) + part.shape), axes,...  42.1 us
    ppermute x4, starting transfers between devices, both_ways(): hi = lax.ppermute(down, axes, [((i + 1) % count, i) for i in range(count)])  14.3 us
    pallas_call x4, Pallas kernels, call(): pl.pallas_call(kernel, out_shape=tuple((jax.ShapeDtypeStruct(s, t) for s,...  9.59 us
    ppermute x4, waiting for transfers between devices, both_ways(): lo = lax.ppermute(up, axes, [(i, (i + 1) % count) for i in range(count)])  3.75 us
    ppermute x4, starting transfers between devices, both_ways(): lo = lax.ppermute(up, axes, [(i, (i + 1) % count) for i in range(count)])  2.5 us
    ppermute x4, waiting for transfers between devices, both_ways(): hi = lax.ppermute(down, axes, [((i + 1) % count, i) for i in range(count)])  2.27 us
  transfers between devices with their start and end apart: 8, of which 4 were waited for; matrix products, arithmetic and copies ran while one was open for 0% of the time, Pallas kernels for 3%

profile of v6, /device:TPU:1, one launch (start us, length us, event | category | flops | bytes accessed | tf_op | source)
XLA Modules:
  0.0 76.7 jit_solution(4991212161351621380)
XLA Ops:
  0.6 1.5 %shard_map.50 = (bf16[64,32,128]{2,1,0:T(8,128)(2,1)S(1)}, bf16[2,32,128]{2,1,0:T(8,128)(2,1)S(1)}, f32[9,128]{1,0:T(8,128)S(1)}) custom-call(bf16[32,8,8,128]{3,2,1,0:T(8,128)(2,1)} %attr_hbm.1, f32[32,32]{1,0:T(8,128)} %start_hbm.1), custom_call_target="tpu_custom_call" | custom-call | flops 1000000 | bytes 1048576 | tf_op jit(solution)/shard_map/pallas_call | solution.py:290
  2.1 6.5 %collective-permute-start.3 = (bf16[2,32,128]{2,1,0:T(8,128)(2,1)S(1)}, bf16[2,32,128]{2,1,0:T(8,128)(2,1)S(1)}, u32[]{:S(2)}, u32[]{:S(2)}) collective-permute-start(bf16[2,32,128]{2,1,0:T(8,128)(2,1)S(1)} %get-tuple-element.11), channel_id=1, source_target_pairs={{1,0},{2,1},{3,2},{4,3},{5,4},{6,5},{7,6},{0,7},{9,8},{10,9},{11,1... | collective-permute-start | bytes 49160 | tf_op jit(solution)/shard_map/ppermute | solution.py:337
  8.6 0.0 collective-permute-start.2
  8.7 1.4 %collective-permute-start = (bf16[16,32,128]{2,1,0:T(8,128)(2,1)S(1)}, bf16[16,32,128]{2,1,0:T(8,128)(2,1)S(1)}, u32[]{:S(2)}, u32[]{:S(2)}) collective-permute-start(bf16[16,32,128]{2,1,0:T(8,128)(2,1)S(1)} %bitcast.16), channel_id=1, source_target_pairs={{0,8},{8,16},{16,24},{24,0},{1,9},{9,17},{17,25},{25,1},{2,10},{10... | collective-permute-start | bytes 393224 | tf_op jit(solution)/shard_map/ppermute | solution.py:336
  10.0 0.0 copy-start
  10.0 1.5 %collective-permute-start.1 = (bf16[16,32,128]{2,1,0:T(8,128)(2,1)S(1)}, bf16[16,32,128]{2,1,0:T(8,128)(2,1)S(1)}, u32[]{:S(2)}, u32[]{:S(2)}) collective-permute-start(bf16[16,32,128]{2,1,0:T(8,128)(2,1)S(1)} %bitcast.15), channel_id=1, source_target_pairs={{8,0},{16,8},{24,16},{0,24},{9,1},{17,9},{25,17},{1,25},{10,2},{18... | collective-permute-start | bytes 393224 | tf_op jit(solution)/shard_map/ppermute | solution.py:337
  11.6 0.0 collective-permute-done.3
  11.6 0.8 %collective-permute-done.2 = bf16[2,32,128]{2,1,0:T(8,128)(2,1)S(1)} collective-permute-done((bf16[2,32,128]{2,1,0:T(8,128)(2,1)S(1)}, bf16[2,32,128]{2,1,0:T(8,128)(2,1)S(1)}, u32[]{:S(2)}, u32[]{:S(2)}) %collective-permute-start.2) | collective-permute-done | bytes 16416 | tf_op jit(solution)/shard_map/ppermute | solution.py:336
  12.4 2.7 %collective-permute-start.5 = (bf16[2,32,128]{2,1,0:T(8,128)(2,1)S(1)}, bf16[2,32,128]{2,1,0:T(8,128)(2,1)S(1)}, u32[]{:S(2)}, u32[]{:S(2)}) collective-permute-start(bf16[2,32,128]{2,1,0:T(8,128)(2,1)S(1)} %broadcast_select_fusion.1.zown), channel_id=1, source_target_pairs={{8,0},{16,8},{24,16},{0,24},{9,1},{17,9},{25,17},{1,25},{10,2},{18... | collective-permute-start | bytes 49160 | tf_op jit(solution)/shard_map/ppermute | solution.py:337
  15.2 0.0 collective-permute-start.4
  15.2 0.9 %collective-permute-done.5 = bf16[2,32,128]{2,1,0:T(8,128)(2,1)S(1)} collective-permute-done((bf16[2,32,128]{2,1,0:T(8,128)(2,1)S(1)}, bf16[2,32,128]{2,1,0:T(8,128)(2,1)S(1)}, u32[]{:S(2)}, u32[]{:S(2)}) %collective-permute-start.5) | collective-permute-done | bytes 16416 | tf_op jit(solution)/shard_map/ppermute | solution.py:337
  16.0 2.9 %collective-permute-done.4 = bf16[2,32,128]{2,1,0:T(8,128)(2,1)S(1)} collective-permute-done((bf16[2,32,128]{2,1,0:T(8,128)(2,1)S(1)}, bf16[2,32,128]{2,1,0:T(8,128)(2,1)S(1)}, u32[]{:S(2)}, u32[]{:S(2)}) %collective-permute-start.4) | collective-permute-done | bytes 16416 | tf_op jit(solution)/shard_map/ppermute | solution.py:336
  19.0 0.0 collective-permute-done.ylo
  19.0 0.0 collective-permute-done.1.yhi
  19.1 3.5 %collective-permute-start.7 = (bf16[26,32,128]{2,1,0:T(8,128)(2,1)S(1)}, bf16[26,32,128]{2,1,0:T(8,128)(2,1)S(1)}, u32[]{:S(2)}, u32[]{:S(2)}) collective-permute-start(bf16[26,32,128]{2,1,0:T(8,128)(2,1)S(1)} %get-tuple-element.26), channel_id=1, source_target_pairs={{32,0},{64,32},{96,64},{128,96},{160,128},{192,160},{224,192},{0,2... | collective-permute-start | bytes 638984 | tf_op jit(solution)/shard_map/ppermute | solution.py:337
  22.6 1.1 %collective-permute-start.6 = (bf16[26,32,128]{2,1,0:T(8,128)(2,1)S(1)}, bf16[26,32,128]{2,1,0:T(8,128)(2,1)S(1)}, u32[]{:S(2)}, u32[]{:S(2)}) collective-permute-start(bf16[26,32,128]{2,1,0:T(8,128)(2,1)S(1)} %get-tuple-element.27), channel_id=1, source_target_pairs={{0,32},{32,64},{64,96},{96,128},{128,160},{160,192},{192,224},{224... | collective-permute-start | bytes 638984 | tf_op jit(solution)/shard_map/ppermute | solution.py:336
  23.7 0.1 stack.27
  23.8 0.0 copy-done
  23.8 2.3 %shard_map.51 = (f32[32,32,128]{2,1,0:T(8,128)S(1)}, f32[32,32,128]{2,1,0:T(8,128)S(1)}, f32[40,32]{1,0:T(8,128)S(1)}) custom-call(bf16[64,32,128]{2,1,0:T(8,128)(2,1)S(1)} %get-tuple-element.10.own, bf16[16,32,128]{2,1,0:T(8,128)(2,1)S(1)} %collective-permute-done.ylo, bf16[16,32,128]{2,1,0:T(8,128)(2,1)S(1)} %collective-permute-done.1.yhi, ...), custom_call_target="tpu_custom_call" | custom-call | flops 500000000 | bytes 3145728 | tf_op jit(solution)/shard_map/pallas_call | solution.py:290
  26.1 1.4 %collective-permute-done.7.xhi = bf16[26,32,128]{2,1,0:T(8,128)(2,1)S(1)} collective-permute-done((bf16[26,32,128]{2,1,0:T(8,128)(2,1)S(1)}, bf16[26,32,128]{2,1,0:T(8,128)(2,1)S(1)}, u32[]{:S(2)}, u32[]{:S(2)}) %collective-permute-start.7) | collective-permute-done | bytes 213024 | tf_op jit(solution)/shard_map/ppermute | solution.py:337
  27.5 0.0 collective-permute-done.6.xlo
  27.5 1.8 %shard_map.52 = f32[9,128]{1,0:T(8,128)S(1)} custom-call(bf16[64,32,128]{2,1,0:T(8,128)(2,1)S(1)} %get-tuple-element.10.own, bf16[26,32,128]{2,1,0:T(8,128)(2,1)S(1)} %collective-permute-done.6.xlo, bf16[26,32,128]{2,1,0:T(8,128)(2,1)S(1)} %collective-permute-done.7.xhi, bf16[768,256]{1,0:T(8,128)(2,1)S(1)} %copy-done, f32[9,128]{1,0:T(8,128)S(1)} %get-tuple-element.12.cent, ...), custom_call_target="tpu_custom_call" | custom-call | flops 200000000 | bytes 2097152 | tf_op jit(solution)/shard_map/pallas_call | solution.py:290
  29.4 11.4 %all_to_all.20 = f32[16,9,1,128]{3,2,1,0:T(1,128)S(1)} all-to-all(f32[16,9,1,128]{3,2,1,0:T(1,128)S(1)} %broadcast_in_dim.37), channel_id=1, replica_groups=mesh['cx'=4,'core'=2,'gy'=4,'gz'=8] {'core','gz'}, dimensions={0} | all-to-all | bytes 147456 | tf_op jit(solution)/shard_map/all_to_all | solution.py:342
  40.7 0.1 reduce_sum.36
  40.8 9.2 %all_to_all.21 = f32[16,9,1,128]{3,2,1,0:T(1,128)S(1)} all-to-all(f32[16,9,1,128]{3,2,1,0:T(1,128)S(1)} %broadcast_in_dim.38), channel_id=1, replica_groups=mesh['cx'=4,'core'=2,'gy'=4,'gz'=8] {'cx','gy'}, dimensions={0} | all-to-all | bytes 147456 | tf_op jit(solution)/shard_map/all_to_all | solution.py:342
  50.1 0.1 reduce_sum.37.cent
  50.1 4.0 %shard_map.53 = (f32[32,8,8,128]{3,2,1,0:T(8,128)}, f32[9,128]{1,0:T(8,128)S(1)}) custom-call(bf16[64,32,128]{2,1,0:T(8,128)(2,1)S(1)} %get-tuple-element.10.own, bf16[16,32,128]{2,1,0:T(8,128)(2,1)S(1)} %collective-permute-done.ylo, bf16[16,32,128]{2,1,0:T(8,128)(2,1)S(1)} %collective-permute-done.1.yhi, ...), custom_call_target="tpu_custom_call" | custom-call | flops 800000000 | bytes 3145728 | tf_op jit(solution)/shard_map/pallas_call | solution.py:290
  54.2 12.0 %all_to_all.22 = f32[16,9,1,128]{3,2,1,0:T(1,128)S(1)} all-to-all(f32[16,9,1,128]{3,2,1,0:T(1,128)S(1)} %broadcast_in_dim.39), channel_id=1, replica_groups=mesh['cx'=4,'core'=2,'gy'=4,'gz'=8] {'core','gz'}, dimensions={0} | all-to-all | bytes 147456 | tf_op jit(solution)/shard_map/all_to_all | solution.py:342
  66.2 0.1 reduce_sum.38
  66.3 9.5 %all_to_all.23 = f32[16,9,1,128]{3,2,1,0:T(1,128)S(1)} all-to-all(f32[16,9,1,128]{3,2,1,0:T(1,128)S(1)} %broadcast_in_dim.40), channel_id=1, replica_groups=mesh['cx'=4,'core'=2,'gy'=4,'gz'=8] {'cx','gy'}, dimensions={0} | all-to-all | bytes 147456 | tf_op jit(solution)/shard_map/all_to_all | solution.py:342
  75.8 0.1 reduce_sum.39
  75.9 0.1 reshape.122
  76.0 0.7 bitcast_divide_fusion
  (17 shorter events, 0.3 us)
Async XLA Ops:
  2.1 9.5 %collective-permute-start.3 = (bf16[2,32,128]{2,1,0:T(8,128)(2,1)S(1)}, bf16[2,32,128]{2,1,0:T(8,128)(2,1)S(1)}, u32[]{:S(2)}, u32[]{:S(2)}) collective-permute-start(bf16[2,32,128]{2,1,0:T(8,128)(2,1)S(1)} %get-tuple-element.11), channel_id=1, source_target_pairs={{1,0},{2,1},{3,2},{4,3},{5,4},{6,5},{7,6},{0,7},{9,8},{10,9},{11,1... | collective-permute-start | bytes 49160 | tf_op jit(solution)/shard_map/ppermute | solution.py:337
  8.6 3.8 %collective-permute-start.2 = (bf16[2,32,128]{2,1,0:T(8,128)(2,1)S(1)}, bf16[2,32,128]{2,1,0:T(8,128)(2,1)S(1)}, u32[]{:S(2)}, u32[]{:S(2)}) collective-permute-start(bf16[2,32,128]{2,1,0:T(8,128)(2,1)S(1)} %get-tuple-element.11), channel_id=1, source_target_pairs={{0,1},{1,2},{2,3},{3,4},{4,5},{5,6},{6,7},{7,0},{8,9},{9,10},{10,1... | collective-permute-start | bytes 49160 | tf_op jit(solution)/shard_map/ppermute | solution.py:336
  8.7 10.3 %collective-permute-start = (bf16[16,32,128]{2,1,0:T(8,128)(2,1)S(1)}, bf16[16,32,128]{2,1,0:T(8,128)(2,1)S(1)}, u32[]{:S(2)}, u32[]{:S(2)}) collective-permute-start(bf16[16,32,128]{2,1,0:T(8,128)(2,1)S(1)} %bitcast.16), channel_id=1, source_target_pairs={{0,8},{8,16},{16,24},{24,0},{1,9},{9,17},{17,25},{25,1},{2,10},{10... | collective-permute-start | bytes 393224 | tf_op jit(solution)/shard_map/ppermute | solution.py:336
  10.0 13.8 %copy-start = (bf16[768,256]{1,0:T(8,128)(2,1)S(1)}, bf16[768,256]{1,0:T(8,128)(2,1)}, u32[]{:S(2)}) copy-start(bf16[768,256]{1,0:T(8,128)(2,1)} %constant.70.clone.matrix) | copy-start | bytes 1179652
  10.0 9.0 %collective-permute-start.1 = (bf16[16,32,128]{2,1,0:T(8,128)(2,1)S(1)}, bf16[16,32,128]{2,1,0:T(8,128)(2,1)S(1)}, u32[]{:S(2)}, u32[]{:S(2)}) collective-permute-start(bf16[16,32,128]{2,1,0:T(8,128)(2,1)S(1)} %bitcast.15), channel_id=1, source_target_pairs={{8,0},{16,8},{24,16},{0,24},{9,1},{17,9},{25,17},{1,25},{10,2},{18... | collective-permute-start | bytes 393224 | tf_op jit(solution)/shard_map/ppermute | solution.py:337
  12.4 3.6 %collective-permute-start.5 = (bf16[2,32,128]{2,1,0:T(8,128)(2,1)S(1)}, bf16[2,32,128]{2,1,0:T(8,128)(2,1)S(1)}, u32[]{:S(2)}, u32[]{:S(2)}) collective-permute-start(bf16[2,32,128]{2,1,0:T(8,128)(2,1)S(1)} %broadcast_select_fusion.1.zown), channel_id=1, source_target_pairs={{8,0},{16,8},{24,16},{0,24},{9,1},{17,9},{25,17},{1,25},{10,2},{18... | collective-permute-start | bytes 49160 | tf_op jit(solution)/shard_map/ppermute | solution.py:337
  15.2 3.8 %collective-permute-start.4 = (bf16[2,32,128]{2,1,0:T(8,128)(2,1)S(1)}, bf16[2,32,128]{2,1,0:T(8,128)(2,1)S(1)}, u32[]{:S(2)}, u32[]{:S(2)}) collective-permute-start(bf16[2,32,128]{2,1,0:T(8,128)(2,1)S(1)} %broadcast_select_fusion.1.zown), channel_id=1, source_target_pairs={{0,8},{8,16},{16,24},{24,0},{1,9},{9,17},{17,25},{25,1},{2,10},{10... | collective-permute-start | bytes 49160 | tf_op jit(solution)/shard_map/ppermute | solution.py:336
  19.1 8.5 %collective-permute-start.7 = (bf16[26,32,128]{2,1,0:T(8,128)(2,1)S(1)}, bf16[26,32,128]{2,1,0:T(8,128)(2,1)S(1)}, u32[]{:S(2)}, u32[]{:S(2)}) collective-permute-start(bf16[26,32,128]{2,1,0:T(8,128)(2,1)S(1)} %get-tuple-element.26), channel_id=1, source_target_pairs={{32,0},{64,32},{96,64},{128,96},{160,128},{192,160},{224,192},{0,2... | collective-permute-start | bytes 638984 | tf_op jit(solution)/shard_map/ppermute | solution.py:337
  22.6 4.9 %collective-permute-start.6 = (bf16[26,32,128]{2,1,0:T(8,128)(2,1)S(1)}, bf16[26,32,128]{2,1,0:T(8,128)(2,1)S(1)}, u32[]{:S(2)}, u32[]{:S(2)}) collective-permute-start(bf16[26,32,128]{2,1,0:T(8,128)(2,1)S(1)} %get-tuple-element.27), channel_id=1, source_target_pairs={{0,32},{32,64},{64,96},{96,128},{128,160},{160,192},{192,224},{224... | collective-permute-start | bytes 638984 | tf_op jit(solution)/shard_map/ppermute | solution.py:336

commit v7 on v6

--- a/solution.py
+++ b/solution.py
@@ -110,7 +110,7 @@
         c = unpacked_centroids(cent)
         self.cbm2 = (-2.0 * c.astype(BF16).astype(F32)).astype(BF16)
         self.csq1 = jnp.broadcast_to(jnp.sum(c * c, axis=1, keepdims=True) + 1.0, (F, 128))
-        self.xlo, self.xhi, self.ylo, self.yhi, self.zlo, self.zhi = [edge[i] for i in range(6)]
+        self.xlo, self.xhi, self.ylo, self.yhi, self.zlo, self.zhi = [edge[i:i + 1, :] for i in range(6)]
         self.band = band_matrix()
         self.lane = lax.broadcasted_iota(jnp.int32, (1, 128), 1)
         self.numer = jnp.zeros((F, F), F32)
@@ -283,7 +283,6 @@
 
 VMEM = pl.BlockSpec(memory_space=pltpu.VMEM)
 ANY = pl.BlockSpec(memory_space=pl.ANY)
-SMEM = pl.BlockSpec(memory_space=pltpu.SMEM)
 
 
 def call(kernel, out_shape, in_specs, scratch_shapes, flops, moved, args):
@@ -313,21 +312,21 @@
 
 def inner_part(own, ylo, yhi, zown, zy, matrix, cent, edge):
     return call(
-        inner_kernel, [columns(4 * W), columns(4 * W), ((F + 8, F), F32)], [VMEM] * 7 + [SMEM],
+        inner_kernel, [columns(4 * W), columns(4 * W), ((F + 8, F), F32)], [VMEM] * 8,
         [pltpu.VMEM(*columns(4 * W)), pltpu.VMEM(*columns(COLS))],
         5 * 10 ** 8, 3 << 20, (own, ylo, yhi, zown, zy, matrix, cent, edge))
 
 
 def outer_part(own, xlo, xhi, matrix, cent, edge, box, kept, sums):
     return call(
-        outer_kernel, [((9, 128), F32)], [VMEM] * 5 + [SMEM] + [VMEM] * 3,
+        outer_kernel, [((9, 128), F32)], [VMEM] * 9,
         [pltpu.VMEM(*columns(4 * W))],
         2 * 10 ** 8, 2 << 20, (own, xlo, xhi, matrix, cent, edge, box, kept, sums))[0]
 
 
 def whole_update(own, ylo, yhi, xlo, xhi, zown, zy, matrix, cent, edge):
     return call(
-        whole_kernel, [((F, W, W, 128), F32), ((9, 128), F32)], [VMEM] * 9 + [SMEM],
+        whole_kernel, [((F, W, W, 128), F32), ((9, 128), F32)], [VMEM] * 10,
         [pltpu.VMEM(*columns(COLS)), pltpu.VMEM(*columns(E * W))],
         8 * 10 ** 8, 3 << 20, (own, ylo, yhi, xlo, xhi, zown, zy, matrix, cent, edge))
 
@@ -350,7 +349,11 @@
 
 def edges():
     gx, gy, gz = lax.axis_index(XS), lax.axis_index("gy"), lax.axis_index("gz")
-    return jnp.stack([gx > 0, gx < 7, gy > 0, gy < 3, gz > 0, gz < 7]).astype(F32)
+    row = lax.broadcasted_iota(jnp.int32, (8, 128), 0)
+    inside = jnp.zeros((8, 128), jnp.bool_)
+    for i, has in enumerate((gx > 0, gx < 7, gy > 0, gy < 3, gz > 0, gz < 7)):
+        inside = inside | ((row == i) & has)
+    return inside.astype(F32)
 
 
 def per_device(attributes, start_centroids):

time: 76.9 us -> 75.9 us (0.987)
  Pallas kernels: 9.59 us -> 7.98 us
    pallas_call x4, Pallas kernels: 9.59 us -> 7.98 us  [call(): pl.pallas_call(kernel, out_shape=tuple((jax.ShapeDtypeStruct(s, t) for s,...]
  transfers between devices with their start and end apart: 8 -> 8, of which waited for: 4 -> 4; matrix products, arithmetic and copies ran while one was open for 0% -> 0% of each run, Pallas kernels for 3% -> 2%
where the time goes in v7:
time: 75.9 us; the launch traced here: 75.6 us
  blocking collectives  42.1 us (55%)
  starting transfers between devices  16.8 us (22%)
  Pallas kernels  7.98 us (11%)
  waiting for transfers between devices  6.58 us (9%)
  other arithmetic  0.95 us (1%)
    all_to_all x4, blocking collectives, gather_sum(): lax.all_to_all(jnp.broadcast_to(part[None], (count,) + part.shape), axes,...  42.1 us
    ppermute x4, starting transfers between devices, both_ways(): hi = lax.ppermute(down, axes, [((i + 1) % count, i) for i in range(count)])  14.3 us
    pallas_call x4, Pallas kernels, call(): pl.pallas_call(kernel, out_shape=tuple((jax.ShapeDtypeStruct(s, t) for s,...  7.98 us
    ppermute x4, waiting for transfers between devices, both_ways(): lo = lax.ppermute(up, axes, [(i, (i + 1) % count) for i in range(count)])  3.75 us
    ppermute x4, waiting for transfers between devices, both_ways(): hi = lax.ppermute(down, axes, [((i + 1) % count, i) for i in range(count)])  2.83 us
    ppermute x4, starting transfers between devices, both_ways(): lo = lax.ppermute(up, axes, [(i, (i + 1) % count) for i in range(count)])  2.5 us
  transfers between devices with their start and end apart: 8, of which 4 were waited for; matrix products, arithmetic and copies ran while one was open for 0% of the time, Pallas kernels for 2%

profile of v7, /device:TPU:1, one launch (start us, length us, event | category | flops | bytes accessed | tf_op | source)
XLA Modules:
  0.0 75.6 jit_solution(8770270024171379768)
XLA Ops:
  0.6 1.5 %shard_map.50 = (bf16[64,32,128]{2,1,0:T(8,128)(2,1)S(1)}, bf16[2,32,128]{2,1,0:T(8,128)(2,1)S(1)}, f32[9,128]{1,0:T(8,128)S(1)}) custom-call(bf16[32,8,8,128]{3,2,1,0:T(8,128)(2,1)} %attr_hbm.1, f32[32,32]{1,0:T(8,128)} %start_hbm.1), custom_call_target="tpu_custom_call" | custom-call | flops 1000000 | bytes 1048576 | tf_op jit(solution)/shard_map/pallas_call | solution.py:289
  2.1 6.5 %collective-permute-start.3 = (bf16[2,32,128]{2,1,0:T(8,128)(2,1)S(1)}, bf16[2,32,128]{2,1,0:T(8,128)(2,1)S(1)}, u32[]{:S(2)}, u32[]{:S(2)}) collective-permute-start(bf16[2,32,128]{2,1,0:T(8,128)(2,1)S(1)} %get-tuple-element.11), channel_id=1, source_target_pairs={{1,0},{2,1},{3,2},{4,3},{5,4},{6,5},{7,6},{0,7},{9,8},{10,9},{11,1... | collective-permute-start | bytes 49160 | tf_op jit(solution)/shard_map/ppermute | solution.py:336
  8.6 0.0 collective-permute-start.2
  8.7 1.4 %collective-permute-start = (bf16[16,32,128]{2,1,0:T(8,128)(2,1)S(1)}, bf16[16,32,128]{2,1,0:T(8,128)(2,1)S(1)}, u32[]{:S(2)}, u32[]{:S(2)}) collective-permute-start(bf16[16,32,128]{2,1,0:T(8,128)(2,1)S(1)} %bitcast.10), channel_id=1, source_target_pairs={{0,8},{8,16},{16,24},{24,0},{1,9},{9,17},{17,25},{25,1},{2,10},{10... | collective-permute-start | bytes 393224 | tf_op jit(solution)/shard_map/ppermute | solution.py:335
  10.0 0.0 copy-start
  10.0 1.5 %collective-permute-start.1 = (bf16[16,32,128]{2,1,0:T(8,128)(2,1)S(1)}, bf16[16,32,128]{2,1,0:T(8,128)(2,1)S(1)}, u32[]{:S(2)}, u32[]{:S(2)}) collective-permute-start(bf16[16,32,128]{2,1,0:T(8,128)(2,1)S(1)} %bitcast.9), channel_id=1, source_target_pairs={{8,0},{16,8},{24,16},{0,24},{9,1},{17,9},{25,17},{1,25},{10,2},{18... | collective-permute-start | bytes 393224 | tf_op jit(solution)/shard_map/ppermute | solution.py:336
  11.6 0.0 collective-permute-done.3
  11.6 0.8 %collective-permute-done.2 = bf16[2,32,128]{2,1,0:T(8,128)(2,1)S(1)} collective-permute-done((bf16[2,32,128]{2,1,0:T(8,128)(2,1)S(1)}, bf16[2,32,128]{2,1,0:T(8,128)(2,1)S(1)}, u32[]{:S(2)}, u32[]{:S(2)}) %collective-permute-start.2) | collective-permute-done | bytes 16416 | tf_op jit(solution)/shard_map/ppermute | solution.py:335
  12.4 2.7 %collective-permute-start.5 = (bf16[2,32,128]{2,1,0:T(8,128)(2,1)S(1)}, bf16[2,32,128]{2,1,0:T(8,128)(2,1)S(1)}, u32[]{:S(2)}, u32[]{:S(2)}) collective-permute-start(bf16[2,32,128]{2,1,0:T(8,128)(2,1)S(1)} %broadcast_select_fusion.1.zown), channel_id=1, source_target_pairs={{8,0},{16,8},{24,16},{0,24},{9,1},{17,9},{25,17},{1,25},{10,2},{18... | collective-permute-start | bytes 49160 | tf_op jit(solution)/shard_map/ppermute | solution.py:336
  15.2 0.0 collective-permute-start.4
  15.2 0.9 %collective-permute-done.5 = bf16[2,32,128]{2,1,0:T(8,128)(2,1)S(1)} collective-permute-done((bf16[2,32,128]{2,1,0:T(8,128)(2,1)S(1)}, bf16[2,32,128]{2,1,0:T(8,128)(2,1)S(1)}, u32[]{:S(2)}, u32[]{:S(2)}) %collective-permute-start.5) | collective-permute-done | bytes 16416 | tf_op jit(solution)/shard_map/ppermute | solution.py:336
  16.0 2.9 %collective-permute-done.4 = bf16[2,32,128]{2,1,0:T(8,128)(2,1)S(1)} collective-permute-done((bf16[2,32,128]{2,1,0:T(8,128)(2,1)S(1)}, bf16[2,32,128]{2,1,0:T(8,128)(2,1)S(1)}, u32[]{:S(2)}, u32[]{:S(2)}) %collective-permute-start.4) | collective-permute-done | bytes 16416 | tf_op jit(solution)/shard_map/ppermute | solution.py:335
  19.0 0.0 collective-permute-done.ylo
  19.0 0.0 collective-permute-done.1.yhi
  19.1 3.5 %collective-permute-start.7 = (bf16[26,32,128]{2,1,0:T(8,128)(2,1)S(1)}, bf16[26,32,128]{2,1,0:T(8,128)(2,1)S(1)}, u32[]{:S(2)}, u32[]{:S(2)}) collective-permute-start(bf16[26,32,128]{2,1,0:T(8,128)(2,1)S(1)} %get-tuple-element.26), channel_id=1, source_target_pairs={{32,0},{64,32},{96,64},{128,96},{160,128},{192,160},{224,192},{0,2... | collective-permute-start | bytes 638984 | tf_op jit(solution)/shard_map/ppermute | solution.py:336
  22.6 1.1 %collective-permute-start.6 = (bf16[26,32,128]{2,1,0:T(8,128)(2,1)S(1)}, bf16[26,32,128]{2,1,0:T(8,128)(2,1)S(1)}, u32[]{:S(2)}, u32[]{:S(2)}) collective-permute-start(bf16[26,32,128]{2,1,0:T(8,128)(2,1)S(1)} %get-tuple-element.27), channel_id=1, source_target_pairs={{0,32},{32,64},{64,96},{96,128},{128,160},{160,192},{192,224},{224... | collective-permute-start | bytes 638984 | tf_op jit(solution)/shard_map/ppermute | solution.py:335
  23.7 0.1 iota.35.edge
  23.8 0.0 copy-done
  23.8 1.7 %shard_map.51 = (f32[32,32,128]{2,1,0:T(8,128)S(1)}, f32[32,32,128]{2,1,0:T(8,128)S(1)}, f32[40,32]{1,0:T(8,128)S(1)}) custom-call(bf16[64,32,128]{2,1,0:T(8,128)(2,1)S(1)} %get-tuple-element.10.own, bf16[16,32,128]{2,1,0:T(8,128)(2,1)S(1)} %collective-permute-done.ylo, bf16[16,32,128]{2,1,0:T(8,128)(2,1)S(1)} %collective-permute-done.1.yhi, ...), custom_call_target="tpu_custom_call" | custom-call | flops 500000000 | bytes 3145728 | tf_op jit(solution)/shard_map/pallas_call | solution.py:289
  25.6 2.0 %collective-permute-done.7.xhi = bf16[26,32,128]{2,1,0:T(8,128)(2,1)S(1)} collective-permute-done((bf16[26,32,128]{2,1,0:T(8,128)(2,1)S(1)}, bf16[26,32,128]{2,1,0:T(8,128)(2,1)S(1)}, u32[]{:S(2)}, u32[]{:S(2)}) %collective-permute-start.7) | collective-permute-done | bytes 213024 | tf_op jit(solution)/shard_map/ppermute | solution.py:336
  27.5 0.0 collective-permute-done.6.xlo
  27.5 1.2 %shard_map.52 = f32[9,128]{1,0:T(8,128)S(1)} custom-call(bf16[64,32,128]{2,1,0:T(8,128)(2,1)S(1)} %get-tuple-element.10.own, bf16[26,32,128]{2,1,0:T(8,128)(2,1)S(1)} %collective-permute-done.6.xlo, bf16[26,32,128]{2,1,0:T(8,128)(2,1)S(1)} %collective-permute-done.7.xhi, bf16[768,256]{1,0:T(8,128)(2,1)S(1)} %copy-done, f32[9,128]{1,0:T(8,128)S(1)} %get-tuple-element.12.cent, ...), custom_call_target="tpu_custom_call" | custom-call | flops 200000000 | bytes 2097152 | tf_op jit(solution)/shard_map/pallas_call | solution.py:289
  28.8 11.4 %all_to_all.20 = f32[16,9,1,128]{3,2,1,0:T(1,128)S(1)} all-to-all(f32[16,9,1,128]{3,2,1,0:T(1,128)S(1)} %broadcast_in_dim.37), channel_id=1, replica_groups=mesh['cx'=4,'core'=2,'gy'=4,'gz'=8] {'core','gz'}, dimensions={0} | all-to-all | bytes 147456 | tf_op jit(solution)/shard_map/all_to_all | solution.py:341
  40.2 0.1 reduce_sum.36
  40.3 9.2 %all_to_all.21 = f32[16,9,1,128]{3,2,1,0:T(1,128)S(1)} all-to-all(f32[16,9,1,128]{3,2,1,0:T(1,128)S(1)} %broadcast_in_dim.38), channel_id=1, replica_groups=mesh['cx'=4,'core'=2,'gy'=4,'gz'=8] {'cx','gy'}, dimensions={0} | all-to-all | bytes 147456 | tf_op jit(solution)/shard_map/all_to_all | solution.py:341
  49.5 0.1 reduce_sum.37.cent
  49.6 3.5 %shard_map.53 = (f32[32,8,8,128]{3,2,1,0:T(8,128)}, f32[9,128]{1,0:T(8,128)S(1)}) custom-call(bf16[64,32,128]{2,1,0:T(8,128)(2,1)S(1)} %get-tuple-element.10.own, bf16[16,32,128]{2,1,0:T(8,128)(2,1)S(1)} %collective-permute-done.ylo, bf16[16,32,128]{2,1,0:T(8,128)(2,1)S(1)} %collective-permute-done.1.yhi, ...), custom_call_target="tpu_custom_call" | custom-call | flops 800000000 | bytes 3145728 | tf_op jit(solution)/shard_map/pallas_call | solution.py:289
  53.1 12.0 %all_to_all.22 = f32[16,9,1,128]{3,2,1,0:T(1,128)S(1)} all-to-all(f32[16,9,1,128]{3,2,1,0:T(1,128)S(1)} %broadcast_in_dim.39), channel_id=1, replica_groups=mesh['cx'=4,'core'=2,'gy'=4,'gz'=8] {'core','gz'}, dimensions={0} | all-to-all | bytes 147456 | tf_op jit(solution)/shard_map/all_to_all | solution.py:341
  65.2 0.1 reduce_sum.38
  65.3 9.5 %all_to_all.23 = f32[16,9,1,128]{3,2,1,0:T(1,128)S(1)} all-to-all(f32[16,9,1,128]{3,2,1,0:T(1,128)S(1)} %broadcast_in_dim.40), channel_id=1, replica_groups=mesh['cx'=4,'core'=2,'gy'=4,'gz'=8] {'cx','gy'}, dimensions={0} | all-to-all | bytes 147456 | tf_op jit(solution)/shard_map/all_to_all | solution.py:341
  74.8 0.1 reduce_sum.39
  74.9 0.1 reshape.122
  74.9 0.7 bitcast_divide_fusion
  (17 shorter events, 0.3 us)
Async XLA Ops:
  2.1 9.5 %collective-permute-start.3 = (bf16[2,32,128]{2,1,0:T(8,128)(2,1)S(1)}, bf16[2,32,128]{2,1,0:T(8,128)(2,1)S(1)}, u32[]{:S(2)}, u32[]{:S(2)}) collective-permute-start(bf16[2,32,128]{2,1,0:T(8,128)(2,1)S(1)} %get-tuple-element.11), channel_id=1, source_target_pairs={{1,0},{2,1},{3,2},{4,3},{5,4},{6,5},{7,6},{0,7},{9,8},{10,9},{11,1... | collective-permute-start | bytes 49160 | tf_op jit(solution)/shard_map/ppermute | solution.py:336
  8.6 3.8 %collective-permute-start.2 = (bf16[2,32,128]{2,1,0:T(8,128)(2,1)S(1)}, bf16[2,32,128]{2,1,0:T(8,128)(2,1)S(1)}, u32[]{:S(2)}, u32[]{:S(2)}) collective-permute-start(bf16[2,32,128]{2,1,0:T(8,128)(2,1)S(1)} %get-tuple-element.11), channel_id=1, source_target_pairs={{0,1},{1,2},{2,3},{3,4},{4,5},{5,6},{6,7},{7,0},{8,9},{9,10},{10,1... | collective-permute-start | bytes 49160 | tf_op jit(solution)/shard_map/ppermute | solution.py:335
  8.7 10.3 %collective-permute-start = (bf16[16,32,128]{2,1,0:T(8,128)(2,1)S(1)}, bf16[16,32,128]{2,1,0:T(8,128)(2,1)S(1)}, u32[]{:S(2)}, u32[]{:S(2)}) collective-permute-start(bf16[16,32,128]{2,1,0:T(8,128)(2,1)S(1)} %bitcast.10), channel_id=1, source_target_pairs={{0,8},{8,16},{16,24},{24,0},{1,9},{9,17},{17,25},{25,1},{2,10},{10... | collective-permute-start | bytes 393224 | tf_op jit(solution)/shard_map/ppermute | solution.py:335
  10.0 13.8 %copy-start = (bf16[768,256]{1,0:T(8,128)(2,1)S(1)}, bf16[768,256]{1,0:T(8,128)(2,1)}, u32[]{:S(2)}) copy-start(bf16[768,256]{1,0:T(8,128)(2,1)} %constant.77.clone.matrix) | copy-start | bytes 1179652
  10.0 9.0 %collective-permute-start.1 = (bf16[16,32,128]{2,1,0:T(8,128)(2,1)S(1)}, bf16[16,32,128]{2,1,0:T(8,128)(2,1)S(1)}, u32[]{:S(2)}, u32[]{:S(2)}) collective-permute-start(bf16[16,32,128]{2,1,0:T(8,128)(2,1)S(1)} %bitcast.9), channel_id=1, source_target_pairs={{8,0},{16,8},{24,16},{0,24},{9,1},{17,9},{25,17},{1,25},{10,2},{18... | collective-permute-start | bytes 393224 | tf_op jit(solution)/shard_map/ppermute | solution.py:336
  12.4 3.6 %collective-permute-start.5 = (bf16[2,32,128]{2,1,0:T(8,128)(2,1)S(1)}, bf16[2,32,128]{2,1,0:T(8,128)(2,1)S(1)}, u32[]{:S(2)}, u32[]{:S(2)}) collective-permute-start(bf16[2,32,128]{2,1,0:T(8,128)(2,1)S(1)} %broadcast_select_fusion.1.zown), channel_id=1, source_target_pairs={{8,0},{16,8},{24,16},{0,24},{9,1},{17,9},{25,17},{1,25},{10,2},{18... | collective-permute-start | bytes 49160 | tf_op jit(solution)/shard_map/ppermute | solution.py:336
  15.2 3.8 %collective-permute-start.4 = (bf16[2,32,128]{2,1,0:T(8,128)(2,1)S(1)}, bf16[2,32,128]{2,1,0:T(8,128)(2,1)S(1)}, u32[]{:S(2)}, u32[]{:S(2)}) collective-permute-start(bf16[2,32,128]{2,1,0:T(8,128)(2,1)S(1)} %broadcast_select_fusion.1.zown), channel_id=1, source_target_pairs={{0,8},{8,16},{16,24},{24,0},{1,9},{9,17},{17,25},{25,1},{2,10},{10... | collective-permute-start | bytes 49160 | tf_op jit(solution)/shard_map/ppermute | solution.py:335
  19.1 8.5 %collective-permute-start.7 = (bf16[26,32,128]{2,1,0:T(8,128)(2,1)S(1)}, bf16[26,32,128]{2,1,0:T(8,128)(2,1)S(1)}, u32[]{:S(2)}, u32[]{:S(2)}) collective-permute-start(bf16[26,32,128]{2,1,0:T(8,128)(2,1)S(1)} %get-tuple-element.26), channel_id=1, source_target_pairs={{32,0},{64,32},{96,64},{128,96},{160,128},{192,160},{224,192},{0,2... | collective-permute-start | bytes 638984 | tf_op jit(solution)/shard_map/ppermute | solution.py:336
  22.6 4.9 %collective-permute-start.6 = (bf16[26,32,128]{2,1,0:T(8,128)(2,1)S(1)}, bf16[26,32,128]{2,1,0:T(8,128)(2,1)S(1)}, u32[]{:S(2)}, u32[]{:S(2)}) collective-permute-start(bf16[26,32,128]{2,1,0:T(8,128)(2,1)S(1)} %get-tuple-element.27), channel_id=1, source_target_pairs={{0,32},{32,64},{64,96},{96,128},{128,160},{160,192},{192,224},{224... | collective-permute-start | bytes 638984 | tf_op jit(solution)/shard_map/ppermute | solution.py:335

commit v8 on v7

--- a/solution.py
+++ b/solution.py
@@ -41,8 +41,7 @@
 
 
 def recip(x):
-    r = pl.reciprocal(x, approx=True)
-    return r * (2.0 - x * r)
+    return pl.reciprocal(x, approx=True)
 
 
 def dot_lanes(a, b):
@@ -61,8 +60,8 @@
 
 
 def store_sums(part, numer, denom):
-    part[0:8, :] = jnp.concatenate([numer[8 * g:8 * g + 8] for g in range(4)], axis=1)
-    part[8:9, :] = jnp.concatenate([denom[0:1]] * 4, axis=1)
+    packed = jnp.concatenate([numer[8 * g:8 * g + 8] for g in range(4)], axis=1)
+    part[...] = jnp.concatenate([packed, jnp.concatenate([denom] * 4, axis=1)], axis=0).astype(BF16)
 
 
 def turned8(v):
@@ -114,6 +113,7 @@
         self.band = band_matrix()
         self.lane = lax.broadcasted_iota(jnp.int32, (1, 128), 1)
         self.numer = jnp.zeros((F, F), F32)
+        self.ends = jnp.where((self.lane < 2) | (self.lane >= 126), 1.0, 0.0)
         self.denom = jnp.zeros((8, F), F32)
 
     def inverse(self, a):
@@ -171,7 +171,7 @@
     def halo_of(self, windows, c):
         half = windows[:, c // 32 * 128:c // 32 * 128 + 128]
         turned = pltpu.roll(half, (126 - 4 * (c % 32)) % 128, 1)
-        return jnp.where((self.lane < 2) | (self.lane >= 126), turned, 0.0)
+        return turned * self.ends
 
     def back(self, x, boxes, inv, own, memb=None):
         ws, ms = [], []
@@ -319,14 +319,14 @@
 
 def outer_part(own, xlo, xhi, matrix, cent, edge, box, kept, sums):
     return call(
-        outer_kernel, [((9, 128), F32)], [VMEM] * 9,
+        outer_kernel, [((16, 128), BF16)], [VMEM] * 9,
         [pltpu.VMEM(*columns(4 * W))],
         2 * 10 ** 8, 2 << 20, (own, xlo, xhi, matrix, cent, edge, box, kept, sums))[0]
 
 
 def whole_update(own, ylo, yhi, xlo, xhi, zown, zy, matrix, cent, edge):
     return call(
-        whole_kernel, [((F, W, W, 128), F32), ((9, 128), F32)], [VMEM] * 10,
+        whole_kernel, [((F, W, W, 128), F32), ((16, 128), BF16)], [VMEM] * 10,
         [pltpu.VMEM(*columns(COLS)), pltpu.VMEM(*columns(E * W))],
         8 * 10 ** 8, 3 << 20, (own, ylo, yhi, xlo, xhi, zown, zy, matrix, cent, edge))
 
@@ -339,12 +339,12 @@
 
 def gather_sum(part, axes, count):
     every = lax.all_to_all(jnp.broadcast_to(part[None], (count,) + part.shape), axes, 0, 0)
-    return jnp.sum(every, axis=0)
+    return jnp.sum(every.astype(F32), axis=0)
 
 
 def total_sums(part):
-    part = gather_sum(part.reshape(9, 1, 128), ("core", "gz"), 16)
-    return gather_sum(part, ("cx", "gy"), 16).reshape(9, 128)
+    part = gather_sum(part[:10].reshape(5, 2, 128), ("core", "gz"), 16)
+    return gather_sum(part.reshape(10, 1, 128)[:9], ("cx", "gy"), 16).reshape(9, 128)
 
 
 def edges():

time: 75.9 us -> 74.9 us (0.987)
  no operation moved by 1% of the time
where the time goes in v8:
time: 74.9 us; the launch traced here: 74.6 us
  blocking collectives  41.6 us (56%)
  starting transfers between devices  16.8 us (22%)
  Pallas kernels  7.35 us (10%)
  waiting for transfers between devices  6.79 us (9%)
  other arithmetic  0.9 us (1%)
  between operations  0.75 us (1%)
    all_to_all x4, blocking collectives, gather_sum(): lax.all_to_all(jnp.broadcast_to(part[None], (count,) + part.shape), axes,...  41.6 us
    ppermute x4, starting transfers between devices, both_ways(): hi = lax.ppermute(down, axes, [((i + 1) % count, i) for i in range(count)])  14.3 us
    pallas_call x4, Pallas kernels, call(): pl.pallas_call(kernel, out_shape=tuple((jax.ShapeDtypeStruct(s, t) for s,...  7.35 us
    ppermute x4, waiting for transfers between devices, both_ways(): lo = lax.ppermute(up, axes, [(i, (i + 1) % count) for i in range(count)])  3.75 us
    ppermute x4, waiting for transfers between devices, both_ways(): hi = lax.ppermute(down, axes, [((i + 1) % count, i) for i in range(count)])  3.04 us
    ppermute x4, starting transfers between devices, both_ways(): lo = lax.ppermute(up, axes, [(i, (i + 1) % count) for i in range(count)])  2.5 us
  transfers between devices with their start and end apart: 8, of which 4 were waited for; matrix products, arithmetic and copies ran while one was open for 0% of the time, Pallas kernels for 2%

profile of v8, /device:TPU:1, one launch (start us, length us, event | category | flops | bytes accessed | tf_op | source)
XLA Modules:
  0.0 74.6 jit_solution(307152957242611532)
XLA Ops:
  0.6 1.5 %shard_map.50 = (bf16[64,32,128]{2,1,0:T(8,128)(2,1)S(1)}, bf16[2,32,128]{2,1,0:T(8,128)(2,1)S(1)}, f32[9,128]{1,0:T(8,128)S(1)}) custom-call(bf16[32,8,8,128]{3,2,1,0:T(8,128)(2,1)} %attr_hbm.1, f32[32,32]{1,0:T(8,128)} %start_hbm.1), custom_call_target="tpu_custom_call" | custom-call | flops 1000000 | bytes 1048576 | tf_op jit(solution)/shard_map/pallas_call | solution.py:289
  2.1 6.5 %collective-permute-start.3 = (bf16[2,32,128]{2,1,0:T(8,128)(2,1)S(1)}, bf16[2,32,128]{2,1,0:T(8,128)(2,1)S(1)}, u32[]{:S(2)}, u32[]{:S(2)}) collective-permute-start(bf16[2,32,128]{2,1,0:T(8,128)(2,1)S(1)} %get-tuple-element.11), channel_id=1, source_target_pairs={{1,0},{2,1},{3,2},{4,3},{5,4},{6,5},{7,6},{0,7},{9,8},{10,9},{11,1... | collective-permute-start | bytes 49160 | tf_op jit(solution)/shard_map/ppermute | solution.py:336
  8.6 0.0 collective-permute-start.2
  8.7 1.4 %collective-permute-start = (bf16[16,32,128]{2,1,0:T(8,128)(2,1)S(1)}, bf16[16,32,128]{2,1,0:T(8,128)(2,1)S(1)}, u32[]{:S(2)}, u32[]{:S(2)}) collective-permute-start(bf16[16,32,128]{2,1,0:T(8,128)(2,1)S(1)} %bitcast.18), channel_id=1, source_target_pairs={{0,8},{8,16},{16,24},{24,0},{1,9},{9,17},{17,25},{25,1},{2,10},{10... | collective-permute-start | bytes 393224 | tf_op jit(solution)/shard_map/ppermute | solution.py:335
  10.0 0.0 copy-start
  10.0 1.5 %collective-permute-start.1 = (bf16[16,32,128]{2,1,0:T(8,128)(2,1)S(1)}, bf16[16,32,128]{2,1,0:T(8,128)(2,1)S(1)}, u32[]{:S(2)}, u32[]{:S(2)}) collective-permute-start(bf16[16,32,128]{2,1,0:T(8,128)(2,1)S(1)} %bitcast.17), channel_id=1, source_target_pairs={{8,0},{16,8},{24,16},{0,24},{9,1},{17,9},{25,17},{1,25},{10,2},{18... | collective-permute-start | bytes 393224 | tf_op jit(solution)/shard_map/ppermute | solution.py:336
  11.6 0.0 collective-permute-done.3
  11.6 0.8 %collective-permute-done.2 = bf16[2,32,128]{2,1,0:T(8,128)(2,1)S(1)} collective-permute-done((bf16[2,32,128]{2,1,0:T(8,128)(2,1)S(1)}, bf16[2,32,128]{2,1,0:T(8,128)(2,1)S(1)}, u32[]{:S(2)}, u32[]{:S(2)}) %collective-permute-start.2) | collective-permute-done | bytes 16416 | tf_op jit(solution)/shard_map/ppermute | solution.py:335
  12.4 2.7 %collective-permute-start.5 = (bf16[2,32,128]{2,1,0:T(8,128)(2,1)S(1)}, bf16[2,32,128]{2,1,0:T(8,128)(2,1)S(1)}, u32[]{:S(2)}, u32[]{:S(2)}) collective-permute-start(bf16[2,32,128]{2,1,0:T(8,128)(2,1)S(1)} %broadcast_select_fusion.1.zown), channel_id=1, source_target_pairs={{8,0},{16,8},{24,16},{0,24},{9,1},{17,9},{25,17},{1,25},{10,2},{18... | collective-permute-start | bytes 49160 | tf_op jit(solution)/shard_map/ppermute | solution.py:336
  15.2 0.0 collective-permute-start.4
  15.2 0.9 %collective-permute-done.5 = bf16[2,32,128]{2,1,0:T(8,128)(2,1)S(1)} collective-permute-done((bf16[2,32,128]{2,1,0:T(8,128)(2,1)S(1)}, bf16[2,32,128]{2,1,0:T(8,128)(2,1)S(1)}, u32[]{:S(2)}, u32[]{:S(2)}) %collective-permute-start.5) | collective-permute-done | bytes 16416 | tf_op jit(solution)/shard_map/ppermute | solution.py:336
  16.0 2.9 %collective-permute-done.4 = bf16[2,32,128]{2,1,0:T(8,128)(2,1)S(1)} collective-permute-done((bf16[2,32,128]{2,1,0:T(8,128)(2,1)S(1)}, bf16[2,32,128]{2,1,0:T(8,128)(2,1)S(1)}, u32[]{:S(2)}, u32[]{:S(2)}) %collective-permute-start.4) | collective-permute-done | bytes 16416 | tf_op jit(solution)/shard_map/ppermute | solution.py:335
  19.0 0.0 collective-permute-done.ylo
  19.0 0.0 collective-permute-done.1.yhi
  19.1 3.5 %collective-permute-start.7 = (bf16[26,32,128]{2,1,0:T(8,128)(2,1)S(1)}, bf16[26,32,128]{2,1,0:T(8,128)(2,1)S(1)}, u32[]{:S(2)}, u32[]{:S(2)}) collective-permute-start(bf16[26,32,128]{2,1,0:T(8,128)(2,1)S(1)} %get-tuple-element.26), channel_id=1, source_target_pairs={{32,0},{64,32},{96,64},{128,96},{160,128},{192,160},{224,192},{0,2... | collective-permute-start | bytes 638984 | tf_op jit(solution)/shard_map/ppermute | solution.py:336
  22.6 1.1 %collective-permute-start.6 = (bf16[26,32,128]{2,1,0:T(8,128)(2,1)S(1)}, bf16[26,32,128]{2,1,0:T(8,128)(2,1)S(1)}, u32[]{:S(2)}, u32[]{:S(2)}) collective-permute-start(bf16[26,32,128]{2,1,0:T(8,128)(2,1)S(1)} %get-tuple-element.27), channel_id=1, source_target_pairs={{0,32},{32,64},{64,96},{96,128},{128,160},{160,192},{192,224},{224... | collective-permute-start | bytes 638984 | tf_op jit(solution)/shard_map/ppermute | solution.py:335
  23.7 0.1 iota.35.edge
  23.8 0.0 copy-done
  23.8 1.5 %shard_map.51 = (f32[32,32,128]{2,1,0:T(8,128)S(1)}, f32[32,32,128]{2,1,0:T(8,128)S(1)}, f32[40,32]{1,0:T(8,128)S(1)}) custom-call(bf16[64,32,128]{2,1,0:T(8,128)(2,1)S(1)} %get-tuple-element.10.own, bf16[16,32,128]{2,1,0:T(8,128)(2,1)S(1)} %collective-permute-done.ylo, bf16[16,32,128]{2,1,0:T(8,128)(2,1)S(1)} %collective-permute-done.1.yhi, ...), custom_call_target="tpu_custom_call" | custom-call | flops 500000000 | bytes 3145728 | tf_op jit(solution)/shard_map/pallas_call | solution.py:289
  25.4 2.2 %collective-permute-done.7.xhi = bf16[26,32,128]{2,1,0:T(8,128)(2,1)S(1)} collective-permute-done((bf16[26,32,128]{2,1,0:T(8,128)(2,1)S(1)}, bf16[26,32,128]{2,1,0:T(8,128)(2,1)S(1)}, u32[]{:S(2)}, u32[]{:S(2)}) %collective-permute-start.7) | collective-permute-done | bytes 213024 | tf_op jit(solution)/shard_map/ppermute | solution.py:336
  27.5 0.0 collective-permute-done.6.xlo
  27.5 1.1 %shard_map.52 = bf16[16,128]{1,0:T(8,128)(2,1)S(1)} custom-call(bf16[64,32,128]{2,1,0:T(8,128)(2,1)S(1)} %get-tuple-element.10.own, bf16[26,32,128]{2,1,0:T(8,128)(2,1)S(1)} %collective-permute-done.6.xlo, bf16[26,32,128]{2,1,0:T(8,128)(2,1)S(1)} %collective-permute-done.7.xhi, bf16[768,256]{1,0:T(8,128)(2,1)S(1)} %copy-done, ...), custom_call_target="tpu_custom_call" | custom-call | flops 200000000 | bytes 2097152 | tf_op jit(solution)/shard_map/pallas_call | solution.py:289
  28.7 11.2 %all_to_all.20 = bf16[16,5,2,128]{3,2,1,0:T(2,128)(2,1)S(1)} all-to-all(bf16[16,5,2,128]{3,2,1,0:T(2,128)(2,1)S(1)} %broadcast_in_dim.46), channel_id=1, replica_groups=mesh['cx'=4,'core'=2,'gy'=4,'gz'=8] {'core','gz'}, dimensions={0} | all-to-all | bytes 81920 | tf_op jit(solution)/shard_map/all_to_all | solution.py:341
  40.0 9.3 %all_to_all.21 = f32[16,9,1,128]{3,2,1,0:T(1,128)S(1)} all-to-all(f32[16,9,1,128]{3,2,1,0:T(1,128)S(1)} %broadcast_in_dim.48), channel_id=1, replica_groups=mesh['cx'=4,'core'=2,'gy'=4,'gz'=8] {'cx','gy'}, dimensions={0} | all-to-all | bytes 147456 | tf_op jit(solution)/shard_map/all_to_all | solution.py:341
  49.2 0.1 reduce_sum.37.cent
  49.3 3.2 %shard_map.53 = (f32[32,8,8,128]{3,2,1,0:T(8,128)}, bf16[16,128]{1,0:T(8,128)(2,1)S(1)}) custom-call(bf16[64,32,128]{2,1,0:T(8,128)(2,1)S(1)} %get-tuple-element.10.own, bf16[16,32,128]{2,1,0:T(8,128)(2,1)S(1)} %collective-permute-done.ylo, bf16[16,32,128]{2,1,0:T(8,128)(2,1)S(1)} %collective-permute-done.1.yhi, ...), custom_call_target="tpu_custom_call" | custom-call | flops 800000000 | bytes 3145728 | tf_op jit(solution)/shard_map/pallas_call | solution.py:289
  52.5 11.6 %all_to_all.22 = bf16[16,5,2,128]{3,2,1,0:T(2,128)(2,1)S(1)} all-to-all(bf16[16,5,2,128]{3,2,1,0:T(2,128)(2,1)S(1)} %broadcast_in_dim.50), channel_id=1, replica_groups=mesh['cx'=4,'core'=2,'gy'=4,'gz'=8] {'core','gz'}, dimensions={0} | all-to-all | bytes 81920 | tf_op jit(solution)/shard_map/all_to_all | solution.py:341
  64.3 9.5 %all_to_all.23 = f32[16,9,1,128]{3,2,1,0:T(1,128)S(1)} all-to-all(f32[16,9,1,128]{3,2,1,0:T(1,128)S(1)} %broadcast_in_dim.52), channel_id=1, replica_groups=mesh['cx'=4,'core'=2,'gy'=4,'gz'=8] {'cx','gy'}, dimensions={0} | all-to-all | bytes 147456 | tf_op jit(solution)/shard_map/all_to_all | solution.py:341
  73.8 0.1 reduce_sum.39
  73.9 0.1 reshape.122
  73.9 0.7 bitcast_divide_fusion
  (25 shorter events, 0.4 us)
Async XLA Ops:
  2.1 9.5 %collective-permute-start.3 = (bf16[2,32,128]{2,1,0:T(8,128)(2,1)S(1)}, bf16[2,32,128]{2,1,0:T(8,128)(2,1)S(1)}, u32[]{:S(2)}, u32[]{:S(2)}) collective-permute-start(bf16[2,32,128]{2,1,0:T(8,128)(2,1)S(1)} %get-tuple-element.11), channel_id=1, source_target_pairs={{1,0},{2,1},{3,2},{4,3},{5,4},{6,5},{7,6},{0,7},{9,8},{10,9},{11,1... | collective-permute-start | bytes 49160 | tf_op jit(solution)/shard_map/ppermute | solution.py:336
  8.6 3.8 %collective-permute-start.2 = (bf16[2,32,128]{2,1,0:T(8,128)(2,1)S(1)}, bf16[2,32,128]{2,1,0:T(8,128)(2,1)S(1)}, u32[]{:S(2)}, u32[]{:S(2)}) collective-permute-start(bf16[2,32,128]{2,1,0:T(8,128)(2,1)S(1)} %get-tuple-element.11), channel_id=1, source_target_pairs={{0,1},{1,2},{2,3},{3,4},{4,5},{5,6},{6,7},{7,0},{8,9},{9,10},{10,1... | collective-permute-start | bytes 49160 | tf_op jit(solution)/shard_map/ppermute | solution.py:335
  8.7 10.3 %collective-permute-start = (bf16[16,32,128]{2,1,0:T(8,128)(2,1)S(1)}, bf16[16,32,128]{2,1,0:T(8,128)(2,1)S(1)}, u32[]{:S(2)}, u32[]{:S(2)}) collective-permute-start(bf16[16,32,128]{2,1,0:T(8,128)(2,1)S(1)} %bitcast.18), channel_id=1, source_target_pairs={{0,8},{8,16},{16,24},{24,0},{1,9},{9,17},{17,25},{25,1},{2,10},{10... | collective-permute-start | bytes 393224 | tf_op jit(solution)/shard_map/ppermute | solution.py:335
  10.0 13.8 %copy-start = (bf16[768,256]{1,0:T(8,128)(2,1)S(1)}, bf16[768,256]{1,0:T(8,128)(2,1)}, u32[]{:S(2)}) copy-start(bf16[768,256]{1,0:T(8,128)(2,1)} %constant.77.clone.matrix) | copy-start | bytes 1179652
  10.0 9.0 %collective-permute-start.1 = (bf16[16,32,128]{2,1,0:T(8,128)(2,1)S(1)}, bf16[16,32,128]{2,1,0:T(8,128)(2,1)S(1)}, u32[]{:S(2)}, u32[]{:S(2)}) collective-permute-start(bf16[16,32,128]{2,1,0:T(8,128)(2,1)S(1)} %bitcast.17), channel_id=1, source_target_pairs={{8,0},{16,8},{24,16},{0,24},{9,1},{17,9},{25,17},{1,25},{10,2},{18... | collective-permute-start | bytes 393224 | tf_op jit(solution)/shard_map/ppermute | solution.py:336
  12.4 3.6 %collective-permute-start.5 = (bf16[2,32,128]{2,1,0:T(8,128)(2,1)S(1)}, bf16[2,32,128]{2,1,0:T(8,128)(2,1)S(1)}, u32[]{:S(2)}, u32[]{:S(2)}) collective-permute-start(bf16[2,32,128]{2,1,0:T(8,128)(2,1)S(1)} %broadcast_select_fusion.1.zown), channel_id=1, source_target_pairs={{8,0},{16,8},{24,16},{0,24},{9,1},{17,9},{25,17},{1,25},{10,2},{18... | collective-permute-start | bytes 49160 | tf_op jit(solution)/shard_map/ppermute | solution.py:336
  15.2 3.8 %collective-permute-start.4 = (bf16[2,32,128]{2,1,0:T(8,128)(2,1)S(1)}, bf16[2,32,128]{2,1,0:T(8,128)(2,1)S(1)}, u32[]{:S(2)}, u32[]{:S(2)}) collective-permute-start(bf16[2,32,128]{2,1,0:T(8,128)(2,1)S(1)} %broadcast_select_fusion.1.zown), channel_id=1, source_target_pairs={{0,8},{8,16},{16,24},{24,0},{1,9},{9,17},{17,25},{25,1},{2,10},{10... | collective-permute-start | bytes 49160 | tf_op jit(solution)/shard_map/ppermute | solution.py:335
  19.1 8.5 %collective-permute-start.7 = (bf16[26,32,128]{2,1,0:T(8,128)(2,1)S(1)}, bf16[26,32,128]{2,1,0:T(8,128)(2,1)S(1)}, u32[]{:S(2)}, u32[]{:S(2)}) collective-permute-start(bf16[26,32,128]{2,1,0:T(8,128)(2,1)S(1)} %get-tuple-element.26), channel_id=1, source_target_pairs={{32,0},{64,32},{96,64},{128,96},{160,128},{192,160},{224,192},{0,2... | collective-permute-start | bytes 638984 | tf_op jit(solution)/shard_map/ppermute | solution.py:336
  22.6 4.9 %collective-permute-start.6 = (bf16[26,32,128]{2,1,0:T(8,128)(2,1)S(1)}, bf16[26,32,128]{2,1,0:T(8,128)(2,1)S(1)}, u32[]{:S(2)}, u32[]{:S(2)}) collective-permute-start(bf16[26,32,128]{2,1,0:T(8,128)(2,1)S(1)} %get-tuple-element.27), channel_id=1, source_target_pairs={{0,32},{32,64},{64,96},{96,128},{128,160},{160,192},{192,224},{224... | collective-permute-start | bytes 638984 | tf_op jit(solution)/shard_map/ppermute | solution.py:335

commit v9 on v8

--- a/solution.py
+++ b/solution.py
@@ -344,7 +344,7 @@
 
 def total_sums(part):
     part = gather_sum(part[:10].reshape(5, 2, 128), ("core", "gz"), 16)
-    return gather_sum(part.reshape(10, 1, 128)[:9], ("cx", "gy"), 16).reshape(9, 128)
+    return gather_sum(part.reshape(10, 1, 128)[:9], ("gy", "cx"), 16).reshape(9, 128)
 
 
 def edges():

time: 74.9 us -> 74.8 us (level)
  no operation moved by 1% of the time
where the time goes in v9:
time: 74.8 us; the launch traced here: 74.5 us
  blocking collectives  41.5 us (55%)
  starting transfers between devices  16.8 us (22%)
  Pallas kernels  7.35 us (10%)
  waiting for transfers between devices  6.79 us (9%)
  other arithmetic  0.9 us (1%)
  between operations  0.75 us (1%)
    all_to_all x4, blocking collectives, gather_sum(): lax.all_to_all(jnp.broadcast_to(part[None], (count,) + part.shape), axes,...  41.5 us
    ppermute x4, starting transfers between devices, both_ways(): hi = lax.ppermute(down, axes, [((i + 1) % count, i) for i in range(count)])  14.3 us
    pallas_call x4, Pallas kernels, call(): pl.pallas_call(kernel, out_shape=tuple((jax.ShapeDtypeStruct(s, t) for s,...  7.35 us
    ppermute x4, waiting for transfers between devices, both_ways(): lo = lax.ppermute(up, axes, [(i, (i + 1) % count) for i in range(count)])  3.75 us
    ppermute x4, waiting for transfers between devices, both_ways(): hi = lax.ppermute(down, axes, [((i + 1) % count, i) for i in range(count)])  3.04 us
    ppermute x4, starting transfers between devices, both_ways(): lo = lax.ppermute(up, axes, [(i, (i + 1) % count) for i in range(count)])  2.5 us
  transfers between devices with their start and end apart: 8, of which 4 were waited for; matrix products, arithmetic and copies ran while one was open for 0% of the time, Pallas kernels for 2%

profile of v9, /device:TPU:1, one launch (start us, length us, event | category | flops | bytes accessed | tf_op | source)
XLA Modules:
  0.0 74.5 jit_solution(12772828416130446793)
XLA Ops:
  0.6 1.5 %shard_map.50 = (bf16[64,32,128]{2,1,0:T(8,128)(2,1)S(1)}, bf16[2,32,128]{2,1,0:T(8,128)(2,1)S(1)}, f32[9,128]{1,0:T(8,128)S(1)}) custom-call(bf16[32,8,8,128]{3,2,1,0:T(8,128)(2,1)} %attr_hbm.1, f32[32,32]{1,0:T(8,128)} %start_hbm.1), custom_call_target="tpu_custom_call" | custom-call | flops 1000000 | bytes 1048576 | tf_op jit(solution)/shard_map/pallas_call | solution.py:289
  2.1 6.5 %collective-permute-start.3 = (bf16[2,32,128]{2,1,0:T(8,128)(2,1)S(1)}, bf16[2,32,128]{2,1,0:T(8,128)(2,1)S(1)}, u32[]{:S(2)}, u32[]{:S(2)}) collective-permute-start(bf16[2,32,128]{2,1,0:T(8,128)(2,1)S(1)} %get-tuple-element.11), channel_id=1, source_target_pairs={{1,0},{2,1},{3,2},{4,3},{5,4},{6,5},{7,6},{0,7},{9,8},{10,9},{11,1... | collective-permute-start | bytes 49160 | tf_op jit(solution)/shard_map/ppermute | solution.py:336
  8.6 0.0 collective-permute-start.2
  8.7 1.4 %collective-permute-start = (bf16[16,32,128]{2,1,0:T(8,128)(2,1)S(1)}, bf16[16,32,128]{2,1,0:T(8,128)(2,1)S(1)}, u32[]{:S(2)}, u32[]{:S(2)}) collective-permute-start(bf16[16,32,128]{2,1,0:T(8,128)(2,1)S(1)} %bitcast.18), channel_id=1, source_target_pairs={{0,8},{8,16},{16,24},{24,0},{1,9},{9,17},{17,25},{25,1},{2,10},{10... | collective-permute-start | bytes 393224 | tf_op jit(solution)/shard_map/ppermute | solution.py:335
  10.0 0.0 copy-start
  10.0 1.5 %collective-permute-start.1 = (bf16[16,32,128]{2,1,0:T(8,128)(2,1)S(1)}, bf16[16,32,128]{2,1,0:T(8,128)(2,1)S(1)}, u32[]{:S(2)}, u32[]{:S(2)}) collective-permute-start(bf16[16,32,128]{2,1,0:T(8,128)(2,1)S(1)} %bitcast.17), channel_id=1, source_target_pairs={{8,0},{16,8},{24,16},{0,24},{9,1},{17,9},{25,17},{1,25},{10,2},{18... | collective-permute-start | bytes 393224 | tf_op jit(solution)/shard_map/ppermute | solution.py:336
  11.6 0.0 collective-permute-done.3
  11.6 0.8 %collective-permute-done.2 = bf16[2,32,128]{2,1,0:T(8,128)(2,1)S(1)} collective-permute-done((bf16[2,32,128]{2,1,0:T(8,128)(2,1)S(1)}, bf16[2,32,128]{2,1,0:T(8,128)(2,1)S(1)}, u32[]{:S(2)}, u32[]{:S(2)}) %collective-permute-start.2) | collective-permute-done | bytes 16416 | tf_op jit(solution)/shard_map/ppermute | solution.py:335
  12.4 2.7 %collective-permute-start.5 = (bf16[2,32,128]{2,1,0:T(8,128)(2,1)S(1)}, bf16[2,32,128]{2,1,0:T(8,128)(2,1)S(1)}, u32[]{:S(2)}, u32[]{:S(2)}) collective-permute-start(bf16[2,32,128]{2,1,0:T(8,128)(2,1)S(1)} %broadcast_select_fusion.1.zown), channel_id=1, source_target_pairs={{8,0},{16,8},{24,16},{0,24},{9,1},{17,9},{25,17},{1,25},{10,2},{18... | collective-permute-start | bytes 49160 | tf_op jit(solution)/shard_map/ppermute | solution.py:336
  15.2 0.0 collective-permute-start.4
  15.2 0.9 %collective-permute-done.5 = bf16[2,32,128]{2,1,0:T(8,128)(2,1)S(1)} collective-permute-done((bf16[2,32,128]{2,1,0:T(8,128)(2,1)S(1)}, bf16[2,32,128]{2,1,0:T(8,128)(2,1)S(1)}, u32[]{:S(2)}, u32[]{:S(2)}) %collective-permute-start.5) | collective-permute-done | bytes 16416 | tf_op jit(solution)/shard_map/ppermute | solution.py:336
  16.0 2.9 %collective-permute-done.4 = bf16[2,32,128]{2,1,0:T(8,128)(2,1)S(1)} collective-permute-done((bf16[2,32,128]{2,1,0:T(8,128)(2,1)S(1)}, bf16[2,32,128]{2,1,0:T(8,128)(2,1)S(1)}, u32[]{:S(2)}, u32[]{:S(2)}) %collective-permute-start.4) | collective-permute-done | bytes 16416 | tf_op jit(solution)/shard_map/ppermute | solution.py:335
  19.0 0.0 collective-permute-done.ylo
  19.0 0.0 collective-permute-done.1.yhi
  19.1 3.5 %collective-permute-start.7 = (bf16[26,32,128]{2,1,0:T(8,128)(2,1)S(1)}, bf16[26,32,128]{2,1,0:T(8,128)(2,1)S(1)}, u32[]{:S(2)}, u32[]{:S(2)}) collective-permute-start(bf16[26,32,128]{2,1,0:T(8,128)(2,1)S(1)} %get-tuple-element.26), channel_id=1, source_target_pairs={{32,0},{64,32},{96,64},{128,96},{160,128},{192,160},{224,192},{0,2... | collective-permute-start | bytes 638984 | tf_op jit(solution)/shard_map/ppermute | solution.py:336
  22.6 1.1 %collective-permute-start.6 = (bf16[26,32,128]{2,1,0:T(8,128)(2,1)S(1)}, bf16[26,32,128]{2,1,0:T(8,128)(2,1)S(1)}, u32[]{:S(2)}, u32[]{:S(2)}) collective-permute-start(bf16[26,32,128]{2,1,0:T(8,128)(2,1)S(1)} %get-tuple-element.27), channel_id=1, source_target_pairs={{0,32},{32,64},{64,96},{96,128},{128,160},{160,192},{192,224},{224... | collective-permute-start | bytes 638984 | tf_op jit(solution)/shard_map/ppermute | solution.py:335
  23.7 0.1 iota.35.edge
  23.8 0.0 copy-done
  23.8 1.5 %shard_map.51 = (f32[32,32,128]{2,1,0:T(8,128)S(1)}, f32[32,32,128]{2,1,0:T(8,128)S(1)}, f32[40,32]{1,0:T(8,128)S(1)}) custom-call(bf16[64,32,128]{2,1,0:T(8,128)(2,1)S(1)} %get-tuple-element.10.own, bf16[16,32,128]{2,1,0:T(8,128)(2,1)S(1)} %collective-permute-done.ylo, bf16[16,32,128]{2,1,0:T(8,128)(2,1)S(1)} %collective-permute-done.1.yhi, ...), custom_call_target="tpu_custom_call" | custom-call | flops 500000000 | bytes 3145728 | tf_op jit(solution)/shard_map/pallas_call | solution.py:289
  25.4 2.2 %collective-permute-done.7.xhi = bf16[26,32,128]{2,1,0:T(8,128)(2,1)S(1)} collective-permute-done((bf16[26,32,128]{2,1,0:T(8,128)(2,1)S(1)}, bf16[26,32,128]{2,1,0:T(8,128)(2,1)S(1)}, u32[]{:S(2)}, u32[]{:S(2)}) %collective-permute-start.7) | collective-permute-done | bytes 213024 | tf_op jit(solution)/shard_map/ppermute | solution.py:336
  27.5 0.0 collective-permute-done.6.xlo
  27.5 1.1 %shard_map.52 = bf16[16,128]{1,0:T(8,128)(2,1)S(1)} custom-call(bf16[64,32,128]{2,1,0:T(8,128)(2,1)S(1)} %get-tuple-element.10.own, bf16[26,32,128]{2,1,0:T(8,128)(2,1)S(1)} %collective-permute-done.6.xlo, bf16[26,32,128]{2,1,0:T(8,128)(2,1)S(1)} %collective-permute-done.7.xhi, bf16[768,256]{1,0:T(8,128)(2,1)S(1)} %copy-done, ...), custom_call_target="tpu_custom_call" | custom-call | flops 200000000 | bytes 2097152 | tf_op jit(solution)/shard_map/pallas_call | solution.py:289
  28.7 11.2 %all_to_all.20 = bf16[16,5,2,128]{3,2,1,0:T(2,128)(2,1)S(1)} all-to-all(bf16[16,5,2,128]{3,2,1,0:T(2,128)(2,1)S(1)} %broadcast_in_dim.46), channel_id=1, replica_groups=mesh['cx'=4,'core'=2,'gy'=4,'gz'=8] {'core','gz'}, dimensions={0} | all-to-all | bytes 81920 | tf_op jit(solution)/shard_map/all_to_all | solution.py:341
  40.0 9.2 %all_to_all.21 = f32[16,9,1,128]{3,2,1,0:T(1,128)S(1)} all-to-all(f32[16,9,1,128]{3,2,1,0:T(1,128)S(1)} %broadcast_in_dim.48), channel_id=1, replica_groups=mesh['cx'=4,'core'=2,'gy'=4,'gz'=8] {'gy','cx'}, dimensions={0} | all-to-all | bytes 147456 | tf_op jit(solution)/shard_map/all_to_all | solution.py:341
  49.2 0.1 reduce_sum.37.cent
  49.3 3.2 %shard_map.53 = (f32[32,8,8,128]{3,2,1,0:T(8,128)}, bf16[16,128]{1,0:T(8,128)(2,1)S(1)}) custom-call(bf16[64,32,128]{2,1,0:T(8,128)(2,1)S(1)} %get-tuple-element.10.own, bf16[16,32,128]{2,1,0:T(8,128)(2,1)S(1)} %collective-permute-done.ylo, bf16[16,32,128]{2,1,0:T(8,128)(2,1)S(1)} %collective-permute-done.1.yhi, ...), custom_call_target="tpu_custom_call" | custom-call | flops 800000000 | bytes 3145728 | tf_op jit(solution)/shard_map/pallas_call | solution.py:289
  52.5 11.6 %all_to_all.22 = bf16[16,5,2,128]{3,2,1,0:T(2,128)(2,1)S(1)} all-to-all(bf16[16,5,2,128]{3,2,1,0:T(2,128)(2,1)S(1)} %broadcast_in_dim.50), channel_id=1, replica_groups=mesh['cx'=4,'core'=2,'gy'=4,'gz'=8] {'core','gz'}, dimensions={0} | all-to-all | bytes 81920 | tf_op jit(solution)/shard_map/all_to_all | solution.py:341
  64.3 9.4 %all_to_all.23 = f32[16,9,1,128]{3,2,1,0:T(1,128)S(1)} all-to-all(f32[16,9,1,128]{3,2,1,0:T(1,128)S(1)} %broadcast_in_dim.52), channel_id=1, replica_groups=mesh['cx'=4,'core'=2,'gy'=4,'gz'=8] {'gy','cx'}, dimensions={0} | all-to-all | bytes 147456 | tf_op jit(solution)/shard_map/all_to_all | solution.py:341
  73.7 0.1 reduce_sum.39
  73.7 0.1 reshape.122
  73.8 0.7 bitcast_divide_fusion
  (25 shorter events, 0.4 us)
Async XLA Ops:
  2.1 9.5 %collective-permute-start.3 = (bf16[2,32,128]{2,1,0:T(8,128)(2,1)S(1)}, bf16[2,32,128]{2,1,0:T(8,128)(2,1)S(1)}, u32[]{:S(2)}, u32[]{:S(2)}) collective-permute-start(bf16[2,32,128]{2,1,0:T(8,128)(2,1)S(1)} %get-tuple-element.11), channel_id=1, source_target_pairs={{1,0},{2,1},{3,2},{4,3},{5,4},{6,5},{7,6},{0,7},{9,8},{10,9},{11,1... | collective-permute-start | bytes 49160 | tf_op jit(solution)/shard_map/ppermute | solution.py:336
  8.6 3.8 %collective-permute-start.2 = (bf16[2,32,128]{2,1,0:T(8,128)(2,1)S(1)}, bf16[2,32,128]{2,1,0:T(8,128)(2,1)S(1)}, u32[]{:S(2)}, u32[]{:S(2)}) collective-permute-start(bf16[2,32,128]{2,1,0:T(8,128)(2,1)S(1)} %get-tuple-element.11), channel_id=1, source_target_pairs={{0,1},{1,2},{2,3},{3,4},{4,5},{5,6},{6,7},{7,0},{8,9},{9,10},{10,1... | collective-permute-start | bytes 49160 | tf_op jit(solution)/shard_map/ppermute | solution.py:335
  8.7 10.3 %collective-permute-start = (bf16[16,32,128]{2,1,0:T(8,128)(2,1)S(1)}, bf16[16,32,128]{2,1,0:T(8,128)(2,1)S(1)}, u32[]{:S(2)}, u32[]{:S(2)}) collective-permute-start(bf16[16,32,128]{2,1,0:T(8,128)(2,1)S(1)} %bitcast.18), channel_id=1, source_target_pairs={{0,8},{8,16},{16,24},{24,0},{1,9},{9,17},{17,25},{25,1},{2,10},{10... | collective-permute-start | bytes 393224 | tf_op jit(solution)/shard_map/ppermute | solution.py:335
  10.0 13.8 %copy-start = (bf16[768,256]{1,0:T(8,128)(2,1)S(1)}, bf16[768,256]{1,0:T(8,128)(2,1)}, u32[]{:S(2)}) copy-start(bf16[768,256]{1,0:T(8,128)(2,1)} %constant.77.clone.matrix) | copy-start | bytes 1179652
  10.0 9.0 %collective-permute-start.1 = (bf16[16,32,128]{2,1,0:T(8,128)(2,1)S(1)}, bf16[16,32,128]{2,1,0:T(8,128)(2,1)S(1)}, u32[]{:S(2)}, u32[]{:S(2)}) collective-permute-start(bf16[16,32,128]{2,1,0:T(8,128)(2,1)S(1)} %bitcast.17), channel_id=1, source_target_pairs={{8,0},{16,8},{24,16},{0,24},{9,1},{17,9},{25,17},{1,25},{10,2},{18... | collective-permute-start | bytes 393224 | tf_op jit(solution)/shard_map/ppermute | solution.py:336
  12.4 3.6 %collective-permute-start.5 = (bf16[2,32,128]{2,1,0:T(8,128)(2,1)S(1)}, bf16[2,32,128]{2,1,0:T(8,128)(2,1)S(1)}, u32[]{:S(2)}, u32[]{:S(2)}) collective-permute-start(bf16[2,32,128]{2,1,0:T(8,128)(2,1)S(1)} %broadcast_select_fusion.1.zown), channel_id=1, source_target_pairs={{8,0},{16,8},{24,16},{0,24},{9,1},{17,9},{25,17},{1,25},{10,2},{18... | collective-permute-start | bytes 49160 | tf_op jit(solution)/shard_map/ppermute | solution.py:336
  15.2 3.8 %collective-permute-start.4 = (bf16[2,32,128]{2,1,0:T(8,128)(2,1)S(1)}, bf16[2,32,128]{2,1,0:T(8,128)(2,1)S(1)}, u32[]{:S(2)}, u32[]{:S(2)}) collective-permute-start(bf16[2,32,128]{2,1,0:T(8,128)(2,1)S(1)} %broadcast_select_fusion.1.zown), channel_id=1, source_target_pairs={{0,8},{8,16},{16,24},{24,0},{1,9},{9,17},{17,25},{25,1},{2,10},{10... | collective-permute-start | bytes 49160 | tf_op jit(solution)/shard_map/ppermute | solution.py:335
  19.1 8.5 %collective-permute-start.7 = (bf16[26,32,128]{2,1,0:T(8,128)(2,1)S(1)}, bf16[26,32,128]{2,1,0:T(8,128)(2,1)S(1)}, u32[]{:S(2)}, u32[]{:S(2)}) collective-permute-start(bf16[26,32,128]{2,1,0:T(8,128)(2,1)S(1)} %get-tuple-element.26), channel_id=1, source_target_pairs={{32,0},{64,32},{96,64},{128,96},{160,128},{192,160},{224,192},{0,2... | collective-permute-start | bytes 638984 | tf_op jit(solution)/shard_map/ppermute | solution.py:336
  22.6 4.9 %collective-permute-start.6 = (bf16[26,32,128]{2,1,0:T(8,128)(2,1)S(1)}, bf16[26,32,128]{2,1,0:T(8,128)(2,1)S(1)}, u32[]{:S(2)}, u32[]{:S(2)}) collective-permute-start(bf16[26,32,128]{2,1,0:T(8,128)(2,1)S(1)} %get-tuple-element.27), channel_id=1, source_target_pairs={{0,32},{32,64},{64,96},{96,128},{128,160},{160,192},{192,224},{224... | collective-permute-start | bytes 638984 | tf_op jit(solution)/shard_map/ppermute | solution.py:335

commit v10 on v8

--- a/solution.py
+++ b/solution.py
@@ -61,7 +61,9 @@
 
 def store_sums(part, numer, denom):
     packed = jnp.concatenate([numer[8 * g:8 * g + 8] for g in range(4)], axis=1)
-    part[...] = jnp.concatenate([packed, jnp.concatenate([denom] * 4, axis=1)], axis=0).astype(BF16)
+    every = jnp.concatenate([packed, jnp.concatenate([denom] * 4, axis=1)], axis=0)
+    for i in range(5):
+        part[i] = every[2 * i:2 * i + 2].astype(BF16)
 
 
 def turned8(v):
@@ -77,7 +79,7 @@
     return v
 
 
-def prepare_kernel(attr_hbm, start_hbm, own, ends, cent, attr, start, sems):
+def prepare_kernel(attr_hbm, start_hbm, own, up, down, ends, cent, attr, start, sems):
     fetch = [
         pltpu.make_async_copy(attr_hbm.at[:, x:x + 4], attr.at[:, x:x + 4], sems.at[x // 4])
         for x in range(0, W, 4)
@@ -97,6 +99,10 @@
                 j = c % 32
                 col = jnp.concatenate([groups[g][y] for g in range(4)], axis=0)
                 own[c] = col.astype(BF16)
+                if y < 2:
+                    down[x * 2 + y] = col.astype(BF16)
+                elif y >= W - 2:
+                    up[x * 2 + y - W + 2] = col.astype(BF16)
                 acc = jnp.where(lane == j, pltpu.roll(col, (4 * j + 2) % 128, 1), acc)
         ends[half] = acc.astype(BF16)
     fetch[-1].wait()
@@ -303,7 +309,7 @@
 
 def prepare(attributes, start):
     return call(
-        prepare_kernel, [columns(COLS, BF16), columns(2, BF16), ((9, 128), F32)], [ANY] * 2,
+        prepare_kernel, [columns(COLS, BF16), columns(2 * W, BF16), columns(2 * W, BF16), columns(2, BF16), ((9, 128), F32)], [ANY] * 2,
         [pltpu.VMEM(attributes.shape, BF16), pltpu.VMEM(start.shape, F32),
          pltpu.SemaphoreType.DMA((3,))],
         10 ** 6, 1 << 20,
@@ -319,14 +325,14 @@
 
 def outer_part(own, xlo, xhi, matrix, cent, edge, box, kept, sums):
     return call(
-        outer_kernel, [((16, 128), BF16)], [VMEM] * 9,
+        outer_kernel, [((5, 2, 128), BF16)], [VMEM] * 9,
         [pltpu.VMEM(*columns(4 * W))],
         2 * 10 ** 8, 2 << 20, (own, xlo, xhi, matrix, cent, edge, box, kept, sums))[0]
 
 
 def whole_update(own, ylo, yhi, xlo, xhi, zown, zy, matrix, cent, edge):
     return call(
-        whole_kernel, [((F, W, W, 128), F32), ((16, 128), BF16)], [VMEM] * 10,
+        whole_kernel, [((F, W, W, 128), F32), ((5, 2, 128), BF16)], [VMEM] * 10,
         [pltpu.VMEM(*columns(COLS)), pltpu.VMEM(*columns(E * W))],
         8 * 10 ** 8, 3 << 20, (own, ylo, yhi, xlo, xhi, zown, zy, matrix, cent, edge))
 
@@ -343,7 +349,7 @@
 
 
 def total_sums(part):
-    part = gather_sum(part[:10].reshape(5, 2, 128), ("core", "gz"), 16)
+    part = gather_sum(part, ("core", "gz"), 16)
     return gather_sum(part.reshape(10, 1, 128)[:9], ("cx", "gy"), 16).reshape(9, 128)
 
 
@@ -360,10 +366,8 @@
     edge = edges()
     matrix = jnp.asarray(halo_matrix(), BF16)
     lane = lax.broadcasted_iota(jnp.int32, (1, 1, 128), 2)
-    own, ends, cent = prepare(attributes, start_centroids)
-    grid = own.reshape(W, W, F, 128)
-    ylo, yhi = both_ways(
-        grid[:, W - 2:].reshape(2 * W, F, 128), grid[:, :2].reshape(2 * W, F, 128), "gy", 4)
+    own, up, down, ends, cent = prepare(attributes, start_centroids)
+    ylo, yhi = both_ways(up, down, "gy", 4)
     zlo, zhi = both_ways(ends, ends, "gz", 8)
     zown = jnp.where(lane % 4 < 2, zlo, zhi)
     zylo, zyhi = both_ways(zown, zown, "gy", 4)

time: 74.9 us -> 74.8 us (level)
  no operation moved by 1% of the time
where the time goes in v10:
time: 74.8 us; the launch traced here: 74.6 us
  blocking collectives  41.6 us (56%)
  starting transfers between devices  16.6 us (22%)
  Pallas kernels  7.34 us (10%)
  waiting for transfers between devices  6.99 us (9%)
  other arithmetic  0.9 us (1%)
  between operations  0.75 us (1%)
    all_to_all x4, blocking collectives, gather_sum(): lax.all_to_all(jnp.broadcast_to(part[None], (count,) + part.shape), axes,...  41.6 us
    ppermute x4, starting transfers between devices, both_ways(): hi = lax.ppermute(down, axes, [((i + 1) % count, i) for i in range(count)])  14.2 us
    pallas_call x4, Pallas kernels, call(): pl.pallas_call(kernel, out_shape=tuple((jax.ShapeDtypeStruct(s, t) for s,...  7.34 us
    ppermute x4, waiting for transfers between devices, both_ways(): lo = lax.ppermute(up, axes, [(i, (i + 1) % count) for i in range(count)])  3.95 us
    ppermute x4, waiting for transfers between devices, both_ways(): hi = lax.ppermute(down, axes, [((i + 1) % count, i) for i in range(count)])  3.04 us
    ppermute x4, starting transfers between devices, both_ways(): lo = lax.ppermute(up, axes, [(i, (i + 1) % count) for i in range(count)])  2.42 us
  transfers between devices with their start and end apart: 8, of which 4 were waited for; matrix products, arithmetic and copies ran while one was open for 0% of the time, Pallas kernels for 2%

profile of v10, /device:TPU:1, one launch (start us, length us, event | category | flops | bytes accessed | tf_op | source)
XLA Modules:
  0.0 74.6 jit_solution(13395497259406417087)
XLA Ops:
  0.6 1.5 %shard_map.50 = (bf16[64,32,128]{2,1,0:T(8,128)(2,1)S(1)}, bf16[16,32,128]{2,1,0:T(8,128)(2,1)S(1)}, bf16[16,32,128]{2,1,0:T(8,128)(2,1)S(1)}, bf16[2,32,128]{2,1,0:T(8,128)(2,1)S(1)}, f32[9,128]{1,0:T(8,128)S(1)}) custom-call(bf16[32,8,8,128]{3,2,1,0:T(8,128)(2,1)} %attr_hbm.1, f32[32,32]{1,0:T(8,128)} %start_hbm.1), custom_call_target="tpu_custom_call" | custom-call | flops 1000000 | bytes 1048576 | tf_op jit(solution)/shard_map/pallas_call | solution.py:295
  2.1 6.5 %collective-permute-start.3 = (bf16[2,32,128]{2,1,0:T(8,128)(2,1)S(1)}, bf16[2,32,128]{2,1,0:T(8,128)(2,1)S(1)}, u32[]{:S(2)}, u32[]{:S(2)}) collective-permute-start(bf16[2,32,128]{2,1,0:T(8,128)(2,1)S(1)} %get-tuple-element.15), channel_id=1, source_target_pairs={{1,0},{2,1},{3,2},{4,3},{5,4},{6,5},{7,6},{0,7},{9,8},{10,9},{11,1... | collective-permute-start | bytes 49160 | tf_op jit(solution)/shard_map/ppermute | solution.py:342
  8.6 0.0 collective-permute-start.2
  8.6 1.3 %collective-permute-start = (bf16[16,32,128]{2,1,0:T(8,128)(2,1)S(1)}, bf16[16,32,128]{2,1,0:T(8,128)(2,1)S(1)}, u32[]{:S(2)}, u32[]{:S(2)}) collective-permute-start(bf16[16,32,128]{2,1,0:T(8,128)(2,1)S(1)} %get-tuple-element.13), channel_id=1, source_target_pairs={{0,8},{8,16},{16,24},{24,0},{1,9},{9,17},{17,25},{25,1},{2,10},{10... | collective-permute-start | bytes 393224 | tf_op jit(solution)/shard_map/ppermute | solution.py:341
  9.9 1.4 %collective-permute-start.1 = (bf16[16,32,128]{2,1,0:T(8,128)(2,1)S(1)}, bf16[16,32,128]{2,1,0:T(8,128)(2,1)S(1)}, u32[]{:S(2)}, u32[]{:S(2)}) collective-permute-start(bf16[16,32,128]{2,1,0:T(8,128)(2,1)S(1)} %get-tuple-element.14), channel_id=1, source_target_pairs={{8,0},{16,8},{24,16},{0,24},{9,1},{17,9},{25,17},{1,25},{10,2},{18... | collective-permute-start | bytes 393224 | tf_op jit(solution)/shard_map/ppermute | solution.py:342
  11.4 0.0 copy-start
  11.4 0.0 collective-permute-done.3
  11.4 1.0 %collective-permute-done.2 = bf16[2,32,128]{2,1,0:T(8,128)(2,1)S(1)} collective-permute-done((bf16[2,32,128]{2,1,0:T(8,128)(2,1)S(1)}, bf16[2,32,128]{2,1,0:T(8,128)(2,1)S(1)}, u32[]{:S(2)}, u32[]{:S(2)}) %collective-permute-start.2) | collective-permute-done | bytes 16416 | tf_op jit(solution)/shard_map/ppermute | solution.py:341
  12.4 2.7 %collective-permute-start.5 = (bf16[2,32,128]{2,1,0:T(8,128)(2,1)S(1)}, bf16[2,32,128]{2,1,0:T(8,128)(2,1)S(1)}, u32[]{:S(2)}, u32[]{:S(2)}) collective-permute-start(bf16[2,32,128]{2,1,0:T(8,128)(2,1)S(1)} %broadcast_select_fusion.1.zown), channel_id=1, source_target_pairs={{8,0},{16,8},{24,16},{0,24},{9,1},{17,9},{25,17},{1,25},{10,2},{18... | collective-permute-start | bytes 49160 | tf_op jit(solution)/shard_map/ppermute | solution.py:342
  15.2 0.0 collective-permute-start.4
  15.2 0.9 %collective-permute-done.5 = bf16[2,32,128]{2,1,0:T(8,128)(2,1)S(1)} collective-permute-done((bf16[2,32,128]{2,1,0:T(8,128)(2,1)S(1)}, bf16[2,32,128]{2,1,0:T(8,128)(2,1)S(1)}, u32[]{:S(2)}, u32[]{:S(2)}) %collective-permute-start.5) | collective-permute-done | bytes 16416 | tf_op jit(solution)/shard_map/ppermute | solution.py:342
  16.0 2.9 %collective-permute-done.4 = bf16[2,32,128]{2,1,0:T(8,128)(2,1)S(1)} collective-permute-done((bf16[2,32,128]{2,1,0:T(8,128)(2,1)S(1)}, bf16[2,32,128]{2,1,0:T(8,128)(2,1)S(1)}, u32[]{:S(2)}, u32[]{:S(2)}) %collective-permute-start.4) | collective-permute-done | bytes 16416 | tf_op jit(solution)/shard_map/ppermute | solution.py:341
  19.0 0.0 collective-permute-done.ylo
  19.0 0.0 collective-permute-done.1.yhi
  19.1 3.5 %collective-permute-start.7 = (bf16[26,32,128]{2,1,0:T(8,128)(2,1)S(1)}, bf16[26,32,128]{2,1,0:T(8,128)(2,1)S(1)}, u32[]{:S(2)}, u32[]{:S(2)}) collective-permute-start(bf16[26,32,128]{2,1,0:T(8,128)(2,1)S(1)} %get-tuple-element.28), channel_id=1, source_target_pairs={{32,0},{64,32},{96,64},{128,96},{160,128},{192,160},{224,192},{0,2... | collective-permute-start | bytes 638984 | tf_op jit(solution)/shard_map/ppermute | solution.py:342
  22.6 1.1 %collective-permute-start.6 = (bf16[26,32,128]{2,1,0:T(8,128)(2,1)S(1)}, bf16[26,32,128]{2,1,0:T(8,128)(2,1)S(1)}, u32[]{:S(2)}, u32[]{:S(2)}) collective-permute-start(bf16[26,32,128]{2,1,0:T(8,128)(2,1)S(1)} %get-tuple-element.29), channel_id=1, source_target_pairs={{0,32},{32,64},{64,96},{96,128},{128,160},{160,192},{192,224},{224... | collective-permute-start | bytes 638984 | tf_op jit(solution)/shard_map/ppermute | solution.py:341
  23.7 0.1 iota.35.edge
  23.8 0.0 copy-done
  23.8 1.5 %shard_map.51 = (f32[32,32,128]{2,1,0:T(8,128)S(1)}, f32[32,32,128]{2,1,0:T(8,128)S(1)}, f32[40,32]{1,0:T(8,128)S(1)}) custom-call(bf16[64,32,128]{2,1,0:T(8,128)(2,1)S(1)} %get-tuple-element.12.own, bf16[16,32,128]{2,1,0:T(8,128)(2,1)S(1)} %collective-permute-done.ylo, bf16[16,32,128]{2,1,0:T(8,128)(2,1)S(1)} %collective-permute-done.1.yhi, ...), custom_call_target="tpu_custom_call" | custom-call | flops 500000000 | bytes 3145728 | tf_op jit(solution)/shard_map/pallas_call | solution.py:295
  25.3 2.2 %collective-permute-done.7.xhi = bf16[26,32,128]{2,1,0:T(8,128)(2,1)S(1)} collective-permute-done((bf16[26,32,128]{2,1,0:T(8,128)(2,1)S(1)}, bf16[26,32,128]{2,1,0:T(8,128)(2,1)S(1)}, u32[]{:S(2)}, u32[]{:S(2)}) %collective-permute-start.7) | collective-permute-done | bytes 213024 | tf_op jit(solution)/shard_map/ppermute | solution.py:342
  27.5 0.0 collective-permute-done.6.xlo
  27.5 1.1 %shard_map.52 = bf16[5,2,128]{2,1,0:T(2,128)(2,1)S(1)} custom-call(bf16[64,32,128]{2,1,0:T(8,128)(2,1)S(1)} %get-tuple-element.12.own, bf16[26,32,128]{2,1,0:T(8,128)(2,1)S(1)} %collective-permute-done.6.xlo, bf16[26,32,128]{2,1,0:T(8,128)(2,1)S(1)} %collective-permute-done.7.xhi, bf16[768,256]{1,0:T(8,128)(2,1)S(1)} %copy-done, ...), custom_call_target="tpu_custom_call" | custom-call | flops 200000000 | bytes 2097152 | tf_op jit(solution)/shard_map/pallas_call | solution.py:295
  28.7 11.2 %all_to_all.20 = bf16[16,5,2,128]{3,2,1,0:T(2,128)(2,1)S(1)} all-to-all(bf16[16,5,2,128]{3,2,1,0:T(2,128)(2,1)S(1)} %broadcast_in_dim.43), channel_id=1, replica_groups=mesh['cx'=4,'core'=2,'gy'=4,'gz'=8] {'core','gz'}, dimensions={0} | all-to-all | bytes 81920 | tf_op jit(solution)/shard_map/all_to_all | solution.py:347
  39.9 9.3 %all_to_all.21 = f32[16,9,1,128]{3,2,1,0:T(1,128)S(1)} all-to-all(f32[16,9,1,128]{3,2,1,0:T(1,128)S(1)} %broadcast_in_dim.45), channel_id=1, replica_groups=mesh['cx'=4,'core'=2,'gy'=4,'gz'=8] {'cx','gy'}, dimensions={0} | all-to-all | bytes 147456 | tf_op jit(solution)/shard_map/all_to_all | solution.py:347
  49.2 0.1 reduce_sum.37.cent
  49.3 3.2 %shard_map.53 = (f32[32,8,8,128]{3,2,1,0:T(8,128)}, bf16[5,2,128]{2,1,0:T(2,128)(2,1)S(1)}) custom-call(bf16[64,32,128]{2,1,0:T(8,128)(2,1)S(1)} %get-tuple-element.12.own, bf16[16,32,128]{2,1,0:T(8,128)(2,1)S(1)} %collective-permute-done.ylo, bf16[16,32,128]{2,1,0:T(8,128)(2,1)S(1)} %collective-permute-done.1.yhi, ...), custom_call_target="tpu_custom_call" | custom-call | flops 800000000 | bytes 3145728 | tf_op jit(solution)/shard_map/pallas_call | solution.py:295
  52.5 11.6 %all_to_all.22 = bf16[16,5,2,128]{3,2,1,0:T(2,128)(2,1)S(1)} all-to-all(bf16[16,5,2,128]{3,2,1,0:T(2,128)(2,1)S(1)} %broadcast_in_dim.46), channel_id=1, replica_groups=mesh['cx'=4,'core'=2,'gy'=4,'gz'=8] {'core','gz'}, dimensions={0} | all-to-all | bytes 81920 | tf_op jit(solution)/shard_map/all_to_all | solution.py:347
  64.2 9.5 %all_to_all.23 = f32[16,9,1,128]{3,2,1,0:T(1,128)S(1)} all-to-all(f32[16,9,1,128]{3,2,1,0:T(1,128)S(1)} %broadcast_in_dim.48), channel_id=1, replica_groups=mesh['cx'=4,'core'=2,'gy'=4,'gz'=8] {'cx','gy'}, dimensions={0} | all-to-all | bytes 147456 | tf_op jit(solution)/shard_map/all_to_all | solution.py:347
  73.7 0.1 reduce_sum.39
  73.8 0.1 reshape.110
  73.9 0.7 bitcast_divide_fusion
  (22 shorter events, 0.3 us)
Async XLA Ops:
  2.1 9.3 %collective-permute-start.3 = (bf16[2,32,128]{2,1,0:T(8,128)(2,1)S(1)}, bf16[2,32,128]{2,1,0:T(8,128)(2,1)S(1)}, u32[]{:S(2)}, u32[]{:S(2)}) collective-permute-start(bf16[2,32,128]{2,1,0:T(8,128)(2,1)S(1)} %get-tuple-element.15), channel_id=1, source_target_pairs={{1,0},{2,1},{3,2},{4,3},{5,4},{6,5},{7,6},{0,7},{9,8},{10,9},{11,1... | collective-permute-start | bytes 49160 | tf_op jit(solution)/shard_map/ppermute | solution.py:342
  8.6 3.8 %collective-permute-start.2 = (bf16[2,32,128]{2,1,0:T(8,128)(2,1)S(1)}, bf16[2,32,128]{2,1,0:T(8,128)(2,1)S(1)}, u32[]{:S(2)}, u32[]{:S(2)}) collective-permute-start(bf16[2,32,128]{2,1,0:T(8,128)(2,1)S(1)} %get-tuple-element.15), channel_id=1, source_target_pairs={{0,1},{1,2},{2,3},{3,4},{4,5},{5,6},{6,7},{7,0},{8,9},{9,10},{10,1... | collective-permute-start | bytes 49160 | tf_op jit(solution)/shard_map/ppermute | solution.py:341
  8.6 10.3 %collective-permute-start = (bf16[16,32,128]{2,1,0:T(8,128)(2,1)S(1)}, bf16[16,32,128]{2,1,0:T(8,128)(2,1)S(1)}, u32[]{:S(2)}, u32[]{:S(2)}) collective-permute-start(bf16[16,32,128]{2,1,0:T(8,128)(2,1)S(1)} %get-tuple-element.13), channel_id=1, source_target_pairs={{0,8},{8,16},{16,24},{24,0},{1,9},{9,17},{17,25},{25,1},{2,10},{10... | collective-permute-start | bytes 393224 | tf_op jit(solution)/shard_map/ppermute | solution.py:341
  9.9 9.1 %collective-permute-start.1 = (bf16[16,32,128]{2,1,0:T(8,128)(2,1)S(1)}, bf16[16,32,128]{2,1,0:T(8,128)(2,1)S(1)}, u32[]{:S(2)}, u32[]{:S(2)}) collective-permute-start(bf16[16,32,128]{2,1,0:T(8,128)(2,1)S(1)} %get-tuple-element.14), channel_id=1, source_target_pairs={{8,0},{16,8},{24,16},{0,24},{9,1},{17,9},{25,17},{1,25},{10,2},{18... | collective-permute-start | bytes 393224 | tf_op jit(solution)/shard_map/ppermute | solution.py:342
  11.4 12.4 %copy-start = (bf16[768,256]{1,0:T(8,128)(2,1)S(1)}, bf16[768,256]{1,0:T(8,128)(2,1)}, u32[]{:S(2)}) copy-start(bf16[768,256]{1,0:T(8,128)(2,1)} %constant.77.clone.matrix) | copy-start | bytes 1179652
  12.4 3.6 %collective-permute-start.5 = (bf16[2,32,128]{2,1,0:T(8,128)(2,1)S(1)}, bf16[2,32,128]{2,1,0:T(8,128)(2,1)S(1)}, u32[]{:S(2)}, u32[]{:S(2)}) collective-permute-start(bf16[2,32,128]{2,1,0:T(8,128)(2,1)S(1)} %broadcast_select_fusion.1.zown), channel_id=1, source_target_pairs={{8,0},{16,8},{24,16},{0,24},{9,1},{17,9},{25,17},{1,25},{10,2},{18... | collective-permute-start | bytes 49160 | tf_op jit(solution)/shard_map/ppermute | solution.py:342
  15.2 3.8 %collective-permute-start.4 = (bf16[2,32,128]{2,1,0:T(8,128)(2,1)S(1)}, bf16[2,32,128]{2,1,0:T(8,128)(2,1)S(1)}, u32[]{:S(2)}, u32[]{:S(2)}) collective-permute-start(bf16[2,32,128]{2,1,0:T(8,128)(2,1)S(1)} %broadcast_select_fusion.1.zown), channel_id=1, source_target_pairs={{0,8},{8,16},{16,24},{24,0},{1,9},{9,17},{17,25},{25,1},{2,10},{10... | collective-permute-start | bytes 49160 | tf_op jit(solution)/shard_map/ppermute | solution.py:341
  19.1 8.5 %collective-permute-start.7 = (bf16[26,32,128]{2,1,0:T(8,128)(2,1)S(1)}, bf16[26,32,128]{2,1,0:T(8,128)(2,1)S(1)}, u32[]{:S(2)}, u32[]{:S(2)}) collective-permute-start(bf16[26,32,128]{2,1,0:T(8,128)(2,1)S(1)} %get-tuple-element.28), channel_id=1, source_target_pairs={{32,0},{64,32},{96,64},{128,96},{160,128},{192,160},{224,192},{0,2... | collective-permute-start | bytes 638984 | tf_op jit(solution)/shard_map/ppermute | solution.py:342
  22.6 4.9 %collective-permute-start.6 = (bf16[26,32,128]{2,1,0:T(8,128)(2,1)S(1)}, bf16[26,32,128]{2,1,0:T(8,128)(2,1)S(1)}, u32[]{:S(2)}, u32[]{:S(2)}) collective-permute-start(bf16[26,32,128]{2,1,0:T(8,128)(2,1)S(1)} %get-tuple-element.29), channel_id=1, source_target_pairs={{0,32},{32,64},{64,96},{96,128},{128,160},{160,192},{192,224},{224... | collective-permute-start | bytes 638984 | tf_op jit(solution)/shard_map/ppermute | solution.py:341
